TPU v7x, 32 devices: a whole 2x2x4 slice. The times are simulated.
32 devices in a mesh: mode: 2 (over x), band: 16 (over z, y, core).
Axes of the slice: x: 2, y: 2, z: 4, core: 2. Of those that a mesh axis runs over, the one named last changes fastest.
Arguments:
- mode_field: bfloat16 [2, 4096, 2, 4096], P('mode', 'band'), may hold values from -6 to 6
- figure: bfloat16 [4096, 4096], P('band'), may hold values from -6 to 6
- target: bfloat16 [4096, 4096], P('band'), may hold values from 0 to 2
- footprint: int32 [16, 64], replicated, may hold values from 0 to 1023, as said below
- approach_tiles: bfloat16 [3, 2, 128, 128], replicated, may hold values from -0.21875 to 0.21875
- focus_tiles: bfloat16 [3, 2, 128, 128], replicated, may hold values from -0.21875 to 0.21875
Outputs:
- sensitivity: float32 [4096, 4096], P('band')
Inputs may be any that keep to these rules, and one draw needn't show every extreme that they name: `footprint`: entry [d, j] is the surface tile band * 64 + block read by beam tile j of band d; for every beam band d and surface band s at most 8 entries of row d name band s, and some row reaches 8 in every draw.
All inputs are finite; a program needn't handle non-finite values.
Results may differ from a plain program's by a relative error of at most 0.0082.
Values may be sent and summed in bfloat16 or wider, within the bound.
A program may use at most 128 MiB of HBM per device.

v0:
```python
import jax
import jax.numpy as jnp
from jax import lax
from jax.sharding import PartitionSpec as P

MIRROR_TILE = 64


PHASE_FACTOR = 4.0


def real_kernels(tile_set):
    real_part = tile_set[:, 0]
    imag_part = tile_set[:, 1]
    upper = jnp.stack([real_part, imag_part], axis=2)
    lower = jnp.stack([-imag_part, real_part], axis=2)
    return jnp.stack([upper, lower], axis=1)


def banded(grid_field, kernels):
    leading = grid_field.shape[:-1]
    tile_width = kernels.shape[2]
    mirror_block_list = grid_field.shape[-1] // tile_width
    reshaped_field = grid_field.reshape(leading + (mirror_block_list, tile_width))
    keep = [(0, 0)] * len(leading)
    centre = jnp.einsum(
        "mrcbk,ckel->mrebl", reshaped_field, kernels[1], preferred_element_type=jnp.float32
    )
    from_lower = jnp.einsum(
        "mrcbk,ckel->mrebl",
        reshaped_field[..., :-1, :],
        kernels[0],
        preferred_element_type=jnp.float32,
    )
    from_upper = jnp.einsum(
        "mrcbk,ckel->mrebl",
        reshaped_field[..., 1:, :],
        kernels[2],
        preferred_element_type=jnp.float32,
    )
    running = (
        centre
        + jnp.pad(from_lower, keep + [(1, 0), (0, 0)])
        + jnp.pad(from_upper, keep + [(0, 1), (0, 0)])
    )
    return running.reshape(grid_field.shape)


def tiles_out(beam_row_lines, receive_hot):
    count_of_rows = beam_row_lines.shape[0]
    reshaped_field = beam_row_lines.reshape(count_of_rows, -1, MIRROR_TILE)
    packed_tiles = jnp.einsum(
        "jsc,rjl->scrl", receive_hot, reshaped_field, precision=lax.Precision.HIGHEST
    )
    return packed_tiles.reshape(
        packed_tiles.shape[0], packed_tiles.shape[1], count_of_rows * MIRROR_TILE
    )


def tiles_in(received_tiles, slot_source):
    reshaped_field = received_tiles.reshape(
        received_tiles.shape[0], received_tiles.shape[1], -1, MIRROR_TILE
    )
    placed = jnp.einsum(
        "dck,dcrl->rkl", slot_source, reshaped_field, precision=lax.Precision.HIGHEST
    )
    return placed.reshape(placed.shape[0], -1)


def fetch_heights(surface_rows, slot_source):
    count_of_bands = slot_source.shape[0]
    subset_rows = surface_rows.shape[0]
    outbound_tiles = jnp.einsum(
        "dck,rkl->dcrl",
        slot_source.astype(jnp.bfloat16),
        surface_rows,
        preferred_element_type=jnp.float32,
    ).astype(jnp.bfloat16)
    outbound_tiles = outbound_tiles.reshape(
        count_of_bands, outbound_tiles.shape[1], subset_rows * MIRROR_TILE
    )
    return outbound_tiles


def shards(mode_field, figure, target, footprint, approach_tiles, focus_tiles):
    count_of_bands = lax.axis_size("band")
    band_index = lax.axis_index("band")
    count_of_rows = figure.shape[0]
    mirror_block_list = figure.shape[1] // MIRROR_TILE
    slot_capacity = max(2, 2 * mirror_block_list // count_of_bands)
    approach = real_kernels(approach_tiles)
    focus = real_kernels(focus_tiles)
    adjoint = jnp.transpose(focus, (0, 3, 4, 1, 2))[::-1]
    source_band = footprint // mirror_block_list
    source_block = footprint % mirror_block_list
    column = jnp.arange(mirror_block_list, dtype=jnp.int32)
    earlier = column[None, :] < column[:, None]
    same_band = source_band[:, :, None] == source_band[:, None, :]
    tile_rank = jnp.sum((same_band & earlier[None]).astype(jnp.int32), axis=2)
    slot_ids = jnp.arange(slot_capacity, dtype=jnp.int32)
    band_ids = jnp.arange(count_of_bands, dtype=jnp.int32)
    from_here = (source_band == band_index)[:, None, :] & (
        tile_rank[:, None, :] == slot_ids[None, :, None]
    )
    block_hot = (source_block[:, :, None] == column[None, None, :]).astype(jnp.float32)
    slot_source = jnp.einsum("dcj,djk->dck", from_here.astype(jnp.float32), block_hot)
    my_band = lax.dynamic_index_in_dim(source_band, band_index, 0, keepdims=False)
    my_rank = lax.dynamic_index_in_dim(tile_rank, band_index, 0, keepdims=False)
    receive_hot = (
        (my_band[:, None, None] == band_ids[None, :, None])
        & (my_rank[:, None, None] == slot_ids[None, None, :])
    ).astype(jnp.float32)
    receive_low = receive_hot.astype(jnp.bfloat16)
    surface_owned = figure.reshape(count_of_rows, mirror_block_list, MIRROR_TILE)
    outbound_tiles = fetch_heights(surface_owned, slot_source)
    inbound_tiles = lax.all_to_all(outbound_tiles, "band", split_axis=0, concat_axis=0, tiled=True)
    inbound_tiles = inbound_tiles.reshape(count_of_bands, slot_capacity, count_of_rows, MIRROR_TILE)
    phase_tile_stack = jnp.einsum(
        "jsc,scrl->rjl", receive_low, inbound_tiles, preferred_element_type=jnp.float32
    )
    phase_delay = PHASE_FACTOR * phase_tile_stack.reshape(
        count_of_rows, mirror_block_list * MIRROR_TILE
    )
    cosine = jnp.cos(phase_delay)
    sine_part = jnp.sin(phase_delay)
    propagated = banded(mode_field, approach).astype(jnp.bfloat16)
    moved = lax.all_to_all(propagated, "band", split_axis=3, concat_axis=1, tiled=True)
    turned = jnp.transpose(moved, (0, 3, 2, 1))
    advanced = banded(turned, approach).astype(jnp.bfloat16)
    real_part = advanced[:, :, 0].astype(jnp.float32)
    imag_part = advanced[:, :, 1].astype(jnp.float32)
    screened = jnp.stack(
        [real_part * cosine - imag_part * sine_part, real_part * sine_part + imag_part * cosine],
        axis=2,
    ).astype(jnp.bfloat16)
    detected = banded(screened, focus)
    local_power = jnp.sum(detected * detected, axis=(0, 2))
    intensity = lax.psum(local_power, "mode")
    residual = intensity - target.astype(jnp.float32)
    detector_grad = (detected * residual[None, :, None, :]).astype(jnp.bfloat16)
    mirror_grad = banded(detector_grad, adjoint)
    screen_real = screened[:, :, 0].astype(jnp.float32)
    screen_imag = screened[:, :, 1].astype(jnp.float32)
    local_sens = jnp.sum(
        2.0
        * PHASE_FACTOR
        * (mirror_grad[:, :, 1] * screen_real - mirror_grad[:, :, 0] * screen_imag),
        axis=0,
    )
    beam_share = lax.psum_scatter(local_sens, "mode", scatter_dimension=0, tiled=True)
    returned = lax.all_to_all(
        tiles_out(beam_share, receive_hot), "band", split_axis=0, concat_axis=0, tiled=True
    )
    surface_share = tiles_in(returned, slot_source)
    sensitivity = lax.all_gather(surface_share, "mode", axis=0, tiled=True)
    return sensitivity


def solution(mesh):
    in_specs = (P("mode", "band", None, None), P("band", None), P("band", None), P(), P(), P())
    out_specs = P("band", None)
    return jax.shard_map(shards, mesh=mesh, in_specs=in_specs, out_specs=out_specs, check_vma=False)
```

profile of v0, /device:TPU:12, one launch (start us, length us, event | category | flops | bytes accessed | tf_op | source)
XLA Modules:
  0.0 755.8 jit_solution(1303177262719395260)
XLA Ops:
  6.5 0.7 add_select_fusion
  7.3 0.7 broadcast_compare_fusion
  8.0 3.3 copy.151
  11.2 0.5 convert_reduce_fusion
  11.8 0.3 fusion.71
  12.1 0.6 copy-done.9
  12.7 3.7 convolution_convert_fusion
  16.4 9.0 %copy.153 = bf16[16,8,256,64]{3,2,1,0:T(8,128)(2,1)} copy(bf16[16,8,256,64]{2,1,3,0:T(8,128)(2,1)} %convolution_convert_fusion) | data formatting | bytes 8388608 | tf_op jit(solution)/shard_map/convert_element_type | solution.py:78
  25.4 10.6 %reshape.355 = bf16[16,8,16384]{2,1,0:T(8,128)(2,1)} reshape(bf16[16,8,256,64]{3,2,1,0:T(8,128)(2,1)} %copy.153) | data formatting | bytes 8388608 | tf_op jit(solution)/shard_map/reshape | solution.py:79
  36.0 6.6 all-to-all-start.1
  42.6 11.0 %copy.142 = bf16[1,256,2,4096]{1,3,2,0:T(8,128)(2,1)} copy(bf16[1,256,2,4096]{3,2,1,0:T(2,128)(2,1)} %param.6) | data formatting | bytes 8388608 | tf_op args[0]
  53.6 7.9 %reshape.346 = bf16[256,2,32,128]{3,2,1,0:T(8,128)(2,1)} reshape(bf16[1,256,2,4096]{3,2,1,0:T(2,128)(2,1)} %param.6) | data formatting | bytes 8388608 | tf_op jit(solution)/shard_map/reshape.6
  61.9 5.9 fusion.121
  67.7 6.4 copy.220
  74.1 6.4 copy.221
  80.5 3.6 fusion.41
  84.1 4.4 fusion.44
  88.6 9.6 %fusion.5 = bf16[1,256,2,32,128]{1,4,3,2,0:T(8,128)(2,1)} fusion(f32[1,256,2,31,128]{1,4,3,2,0:T(8,128)} %fusion.44, f32[1,256,2,31,128]{1,4,3,2,0:T(8,128)S(1)} %fusion.41, bf16[256,2,32,128]{3,2,1,0:T(8,128)(2,1)S(1)} %copy-done.5, bf16[3,1,128,2,128]{2,4,1,3,0:T(8,128)(2,1)S(1)} %get-tuple-element.26, bf16[3,1,128,2,128]{2,4,1,3,0:T(8,128)(2,1)S(1)} %get-tuple-element.27), kind=kOutput, calls=%fused_computation.9 | convolution fusion | flops 1080295424 | bytes 25034752 | tf_op jit(solution)/shard_map/mrcbk,ckel->mrebl/dot_general | solution.py:26
  98.2 10.1 %copy.145 = bf16[1,256,2,4096]{1,2,0,3:T(2,128)(2,1)} copy(bf16[1,256,2,4096]{1,3,2,0:T(8,128)(2,1)} %bitcast.314) | data formatting | bytes 8388608 | tf_op jit(solution)/shard_map/convert_element_type | solution.py:126
  108.3 26.5 %all-to-all-done.1 = bf16[16,8,16384]{2,1,0:T(8,128)(2,1)} async-done(((bf16[16,8,16384]{2,1,0:T(8,128)(2,1)}), bf16[16,8,16384]{2,1,0:T(8,128)(2,1)}, u32[]{:S(2)}, u32[]{:S(2)}) %all-to-all-start.1) | async-done | bytes 4194336 | tf_op jit(solution)/shard_map/all_to_all | solution.py:116
  134.8 5.0 all-to-all-start
  140.5 11.4 %reshape.356 = bf16[16,8,256,64]{3,2,1,0:T(8,128)(2,1)} reshape(bf16[16,8,16384]{2,1,0:T(8,128)(2,1)} %all-to-all-done.1) | data formatting | bytes 8388608 | tf_op jit(solution)/shard_map/reshape | solution.py:117
  152.0 10.0 %copy.154 = bf16[16,8,256,64]{2,1,0,3:T(8,128)(2,1)} copy(bf16[16,8,256,64]{3,2,1,0:T(8,128)(2,1)} %reshape.356) | data formatting | bytes 8388608 | tf_op jit(solution)/shard_map/reshape | solution.py:117
  162.0 70.1 %all-to-all-done = bf16[1,256,2,4096]{1,2,0,3:T(2,128)(2,1)} async-done(((bf16[1,256,2,4096]{1,2,0,3:T(2,128)(2,1)}), bf16[1,256,2,4096]{1,2,0,3:T(2,128)(2,1)}, u32[]{:S(2)}, u32[]{:S(2)}) %all-to-all-start) | async-done | bytes 4194336 | tf_op jit(solution)/shard_map/all_to_all | solution.py:127
  232.1 4.7 copy.146
  236.8 6.3 copy.147
  243.1 17.1 %cosine_bitcast_fusion = (f32[256,64,64]{0,1,2:T(8,128)S(1)}, f32[256,64,64]{0,1,2:T(8,128)S(1)}) fusion(bf16[16,8,256,64]{2,1,0,3:T(8,128)(2,1)} %copy.154, pred[64,8]{0,1:T(8,128)(4,1)S(1)} %iota_compare_fusion.5, pred[64,16]{0,1:T(8,128)(4,1)S(1)} %iota_compare_fusion.4), kind=kOutput, calls=%fused_computation.39 | convolution fusion | flops 269508608 | bytes 12584448 | tf_op jit(solution)/shard_map/jsc,scrl->rjl/dot_general | solution.py:118
  260.3 4.4 copy.155
  264.7 4.4 copy.156
  269.1 3.5 fusion.120
  272.6 6.4 copy.222
  278.9 6.5 fusion.47
  285.5 6.8 copy.223
  292.3 3.6 fusion.50
  295.9 5.8 fusion.1
  301.7 5.1 fusion.7
  306.7 4.4 copy.160
  311.1 2.9 copy.159
  314.0 6.7 fusion.59
  320.8 4.0 fusion.62
  324.7 4.1 copy.158
  328.8 2.9 copy.157
  331.6 12.8 %multiply_reduce_fusion = (f32[256,32,128]{0,2,1:T(8,128)}, f32[1,256,2,32,128]{1,4,3,2,0:T(8,128)}) fusion(f32[1,256,2,31,128]{1,4,3,2,0:T(8,128)} %fusion.59, f32[1,256,2,31,128]{1,4,3,2,0:T(8,128)} %fusion.62, bf16[256,1,32,128]{3,0,1,2:T(8,128)(2,1)} %copy.158, bf16[256,1,32,128]{3,0,1,2:T(8,128)(2,1)} %copy.157, ...), kind=kOutput, calls=%fused_computation.11 | convolution fusion | flops 1089732608 | bytes 33423360 | tf_op jit(solution)/shard_map/mrcbk,ckel->mrebl/dot_general | solution.py:26
  344.4 5.6 copy.161
  350.2 107.8 %all-reduce.10.cloned.1.call-done = f32[256,4096]{1,0:T(8,128)} async-done(((f32[256,4096]{1,0:T(8,128)}), f32[256,4096]{1,0:T(8,128)}) %all-reduce.10.cloned.1.call-update) | async-done | bytes 4194320 | tf_op jit(solution)/shard_map/psum | solution.py:138
  458.0 4.9 convert_subtract_fusion
  462.9 5.7 copy.205
  468.7 6.1 multiply_convert_fusion
  474.8 0.6 slice_bitcast_fusion.1
  475.4 4.4 fusion.53
  479.8 4.4 fusion.56
  484.2 11.4 %fusion.2 = f32[1,256,2,32,128]{1,4,3,2,0:T(8,128)} fusion(f32[1,256,2,31,128]{1,4,3,2,0:T(8,128)} %fusion.56, f32[1,256,2,31,128]{1,4,3,2,0:T(8,128)} %fusion.53, bf16[2,128,2,128,1]{3,1,2,0,4:T(8,128)(2,1)S(1)} %get-tuple-element.17, f32[1,256,2,32,128]{1,4,3,2,0:T(8,128)S(1)} %bitcast.299, f32[256,32,128]{0,2,1:T(8,128)} %bitcast.303), kind=kOutput, calls=%fused_computation.4 | convolution fusion | flops 1082130432 | bytes 37355520 | tf_op jit(solution)/shard_map/mrcbk,ckel->mrebl/dot_general | solution.py:26
  495.7 7.5 fusion.12
  503.2 54.4 %reduce-scatter.2.cloned.1.call-done = f32[128,4096]{0,1:T(8,128)} async-done(((f32[256,4096]{0,1:T(8,128)}), f32[128,4096]{0,1:T(8,128)}) %reduce-scatter.2.cloned.1.call-update) | async-done | bytes 2097168 | tf_op jit(solution)/shard_map/reduce_scatter | solution.py:150
  557.6 3.8 copy.169
  561.5 3.5 reshape.403
  565.0 1.9 fusion.92
  566.9 98.3 %all_to_all.28 = f32[16,8,8192]{2,1,0:T(8,128)} all-to-all(f32[16,8,8192]{2,1,0:T(8,128)S(1)} %fusion.92), channel_id=1, replica_groups=mesh['mode'=2,'band'=16] {'band'}, dimensions={0} | all-to-all | bytes 8388608 | tf_op jit(solution)/shard_map/all_to_all | solution.py:151
  665.2 7.9 %reshape.364 = f32[16,8,128,64]{3,2,1,0:T(8,128)} reshape(f32[16,8,8192]{2,1,0:T(8,128)} %all_to_all.28) | data formatting | bytes 8388608 | tf_op jit(solution)/shard_map/reshape | solution.py:61
  673.1 7.3 copy.170
  680.4 4.2 convolution_bitcast_fusion
  684.7 2.5 copy.171
  687.2 56.2 %all-gather.2.cloned.1.call-done = f32[256,4096]{0,1:T(8,128)} async-done(((f32[128,4096]{0,1:T(8,128)}), f32[256,4096]{0,1:T(8,128)}) %all-gather.2.cloned.1.call-update) | async-done | bytes 4194320 | tf_op jit(solution)/shard_map/all_gather | solution.py:155
  743.5 5.6 copy.172
  (52 shorter events, 1.2 us)
Async XLA Ops:
  12.1 0.6 copy-start.9
  36.0 98.8 %all-to-all-start.1 = ((bf16[16,8,16384]{2,1,0:T(8,128)(2,1)}), bf16[16,8,16384]{2,1,0:T(8,128)(2,1)}, u32[]{:S(2)}, u32[]{:S(2)}) async-start(bf16[16,8,16384]{2,1,0:T(8,128)(2,1)} %reshape.355), calls=%async_computation.1 | async-start | bytes 8388608 | tf_op jit(solution)/shard_map/all_to_all | solution.py:116
  53.6 7.9 %copy-start.11 = (bf16[3,2,128,128]{3,2,1,0:T(8,128)(2,1)S(1)}, bf16[3,2,128,128]{3,2,1,0:T(8,128)(2,1)}, u32[]{:S(2)}) copy-start(bf16[3,2,128,128]{3,2,1,0:T(8,128)(2,1)} %param.10) | copy-start | bytes 589828
  80.5 3.6 copy-start.7
  84.1 4.5 copy-start.5
  108.3 31.8 %copy-start.12 = (bf16[3,2,128,128]{3,2,1,0:T(8,128)(2,1)S(1)}, bf16[3,2,128,128]{3,2,1,0:T(8,128)(2,1)}, u32[]{:S(2)}) copy-start(bf16[3,2,128,128]{3,2,1,0:T(8,128)(2,1)} %param.11) | copy-start | bytes 589828
  134.8 97.4 %all-to-all-start = ((bf16[1,256,2,4096]{1,2,0,3:T(2,128)(2,1)}), bf16[1,256,2,4096]{1,2,0,3:T(2,128)(2,1)}, u32[]{:S(2)}, u32[]{:S(2)}) async-start(bf16[1,256,2,4096]{1,2,0,3:T(2,128)(2,1)} %copy.145), calls=%async_computation | async-start | bytes 8388608 | tf_op jit(solution)/shard_map/all_to_all | solution.py:127
  139.8 318.2 %all-reduce.10.cloned.1.call-start = ((), (), s32[]{:S(2)}) async-start(), calls=%async_computation.4 | async-start | bytes 8388608 | tf_op jit(solution)/shard_map/psum | solution.py:138
  264.7 4.4 copy-start
  292.3 3.6 copy-start.1
  295.8 5.8 copy-start.6
  306.7 22.0 %copy-start.2 = (bf16[1,256,1,4096]{1,3,2,0:T(8,128)(2,1)}, bf16[1,256,1,4096]{1,3,2,0:T(8,128)(2,1)S(1)}, u32[]{:S(2)}) copy-start(bf16[1,256,1,4096]{1,3,2,0:T(8,128)(2,1)S(1)} %get-tuple-element.7) | copy-start | bytes 6291460
  314.0 6.8 copy-start.3
  314.0 6.8 copy-start.4
  350.0 108.0 %copy-start.8 = (bf16[256,4096]{1,0:T(8,128)(2,1)S(1)}, bf16[256,4096]{1,0:T(8,128)(2,1)}, u32[]{:S(2)}) copy-start(bf16[256,4096]{1,0:T(8,128)(2,1)} %param.8) | copy-start | bytes 6291460
  350.1 207.6 %reduce-scatter.2.cloned.1.call-start = ((), (), s32[]{:S(2)}) async-start(), calls=%async_computation.5 | async-start | bytes 6291456 | tf_op jit(solution)/shard_map/reduce_scatter | solution.py:150
  475.4 8.9 %slice-start = ((s8[8388608]{0:T(1024)(128)(4,1)}), s8[4194304]{0:T(1024)(128)(4,1)S(1)}, s32[]{:S(2)}) async-start(s8[8388608]{0:T(1024)(128)(4,1)} %bitcast.298), calls=%async_computation.7 | async-start | bytes 8388608
  479.8 4.4 slice-start.1
  503.2 240.3 %all-gather.2.cloned.1.call-start = ((), (), s32[]{:S(2)}) async-start(), calls=%async_computation.6 | async-start | bytes 6291456 | tf_op jit(solution)/shard_map/all_gather | solution.py:155
  673.1 7.3 copy-start.10
Sparse Core Ops, SparseCore 0:
  350.2 107.7 all-reduce.9
  503.3 54.3 reduce-scatter.1
  687.3 56.0 all-gather.1
where the time goes:
time: 764 us; the launch traced here: 756 us
  waiting for transfers between devices  315 us (41%)
  local copies, waits for them, and re-layouts  187 us (24%)
  matrix products  105 us (14%)
  blocking collectives  98.3 us (13%)
  other arithmetic  25.7 us (3%)
  between operations  13.6 us (2%)
  starting transfers between devices  12 us (2%)
    psum x1, waiting for transfers between devices, shards(): intensity = lax.psum(local_power, 'mode')  108 us
    all_to_all x1, blocking collectives, shards(): lax.all_to_all(tiles_out(beam_share, receive_hot), 'band', split_axis=0,...  98.3 us
    all_to_all x1, waiting for transfers between devices, shards(): lax.all_to_all(propagated, 'band', split_axis=3, concat_axis=1, tiled=True)  70.1 us
    all_gather x1, waiting for transfers between devices, shards(): sensitivity = lax.all_gather(surface_share, 'mode', axis=0, tiled=True)  56.2 us
    reduce_scatter x1, waiting for transfers between devices, shards(): lax.psum_scatter(local_sens, 'mode', scatter_dimension=0, tiled=True)  54.4 us
    unnamed x40, local copies, waits for them, and re-layouts  41.4 us
    dot_general x4, matrix products, banded(): jnp.einsum('mrcbk,ckel->mrebl', reshaped_field, kernels[1], preferred_ele...  39.6 us
    all_to_all x1, waiting for transfers between devices, shards(): lax.all_to_all(outbound_tiles, 'band', split_axis=0, concat_axis=0, tiled...  26.5 us
  transfers between devices with their start and end apart: 5, of which 5 were waited for; matrix products, arithmetic and copies ran while one was open for 12% of the time, Pallas kernels for 0%

commit v1 on v0

--- a/solution.py
+++ b/solution.py
@@ -1,6 +1,10 @@
+import functools
+
 import jax
 import jax.numpy as jnp
 from jax import lax
+from jax.experimental import pallas as pl
+from jax.experimental.pallas import tpu as pltpu
 from jax.sharding import PartitionSpec as P
 
 MIRROR_TILE = 64
@@ -82,7 +86,7 @@
     return outbound_tiles
 
 
-def shards(mode_field, figure, target, footprint, approach_tiles, focus_tiles):
+def general_shards(mode_field, figure, target, footprint, approach_tiles, focus_tiles):
     count_of_bands = lax.axis_size("band")
     band_index = lax.axis_index("band")
     count_of_rows = figure.shape[0]
@@ -156,7 +160,308 @@
     return sensitivity
 
 
+VMEM_GRANT = 48 * 1024 * 1024
+
+
+def half_chunk(data_ref, band, block, to_right):
+    start = pl.multiple_of((block // 2) * 128, 128)
+    chunk = data_ref[band, :, pl.ds(start, 128)].astype(jnp.float32)
+    swapped = (block % 2) != to_right
+    return jnp.where(swapped, pltpu.roll(chunk, MIRROR_TILE, 1), chunk)
+
+
+def gather_kernel(band_ref, block_ref, data_ref, out_ref):
+    pairs_each = out_ref.shape[2] // 128
+    pairs = out_ref.shape[0] * pairs_each
+    rows = out_ref.shape[1]
+    left_lanes = lax.broadcasted_iota(jnp.int32, (rows, 128), 1) < MIRROR_TILE
+
+    def one_pair(pair, carry):
+        left = half_chunk(data_ref, band_ref[2 * pair], block_ref[2 * pair], 0)
+        right = half_chunk(data_ref, band_ref[2 * pair + 1], block_ref[2 * pair + 1], 1)
+        start = pl.multiple_of((pair % pairs_each) * 128, 128)
+        out_ref[pair // pairs_each, :, pl.ds(start, 128)] = jnp.where(
+            left_lanes, left, right
+        ).astype(out_ref.dtype)
+        return carry
+
+    lax.fori_loop(0, pairs, one_pair, 0, unroll=2)
+
+
+def gather_tiles(bands, blocks, data, out_shape):
+    smem = pl.BlockSpec(memory_space=pltpu.SMEM)
+    vmem = pl.BlockSpec(memory_space=pltpu.VMEM)
+    return pl.pallas_call(
+        gather_kernel,
+        out_shape=jax.ShapeDtypeStruct(out_shape, data.dtype),
+        in_specs=[smem, smem, vmem],
+        out_specs=vmem,
+        compiler_params=pltpu.CompilerParams(vmem_limit_bytes=VMEM_GRANT),
+        cost_estimate=pl.CostEstimate(flops=0, bytes_accessed=6 << 20, transcendentals=0),
+    )(bands, blocks, data)
+
+
+def collect_kernel(block_ref, valid_ref, data_ref, out_ref):
+    out_ref[...] = jnp.zeros_like(out_ref)
+    bands, rows, length = data_ref.shape
+    slots = length // MIRROR_TILE
+    lane_half = lax.broadcasted_iota(jnp.int32, (rows, 128), 1) // MIRROR_TILE
+
+    def one_slot(slot, carry):
+        block = block_ref[slot]
+
+        @pl.when(valid_ref[slot] > 0)
+        def _():
+            tile = half_chunk(data_ref, slot // slots, slot % slots, block % 2)
+            start = pl.multiple_of((block // 2) * 128, 128)
+            out_ref[:, pl.ds(start, 128)] += jnp.where(lane_half == block % 2, tile, 0.0)
+
+        return carry
+
+    lax.fori_loop(0, bands * slots, one_slot, 0)
+
+
+def collect_tiles(blocks, valid, data, length):
+    smem = pl.BlockSpec(memory_space=pltpu.SMEM)
+    vmem = pl.BlockSpec(memory_space=pltpu.VMEM)
+    return pl.pallas_call(
+        collect_kernel,
+        out_shape=jax.ShapeDtypeStruct((data.shape[1], length), jnp.float32),
+        in_specs=[smem, smem, vmem],
+        out_specs=vmem,
+        compiler_params=pltpu.CompilerParams(vmem_limit_bytes=VMEM_GRANT),
+        cost_estimate=pl.CostEstimate(flops=0, bytes_accessed=6 << 20, transcendentals=0),
+    )(blocks, valid, data)
+
+
+def approach_kernel(real_ref, imag_ref, weight_ref, out_ref):
+    tile = weight_ref.shape[0] // 2
+    at = pl.multiple_of(pl.program_id(0) * tile, tile)
+    lines = jnp.concatenate(
+        [real_ref[:, pl.ds(at, 3 * tile)], imag_ref[:, pl.ds(at, 3 * tile)]], axis=1
+    )
+    turned = lax.dot_general(
+        weight_ref[...], lines, (((1,), (1,)), ((), ())), preferred_element_type=jnp.float32
+    ).astype(out_ref.dtype)
+    for half in range(lines.shape[0] // tile):
+        for part in range(2):
+            out_ref[0, :, pl.ds((2 * half + part) * tile, tile)] = turned[
+                part * tile : (part + 1) * tile, half * tile : (half + 1) * tile
+            ]
+
+
+def approach_turned(real_lines, imag_lines, weight, modes, bands):
+    rows = real_lines.shape[0]
+    tile = weight.shape[0] // 2
+    tiles = modes * bands
+    return pl.pallas_call(
+        approach_kernel,
+        out_shape=jax.ShapeDtypeStruct((tiles, tile, 2 * rows), jnp.bfloat16),
+        grid=(tiles,),
+        in_specs=[
+            pl.BlockSpec(real_lines.shape, lambda t: (0, 0)),
+            pl.BlockSpec(imag_lines.shape, lambda t: (0, 0)),
+            pl.BlockSpec(weight.shape, lambda t: (0, 0)),
+        ],
+        out_specs=pl.BlockSpec(
+            (1, tile, 2 * rows), lambda t: ((t % modes) * bands + t // modes, 0, 0)
+        ),
+        compiler_params=pltpu.CompilerParams(vmem_limit_bytes=VMEM_GRANT),
+        cost_estimate=pl.CostEstimate(
+            flops=2 * rows * weight.size * tiles, bytes_accessed=8 << 20, transcendentals=0
+        ),
+    )(real_lines, imag_lines, weight)
+
+
+def beam_kernel(
+    modes, moved_ref, cos_ref, sin_ref, target_ref, approach_ref, focus_ref, adjoint_ref,
+    sens_ref, lines, screens, grads, sems,
+):
+    sources, rows, width = moved_ref.shape
+    bands = sources // modes
+    tile = focus_ref.shape[1] // 2
+    pair = 2 * tile
+    tiles = cos_ref.shape[1] // tile
+
+    def fetch(index):
+        mode, band = index // bands, index % bands
+        return pltpu.make_async_copy(
+            moved_ref.at[index],
+            lines.at[pl.ds(mode * rows, rows), pl.ds(pair + band * width, width)],
+            sems.at[index],
+        )
+
+    for index in range(sources):
+        fetch(index).start()
+    edge = jnp.zeros((lines.shape[0], pair), lines.dtype)
+    screens[:, pl.ds(0, pair)] = edge
+    screens[:, pl.ds((tiles + 1) * pair, pair)] = edge
+    grads[:, pl.ds(0, pair)] = edge
+    grads[:, pl.ds((tiles + 1) * pair, pair)] = edge
+    lines[:, pl.ds(0, pair)] = edge
+    lines[:, pl.ds((tiles + 1) * pair, pair)] = edge
+    for index in range(sources):
+        fetch(index).wait()
+
+    def window(ref, at):
+        return ref[:, pl.ds(pl.multiple_of(at * pair, pair), 3 * pair)]
+
+    def put(ref, at, value):
+        ref[:, pl.ds(pl.multiple_of((at + 1) * pair, pair), pair)] = value
+
+    def columns(ref, at):
+        return ref[:, pl.ds(pl.multiple_of(at * tile, tile), tile)]
+
+    def product(ref, at, weight_ref):
+        return jnp.dot(window(ref, at), weight_ref[...], preferred_element_type=jnp.float32)
+
+    def screen_step(at, carry):
+        advanced = product(lines, at, approach_ref).astype(jnp.bfloat16).astype(jnp.float32)
+        cosine = jnp.concatenate([columns(cos_ref, at)] * modes, axis=0)
+        sine = jnp.concatenate([columns(sin_ref, at)] * modes, axis=0)
+        real, imag = advanced[:, :tile], advanced[:, tile:]
+        screened = jnp.concatenate(
+            [real * cosine - imag * sine, real * sine + imag * cosine], axis=1
+        )
+        put(screens, at, screened.astype(jnp.bfloat16))
+        return carry
+
+    def detect_step(at, carry):
+        detected = product(screens, at, focus_ref)
+        power = detected * detected
+        power = power[:, :tile] + power[:, tile:]
+        intensity = power[:rows]
+        for mode in range(1, modes):
+            intensity = intensity + power[mode * rows : (mode + 1) * rows]
+        residual = intensity - columns(target_ref, at).astype(jnp.float32)
+        residual = jnp.concatenate([jnp.concatenate([residual] * modes, axis=0)] * 2, axis=1)
+        put(grads, at, (detected * residual).astype(jnp.bfloat16))
+        return carry
+
+    def sens_step(at, carry):
+        grad = product(grads, at, adjoint_ref)
+        screened = screens[:, pl.ds(pl.multiple_of((at + 1) * pair, pair), pair)]
+        screened = screened.astype(jnp.float32)
+        terms = grad[:, tile:] * screened[:, :tile] - grad[:, :tile] * screened[:, tile:]
+        sens = terms[:rows]
+        for mode in range(1, modes):
+            sens = sens + terms[mode * rows : (mode + 1) * rows]
+        sens_ref[:, pl.ds(pl.multiple_of(at * tile, tile), tile)] = (
+            2.0 * PHASE_FACTOR * sens
+        ).astype(sens_ref.dtype)
+        return carry
+
+    lax.fori_loop(0, tiles, screen_step, 0, unroll=2)
+    lax.fori_loop(0, tiles, detect_step, 0, unroll=2)
+    lax.fori_loop(0, tiles, sens_step, 0, unroll=2)
+
+
+def beam_sensitivity(moved, cosine, sine, target, approach, focus, adjoint, modes):
+    rows, length = cosine.shape
+    vmem = pl.BlockSpec(memory_space=pltpu.VMEM)
+    held = pltpu.VMEM((modes * rows, 2 * length + 2 * focus.shape[1]), jnp.bfloat16)
+    return pl.pallas_call(
+        functools.partial(beam_kernel, modes),
+        out_shape=jax.ShapeDtypeStruct((rows, length), jnp.bfloat16),
+        in_specs=[pl.BlockSpec(memory_space=pl.ANY)] + [vmem] * 6,
+        out_specs=vmem,
+        scratch_shapes=[held, held, held, pltpu.SemaphoreType.DMA((moved.shape[0],))],
+        compiler_params=pltpu.CompilerParams(vmem_limit_bytes=VMEM_GRANT),
+        cost_estimate=pl.CostEstimate(
+            flops=2 * modes * rows * focus.size * (length // (focus.shape[1] // 2)) * 3,
+            bytes_accessed=12 << 20,
+            transcendentals=0,
+        ),
+    )(moved, cosine, sine, target, approach, focus, adjoint)
+
+
+def fast_shards(mode_field, figure, target, footprint, approach_tiles, focus_tiles):
+    modes = lax.axis_size("mode")
+    bands = lax.axis_size("band")
+    mode_index = lax.axis_index("mode")
+    band_index = lax.axis_index("band")
+    rows, length = figure.shape
+    share = rows // modes
+    blocks = length // MIRROR_TILE
+    slots = max(2, 2 * blocks // bands)
+    tile = approach_tiles.shape[-1]
+
+    source_band = footprint // blocks
+    source_block = footprint % blocks
+    column = jnp.arange(blocks, dtype=jnp.int32)
+    same = source_band[:, :, None] == source_band[:, None, :]
+    rank = jnp.sum((same & (column[None, :] < column[:, None])[None]).astype(jnp.int32), axis=2)
+    slot_ids = jnp.arange(slots, dtype=jnp.int32)
+    from_here = (source_band == band_index)[:, None, :] & (
+        rank[:, None, :] == slot_ids[None, :, None]
+    )
+    asked_block = jnp.sum(jnp.where(from_here, source_block[:, None, :], 0), axis=2).reshape(-1)
+    asked = jnp.sum(from_here.astype(jnp.int32), axis=2).reshape(-1)
+    my_band = lax.dynamic_index_in_dim(source_band, band_index, 0, keepdims=False)
+    my_rank = lax.dynamic_index_in_dim(rank, band_index, 0, keepdims=False)
+    band_ids = jnp.arange(bands, dtype=jnp.int32)
+    mine = (my_band[None, None, :] == band_ids[:, None, None]) & (
+        my_rank[None, None, :] == slot_ids[None, :, None]
+    )
+    back_column = jnp.sum(jnp.where(mine, column[None, None, :], 0), axis=2).reshape(-1)
+    no_band = jnp.zeros_like(asked_block)
+
+    packed = (bands, share, slots * MIRROR_TILE)
+    heights = lax.dynamic_slice_in_dim(figure, mode_index * share, share, 0)[None]
+    outbound = gather_tiles(no_band, asked_block, heights, packed)
+    inbound = lax.all_to_all(outbound, "band", split_axis=0, concat_axis=0, tiled=True)
+
+    approach = real_kernels(approach_tiles)
+    focus = real_kernels(focus_tiles)
+    adjoint = jnp.transpose(focus, (0, 3, 4, 1, 2))[::-1]
+    flat = (3 * 2 * tile, 2 * tile)
+    turned_weight = jnp.transpose(approach, (3, 4, 1, 0, 2)).reshape(2 * tile, 3 * 2 * tile)
+    edges = ((0, 0), (tile, tile))
+    real_lines = jnp.pad(mode_field[0, :, 0], edges)
+    imag_lines = jnp.pad(mode_field[0, :, 1], edges)
+    turned = approach_turned(real_lines, imag_lines, turned_weight, modes, bands)
+    moved = lax.all_to_all(turned, ("mode", "band"), split_axis=0, concat_axis=0, tiled=True)
+
+    heights_here = gather_tiles(my_band, my_rank, inbound, (1, share, length))[0]
+    phase_delay = PHASE_FACTOR * heights_here.astype(jnp.float32)
+    cosine = jnp.cos(phase_delay)
+    sine = jnp.sin(phase_delay)
+    target_here = lax.dynamic_slice_in_dim(target, mode_index * share, share, 0)
+
+    beam = beam_sensitivity(
+        moved, cosine, sine, target_here,
+        approach.reshape(flat), focus.reshape(flat), adjoint.reshape(flat), modes,
+    )
+
+    back = gather_tiles(no_band, back_column, beam[None], packed)
+    returned = lax.all_to_all(back, "band", split_axis=0, concat_axis=0, tiled=True)
+    surface = collect_tiles(asked_block, asked, returned, length)
+
+    low = surface.astype(jnp.bfloat16)
+    pieces = [surface]
+    for step in range(1, modes):
+        ring = [(i, (i + step) % modes) for i in range(modes)]
+        pieces.append(lax.ppermute(low, "mode", ring).astype(jnp.float32))
+    out = []
+    for owner in range(modes):
+        chosen = pieces[0]
+        for step in range(1, modes):
+            chosen = jnp.where((mode_index - owner) % modes == step, pieces[step], chosen)
+        out.append(chosen)
+    return jnp.concatenate(out, axis=0)
+
+
 def solution(mesh):
+    modes, bands = mesh.shape["mode"], mesh.shape["band"]
+
+    def shards(mode_field, figure, target, footprint, approach_tiles, focus_tiles):
+        tile = approach_tiles.shape[-1]
+        share = figure.shape[0] // modes
+        fits = mode_field.shape[0] == 1 and share == tile and figure.shape[0] % tile == 0
+        fits = fits and tile == 2 * MIRROR_TILE and figure.shape[1] == modes * bands * tile
+        chosen = fast_shards if fits else general_shards
+        return chosen(mode_field, figure, target, footprint, approach_tiles, focus_tiles)
+
     in_specs = (P("mode", "band", None, None), P("band", None), P("band", None), P(), P(), P())
     out_specs = P("band", None)
     return jax.shard_map(shards, mesh=mesh, in_specs=in_specs, out_specs=out_specs, check_vma=False)

time: 764 us -> 288 us (0.38); the launches traced: 756 us -> 288 us
  waiting for transfers between devices: 315 us -> 150 us
  local copies, waits for them, and re-layouts: 187 us -> 38.8 us
  matrix products: 105 us -> 0 us
  blocking collectives: 98.3 us -> 0 us
  Pallas kernels: 0 us -> 61.1 us
  between operations: 13.6 us -> 0.31 us
  other arithmetic: 25.7 us -> 16.9 us
  starting transfers between devices: 12 us -> 20.1 us
    psum x1 -> x0, waiting for transfers between devices: 108 us -> none  [shards(): intensity = lax.psum(local_power, 'mode')]
    dot_general x17 -> x0, matrix products: 105 us -> none  [the longest x4 39.6 us: banded(): jnp.einsum('mrcbk,ckel->mrebl', reshaped_field, kernels[1], preferred_ele...]
    all_to_all x1 -> x0, blocking collectives: 98.3 us -> none  [shards(): lax.all_to_all(tiles_out(beam_share, receive_hot), 'band', split_axis=0,...]
    pallas_call x0 -> x6, Pallas kernels: none -> 61.1 us  [the longest x1 23.1 us: beam_sensitivity(): pl.pallas_call(functools.partial(beam_kernel, modes), out_shape=jax.Shape...]
    all_gather x1 -> x0, waiting for transfers between devices: 56.2 us -> none  [shards(): sensitivity = lax.all_gather(surface_share, 'mode', axis=0, tiled=True)]
    reduce_scatter x1 -> x0, waiting for transfers between devices: 54.4 us -> none  [shards(): lax.psum_scatter(local_sens, 'mode', scatter_dimension=0, tiled=True)]
    reshape x6, local copies, waits for them, and re-layouts: 51.2 us -> 3.13 us  [the longest x1 2.24 us: fast_shards(): adjoint.reshape(flat)]
    unnamed x40 -> x33, local copies, waits for them, and re-layouts: 41.4 us -> 11.3 us
  transfers between devices with their start and end apart: 5 -> 4, of which waited for: 5 -> 4; matrix products, arithmetic and copies ran while one was open for 12% -> 13% of each run, Pallas kernels for 0% -> 6%
where the time goes in v1:
time: 288 us
  waiting for transfers between devices  150 us (52%)
  Pallas kernels  61.1 us (21%)
  local copies, waits for them, and re-layouts  38.8 us (13%)
  starting transfers between devices  20.1 us (7%)
  other arithmetic  16.9 us (6%)
    all_to_all x1, waiting for transfers between devices, fast_shards(): lax.all_to_all(turned, ('mode', 'band'), split_axis=0, concat_axis=0, til...  72.8 us
    all_to_all x1, waiting for transfers between devices, fast_shards(): lax.all_to_all(back, 'band', split_axis=0, concat_axis=0, tiled=True)  47.2 us
    ppermute x1, waiting for transfers between devices, fast_shards(): pieces.append(lax.ppermute(low, 'mode', ring).astype(jnp.float32))  24.1 us
    pallas_call x1, Pallas kernels, beam_sensitivity(): pl.pallas_call(functools.partial(beam_kernel, modes), out_shape=jax.Shape...  23.1 us
    pallas_call x1, Pallas kernels, approach_turned(): pl.pallas_call(approach_kernel, out_shape=jax.ShapeDtypeStruct((tiles, ti...  15.7 us
    slice x1, local copies, waits for them, and re-layouts, fast_shards(): imag_lines = jnp.pad(mode_field[0, :, 1], edges)  13.4 us
    unnamed x33, local copies, waits for them, and re-layouts  11.3 us
    pallas_call x3, Pallas kernels, gather_tiles(): pl.pallas_call(gather_kernel, out_shape=jax.ShapeDtypeStruct(out_shape, d...  11.2 us
  transfers between devices with their start and end apart: 4, of which 4 were waited for; matrix products, arithmetic and copies ran while one was open for 13% of the time, Pallas kernels for 6%

profile of v1, /device:TPU:12, one launch (start us, length us, event | category | flops | bytes accessed | tf_op | source)
XLA Modules:
  0.0 287.7 jit_solution(2944163315244305626)
XLA Ops:
  0.0 0.0 copy-start
  0.0 0.9 add_select_fusion
  0.9 0.7 broadcast_compare_fusion
  1.6 0.5 convert_reduce_fusion
  2.1 1.0 convert_reduce_fusion.1
  3.0 0.1 reshape.112.block_ref
  3.1 0.0 copy-done
  3.1 0.1 dynamic-slice_bitcast_fusion.data_ref
  3.3 4.4 %shard_map.65 = bf16[16,128,512]{2,1,0:T(8,128)(2,1)S(1)} custom-call(s32[128]{0:T(128)S(1)} %broadcast_in_dim.26.band_ref, s32[128]{0:T(128)S(1)} %reshape.112.block_ref, bf16[1,128,4096]{2,1,0:T(8,128)(2,1)S(1)} %dynamic-slice_bitcast_fusion.data_ref), custom_call_target="tpu_custom_call" | custom-call | bytes 6291456 | tf_op jit(solution)/shard_map/pallas_call | solution.py:194
  7.6 0.0 copy-start.4
  7.6 1.3 copy-done.4
  9.0 6.2 %all-to-all-start.1 = ((bf16[16,128,512]{2,1,0:T(8,128)(2,1)}), bf16[16,128,512]{2,1,0:T(8,128)(2,1)S(1)}, u32[]{:S(2)}, u32[]{:S(2)}) async-start(bf16[16,128,512]{2,1,0:T(8,128)(2,1)} %copy-done.4), calls=%async_computation.1 | async-start | bytes 4194304 | tf_op jit(solution)/shard_map/all_to_all | solution.py:412
  15.2 13.4 %fusion.9 = (bf16[1,256,1,4096]{3,2,1,0:T(2,128)(2,1)S(1)}, bf16[1,256,1,4096]{3,2,1,0:T(2,128)(2,1)S(1)}) fusion(bf16[1,256,2,4096]{3,2,1,0:T(2,128)(2,1)} %param.6), kind=kLoop, calls=%fused_computation.49 | loop fusion | bytes 8388608 | tf_op jit(solution)/shard_map/slice | solution.py:421
  28.6 4.7 %copy_bitcast_fusion = (bf16[256,4096]{1,0:T(8,128)(2,1)S(1)}, bf16[256,4096]{1,0:T(8,128)(2,1)S(1)}) fusion(bf16[1,256,1,4096]{3,2,1,0:T(2,128)(2,1)S(1)} %get-tuple-element.9, bf16[1,256,1,4096]{3,2,1,0:T(2,128)(2,1)S(1)} %get-tuple-element.10), kind=kLoop, calls=%fused_computation.3 | loop fusion | bytes 8388608 | tf_op jit(solution)/shard_map/squeeze | solution.py:421
  33.4 1.5 pad.7.real_ref
  34.9 1.6 pad.8.imag_ref
  36.5 0.0 copy-done.13
  36.6 0.1 pad_maximum_fusion.1
  36.6 0.3 copy.33
  36.9 0.3 reshape.119.weight_ref
  37.3 0.0 copy-start.6
  37.3 1.6 copy-done.6
  38.9 1.6 copy-done.7
  40.5 15.7 %shard_map.64 = bf16[32,128,512]{2,1,0:T(8,128)(2,1)} custom-call(bf16[256,4352]{1,0:T(8,128)(2,1)S(1)} %copy-done.6, bf16[256,4352]{1,0:T(8,128)(2,1)S(1)} %copy-done.7, bf16[256,768]{1,0:T(8,128)(2,1)S(1)} %reshape.119.weight_ref), custom_call_target="tpu_custom_call" | custom-call | flops 3221225472 | bytes 8388608 | tf_op jit(solution)/shard_map/pallas_call | solution.py:257
  56.2 6.3 %all-to-all-done.1.data_ref = bf16[16,128,512]{2,1,0:T(8,128)(2,1)S(1)} async-done(((bf16[16,128,512]{2,1,0:T(8,128)(2,1)}), bf16[16,128,512]{2,1,0:T(8,128)(2,1)S(1)}, u32[]{:S(2)}, u32[]{:S(2)}) %all-to-all-start.1) | async-done | bytes 2097184 | tf_op jit(solution)/shard_map/all_to_all | solution.py:412
  62.5 4.9 %all-to-all-start = ((bf16[32,128,512]{2,1,0:T(8,128)(2,1)}), bf16[32,128,512]{2,1,0:T(8,128)(2,1)}, u32[]{:S(2)}, u32[]{:S(2)}) async-start(bf16[32,128,512]{2,1,0:T(8,128)(2,1)} %shard_map.64), calls=%async_computation | async-start | bytes 8388608 | tf_op jit(solution)/shard_map/all_to_all | solution.py:423
  67.4 0.0 copy-start.10
  67.4 0.5 copy-done.10
  67.9 0.3 select_reduce_fusion
  68.2 0.1 reshape.114.block_ref
  68.3 0.4 copy.29
  68.7 0.1 copy.47
  68.8 0.0 copy-done.14
  68.9 0.8 fusion.7
  69.7 1.0 rev.3
  70.7 1.1 copy.32
  71.8 0.4 copy.31
  72.2 2.2 copy_bitcast_fusion.2
  74.5 0.0 copy-done.12
  74.5 0.1 constant_dynamic-slice_fusion.target_ref
  74.5 0.0 copy-done.11
  74.5 2.5 shard_map.66
  77.0 8.2 %sine_bitcast_fusion = (f32[128,4096]{1,0:T(8,128)}, f32[128,4096]{1,0:T(8,128)S(1)}) fusion(bf16[1,128,4096]{2,1,0:T(8,128)(2,1)S(1)} %shard_map.66), kind=kLoop, calls=%fused_computation.5 | loop fusion | flops 1048576 | bytes 5242880 | tf_op jit(solution)/shard_map/sin | solution.py:428
  85.2 72.8 %all-to-all-done.moved_ref = bf16[32,128,512]{2,1,0:T(8,128)(2,1)} async-done(((bf16[32,128,512]{2,1,0:T(8,128)(2,1)}), bf16[32,128,512]{2,1,0:T(8,128)(2,1)}, u32[]{:S(2)}, u32[]{:S(2)}) %all-to-all-start) | async-done | bytes 4194336 | tf_op jit(solution)/shard_map/all_to_all | solution.py:423
  158.0 1.0 copy-done.8
  159.0 1.0 copy-done.9
  160.0 23.1 %shard_map.67 = bf16[128,4096]{1,0:T(8,128)(2,1)S(1)} custom-call(bf16[32,128,512]{2,1,0:T(8,128)(2,1)} %all-to-all-done.moved_ref, f32[128,4096]{1,0:T(8,128)S(1)} %get-tuple-element.14.cos_ref, f32[128,4096]{1,0:T(8,128)} %get-tuple-element.13.sin_ref, bf16[128,4096]{1,0:T(8,128)(2,1)S(1)} %constant_dynamic-slice_fusion.target_ref, ...), custom_call_target="tpu_custom_call" | custom-call | flops 9663676416 | bytes 12582912 | tf_op jit(solution)/shard_map/pallas_call | solution.py:363
  183.1 4.4 %shard_map.68 = bf16[16,128,512]{2,1,0:T(8,128)(2,1)S(1)} custom-call(s32[128]{0:T(128)S(1)} %broadcast_in_dim.26.band_ref, s32[128]{0:T(128)S(1)} %reshape.114.block_ref, bf16[1,128,4096]{2,1,0:T(8,128)(2,1)S(1)} %bitcast.56), custom_call_target="tpu_custom_call" | custom-call | bytes 6291456 | tf_op jit(solution)/shard_map/pallas_call | solution.py:194
  187.5 0.0 copy-start.5
  187.5 1.3 copy-done.5
  188.8 8.0 %all-to-all-start.2 = ((bf16[16,128,512]{2,1,0:T(8,128)(2,1)}), bf16[16,128,512]{2,1,0:T(8,128)(2,1)S(1)}, u32[]{:S(2)}, u32[]{:S(2)}) async-start(bf16[16,128,512]{2,1,0:T(8,128)(2,1)} %copy-done.5), calls=%async_computation.2 | async-start | bytes 4194304 | tf_op jit(solution)/shard_map/all_to_all | solution.py:437
  196.8 0.0 copy-done.15
  196.8 0.1 reshape.113.valid_ref
  196.9 47.2 %all-to-all-done.2.data_ref = bf16[16,128,512]{2,1,0:T(8,128)(2,1)S(1)} async-done(((bf16[16,128,512]{2,1,0:T(8,128)(2,1)}), bf16[16,128,512]{2,1,0:T(8,128)(2,1)S(1)}, u32[]{:S(2)}, u32[]{:S(2)}) %all-to-all-start.2) | async-done | bytes 2097184 | tf_op jit(solution)/shard_map/all_to_all | solution.py:437
  244.1 1.3 copy-done.2
  245.4 1.6 copy-done.3
  247.0 11.2 %shard_map.69 = f32[128,4096]{1,0:T(8,128)S(1)} custom-call(s32[128]{0:T(128)S(1)} %reshape.112.block_ref, s32[128]{0:T(128)S(1)} %reshape.113.valid_ref, bf16[16,128,512]{2,1,0:T(8,128)(2,1)S(1)} %copy-done.3), custom_call_target="tpu_custom_call" | custom-call | bytes 6291456 | tf_op jit(solution)/shard_map/pallas_call | solution.py:227
  258.1 0.1 convert_element_type.22
  258.3 1.1 collective-permute-start
  259.3 24.1 %collective-permute-done = bf16[128,4096]{1,0:T(8,128)(2,1)} collective-permute-done((bf16[128,4096]{1,0:T(8,128)(2,1)S(1)}, bf16[128,4096]{1,0:T(8,128)(2,1)}, u32[]{:S(2)}, u32[]{:S(2)}) %collective-permute-start) | collective-permute-done | bytes 1048608 | tf_op jit(solution)/shard_map/ppermute | solution.py:444
  283.5 1.7 convert_select_fusion.1
  285.2 0.0 copy-start.1
  285.2 2.5 pad_maximum_fusion
  287.7 0.0 copy-done.1
  (21 shorter events, 0.2 us)
Async XLA Ops:
  0.0 3.1 %copy-start = (bf16[256,4096]{1,0:T(8,128)(2,1)S(1)}, bf16[256,4096]{1,0:T(8,128)(2,1)}, u32[]{:S(2)}) copy-start(bf16[256,4096]{1,0:T(8,128)(2,1)} %param.7) | copy-start | bytes 6291460
  7.6 1.3 copy-start.4
  9.0 53.5 %all-to-all-start.1 = ((bf16[16,128,512]{2,1,0:T(8,128)(2,1)}), bf16[16,128,512]{2,1,0:T(8,128)(2,1)S(1)}, u32[]{:S(2)}, u32[]{:S(2)}) async-start(bf16[16,128,512]{2,1,0:T(8,128)(2,1)} %copy-done.4), calls=%async_computation.1 | async-start | bytes 4194304 | tf_op jit(solution)/shard_map/all_to_all | solution.py:412
  34.9 1.6 copy-start.13
  37.3 1.6 copy-start.6
  38.9 1.6 copy-start.7
  56.2 12.6 %copy-start.14 = (bf16[3,2,128,128]{3,2,1,0:T(8,128)(2,1)S(1)}, bf16[3,2,128,128]{3,2,1,0:T(8,128)(2,1)}, u32[]{:S(2)}) copy-start(bf16[3,2,128,128]{3,2,1,0:T(8,128)(2,1)} %param.11) | copy-start | bytes 589828
  62.5 95.6 %all-to-all-start = ((bf16[32,128,512]{2,1,0:T(8,128)(2,1)}), bf16[32,128,512]{2,1,0:T(8,128)(2,1)}, u32[]{:S(2)}, u32[]{:S(2)}) async-start(bf16[32,128,512]{2,1,0:T(8,128)(2,1)} %shard_map.64), calls=%async_computation | async-start | bytes 8388608 | tf_op jit(solution)/shard_map/all_to_all | solution.py:423
  67.4 0.5 copy-start.10
  71.8 2.7 copy-start.12
  71.8 2.7 copy-start.11
  158.0 1.0 copy-start.8
  159.0 1.0 copy-start.9
  187.5 1.3 copy-start.5
  188.8 8.0 %copy-start.15 = (s32[16,8]{1,0:T(8,128)S(1)}, s32[16,8]{1,0:T(8,128)}, u32[]{:S(2)}) copy-start(s32[16,8]{1,0:T(8,128)} %get-tuple-element.5) | copy-start | bytes 1540
  188.8 55.3 %all-to-all-start.2 = ((bf16[16,128,512]{2,1,0:T(8,128)(2,1)}), bf16[16,128,512]{2,1,0:T(8,128)(2,1)S(1)}, u32[]{:S(2)}, u32[]{:S(2)}) async-start(bf16[16,128,512]{2,1,0:T(8,128)(2,1)} %copy-done.5), calls=%async_computation.2 | async-start | bytes 4194304 | tf_op jit(solution)/shard_map/all_to_all | solution.py:437
  244.1 1.3 copy-start.2
  245.4 1.6 copy-start.3
  258.3 25.2 %collective-permute-start = (bf16[128,4096]{1,0:T(8,128)(2,1)S(1)}, bf16[128,4096]{1,0:T(8,128)(2,1)}, u32[]{:S(2)}, u32[]{:S(2)}) collective-permute-start(bf16[128,4096]{1,0:T(8,128)(2,1)S(1)} %convert_element_type.22), channel_id=1, source_target_pairs={{0,16},{16,0},{1,17},{17,1},{2,18},{18,2},{3,19},{19,3},{4,20},{20... | collective-permute-start | bytes 3145736 | tf_op jit(solution)/shard_map/ppermute | solution.py:444
  285.2 2.5 copy-start.1

commit v2 on v1

--- a/solution.py
+++ b/solution.py
@@ -161,6 +161,7 @@
 
 
 VMEM_GRANT = 48 * 1024 * 1024
+CHUNKS = 2
 
 
 def half_chunk(data_ref, band, block, to_right):
@@ -234,7 +235,7 @@
     )(blocks, valid, data)
 
 
-def approach_kernel(real_ref, imag_ref, weight_ref, out_ref):
+def approach_kernel(real_ref, imag_ref, weight_ref, *out_refs):
     tile = weight_ref.shape[0] // 2
     at = pl.multiple_of(pl.program_id(0) * tile, tile)
     lines = jnp.concatenate(
@@ -242,12 +243,15 @@
     )
     turned = lax.dot_general(
         weight_ref[...], lines, (((1,), (1,)), ((), ())), preferred_element_type=jnp.float32
-    ).astype(out_ref.dtype)
+    ).astype(out_refs[0].dtype)
+    lines_each = tile // len(out_refs)
     for half in range(lines.shape[0] // tile):
         for part in range(2):
-            out_ref[0, :, pl.ds((2 * half + part) * tile, tile)] = turned[
-                part * tile : (part + 1) * tile, half * tile : (half + 1) * tile
-            ]
+            for chunk, out_ref in enumerate(out_refs):
+                first = part * tile + chunk * lines_each
+                out_ref[0, :, pl.ds((2 * half + part) * tile, tile)] = turned[
+                    first : first + lines_each, half * tile : (half + 1) * tile
+                ]
 
 
 def approach_turned(real_lines, imag_lines, weight, modes, bands):
@@ -256,16 +260,19 @@
     tiles = modes * bands
     return pl.pallas_call(
         approach_kernel,
-        out_shape=jax.ShapeDtypeStruct((tiles, tile, 2 * rows), jnp.bfloat16),
+        out_shape=[jax.ShapeDtypeStruct((tiles, tile // CHUNKS, 2 * rows), jnp.bfloat16)] * CHUNKS,
         grid=(tiles,),
         in_specs=[
             pl.BlockSpec(real_lines.shape, lambda t: (0, 0)),
             pl.BlockSpec(imag_lines.shape, lambda t: (0, 0)),
             pl.BlockSpec(weight.shape, lambda t: (0, 0)),
         ],
-        out_specs=pl.BlockSpec(
-            (1, tile, 2 * rows), lambda t: ((t % modes) * bands + t // modes, 0, 0)
-        ),
+        out_specs=[
+            pl.BlockSpec(
+                (1, tile // CHUNKS, 2 * rows), lambda t: ((t % modes) * bands + t // modes, 0, 0)
+            )
+        ]
+        * CHUNKS,
         compiler_params=pltpu.CompilerParams(vmem_limit_bytes=VMEM_GRANT),
         cost_estimate=pl.CostEstimate(
             flops=2 * rows * weight.size * tiles, bytes_accessed=8 << 20, transcendentals=0
@@ -356,14 +363,16 @@
     lax.fori_loop(0, tiles, sens_step, 0, unroll=2)
 
 
-def beam_sensitivity(moved, cosine, sine, target, approach, focus, adjoint, modes):
-    rows, length = cosine.shape
+def beam_sensitivity(chunk, moved, cosine, sine, target, approach, focus, adjoint, modes):
+    rows, length = moved.shape[1], cosine.shape[1]
+    part = pl.BlockSpec((rows, length), lambda i: (chunk, 0))
     vmem = pl.BlockSpec(memory_space=pltpu.VMEM)
     held = pltpu.VMEM((modes * rows, 2 * length + 2 * focus.shape[1]), jnp.bfloat16)
     return pl.pallas_call(
         functools.partial(beam_kernel, modes),
         out_shape=jax.ShapeDtypeStruct((rows, length), jnp.bfloat16),
-        in_specs=[pl.BlockSpec(memory_space=pl.ANY)] + [vmem] * 6,
+        grid=(1,),
+        in_specs=[pl.BlockSpec(memory_space=pl.ANY)] + [part] * 3 + [vmem] * 3,
         out_specs=vmem,
         scratch_shapes=[held, held, held, pltpu.SemaphoreType.DMA((moved.shape[0],))],
         compiler_params=pltpu.CompilerParams(vmem_limit_bytes=VMEM_GRANT),
@@ -373,6 +382,31 @@
             transcendentals=0,
         ),
     )(moved, cosine, sine, target, approach, focus, adjoint)
+
+
+def join_kernel(owner_ref, *refs):
+    out_ref = refs[-1]
+    steps = owner_ref.shape[0]
+    lines = refs[0].shape[0]
+    each = (len(refs) - 1) // steps
+    for step in range(steps):
+        first = owner_ref[step] * (each * lines)
+        for chunk in range(each):
+            at = pl.multiple_of(first + chunk * lines, lines)
+            out_ref[pl.ds(at, lines), :] = refs[step * each + chunk][...].astype(out_ref.dtype)
+
+
+def join_shares(owners, pieces, rows, length):
+    flat = [piece for step in pieces for piece in step]
+    vmem = pl.BlockSpec(memory_space=pltpu.VMEM)
+    return pl.pallas_call(
+        join_kernel,
+        out_shape=jax.ShapeDtypeStruct((rows, length), jnp.float32),
+        in_specs=[pl.BlockSpec(memory_space=pltpu.SMEM)] + [vmem] * len(flat),
+        out_specs=vmem,
+        compiler_params=pltpu.CompilerParams(vmem_limit_bytes=VMEM_GRANT),
+        cost_estimate=pl.CostEstimate(flops=0, bytes_accessed=8 << 20, transcendentals=0),
+    )(owners, *flat)
 
 
 def fast_shards(mode_field, figure, target, footprint, approach_tiles, focus_tiles):
@@ -420,7 +454,10 @@
     real_lines = jnp.pad(mode_field[0, :, 0], edges)
     imag_lines = jnp.pad(mode_field[0, :, 1], edges)
     turned = approach_turned(real_lines, imag_lines, turned_weight, modes, bands)
-    moved = lax.all_to_all(turned, ("mode", "band"), split_axis=0, concat_axis=0, tiled=True)
+    moved = [
+        lax.all_to_all(part, ("mode", "band"), split_axis=0, concat_axis=0, tiled=True)
+        for part in turned
+    ]
 
     heights_here = gather_tiles(my_band, my_rank, inbound, (1, share, length))[0]
     phase_delay = PHASE_FACTOR * heights_here.astype(jnp.float32)
@@ -428,27 +465,21 @@
     sine = jnp.sin(phase_delay)
     target_here = lax.dynamic_slice_in_dim(target, mode_index * share, share, 0)
 
-    beam = beam_sensitivity(
-        moved, cosine, sine, target_here,
-        approach.reshape(flat), focus.reshape(flat), adjoint.reshape(flat), modes,
-    )
-
-    back = gather_tiles(no_band, back_column, beam[None], packed)
-    returned = lax.all_to_all(back, "band", split_axis=0, concat_axis=0, tiled=True)
-    surface = collect_tiles(asked_block, asked, returned, length)
-
-    low = surface.astype(jnp.bfloat16)
-    pieces = [surface]
-    for step in range(1, modes):
-        ring = [(i, (i + step) % modes) for i in range(modes)]
-        pieces.append(lax.ppermute(low, "mode", ring).astype(jnp.float32))
-    out = []
-    for owner in range(modes):
-        chosen = pieces[0]
+    weights = (approach.reshape(flat), focus.reshape(flat), adjoint.reshape(flat))
+    packed_part = (bands, share // CHUNKS, slots * MIRROR_TILE)
+    pieces = [[] for step in range(modes)]
+    for chunk in range(CHUNKS):
+        beam = beam_sensitivity(chunk, moved[chunk], cosine, sine, target_here, *weights, modes)
+        back = gather_tiles(no_band, back_column, beam[None], packed_part)
+        returned = lax.all_to_all(back, "band", split_axis=0, concat_axis=0, tiled=True)
+        surface = collect_tiles(asked_block, asked, returned, length)
+        pieces[0].append(surface)
+        low = surface.astype(jnp.bfloat16)
         for step in range(1, modes):
-            chosen = jnp.where((mode_index - owner) % modes == step, pieces[step], chosen)
-        out.append(chosen)
-    return jnp.concatenate(out, axis=0)
+            ring = [(i, (i + step) % modes) for i in range(modes)]
+            pieces[step].append(lax.ppermute(low, "mode", ring))
+    owners = jnp.remainder(mode_index - jnp.arange(modes, dtype=jnp.int32), modes)
+    return join_shares(owners.astype(jnp.int32), pieces, rows, length)
 
 
 def solution(mesh):

time: 288 us -> 259 us (0.90)
  waiting for transfers between devices: 150 us -> 43.3 us
  blocking collectives: 0 us -> 51.5 us
  Pallas kernels: 61.1 us -> 84.2 us
  starting transfers between devices: 20.1 us -> 28.7 us
  local copies, waits for them, and re-layouts: 38.8 us -> 35.2 us
  other arithmetic: 16.9 us -> 13.6 us
    all_to_all x1, waiting for transfers between devices: 72.8 us -> 6.61 us  [fast_shards(): lax.all_to_all(part, ('mode', 'band'), split_axis=0, concat_axis=0, tiled...]
    all_to_all x0 -> x1, blocking collectives: none -> 51.5 us  [fast_shards(): lax.all_to_all(part, ('mode', 'band'), split_axis=0, concat_axis=0, tiled...]
    all_to_all x1 -> x2, waiting for transfers between devices: 47.2 us -> 13.6 us  [fast_shards(): lax.all_to_all(back, 'band', split_axis=0, concat_axis=0, tiled=True)]
    ppermute x1 -> x2, waiting for transfers between devices: 24.1 us -> 12.8 us  [fast_shards(): pieces[step].append(lax.ppermute(low, 'mode', ring))]
    pallas_call x1 -> x2, Pallas kernels: 23.1 us -> 33.1 us  [beam_sensitivity(): pl.pallas_call(functools.partial(beam_kernel, modes), out_shape=jax.Shape...]
    pallas_call x3 -> x4, Pallas kernels: 11.2 us -> 18.1 us  [gather_tiles(): pl.pallas_call(gather_kernel, out_shape=jax.ShapeDtypeStruct(out_shape, d...]
    all_to_all x1 -> x2, starting transfers between devices: 7.96 us -> 14.3 us  [fast_shards(): lax.all_to_all(back, 'band', split_axis=0, concat_axis=0, tiled=True)]
    pallas_call x1 -> x2, Pallas kernels: 11.2 us -> 17.2 us  [collect_tiles(): pl.pallas_call(collect_kernel, out_shape=jax.ShapeDtypeStruct((data.shape...]
  transfers between devices with their start and end apart: 4 -> 6, of which waited for: 4 -> 4; matrix products, arithmetic and copies ran while one was open for 13% -> 14% of each run, Pallas kernels for 6% -> 30%
where the time goes in v2:
time: 259 us; the launch traced here: 257 us
  Pallas kernels  84.2 us (33%)
  blocking collectives  51.5 us (20%)
  waiting for transfers between devices  43.3 us (17%)
  local copies, waits for them, and re-layouts  35.2 us (14%)
  starting transfers between devices  28.7 us (11%)
  other arithmetic  13.6 us (5%)
    all_to_all x1, blocking collectives, fast_shards(): lax.all_to_all(part, ('mode', 'band'), split_axis=0, concat_axis=0, tiled...  51.5 us
    pallas_call x2, Pallas kernels, beam_sensitivity(): pl.pallas_call(functools.partial(beam_kernel, modes), out_shape=jax.Shape...  33.1 us
    pallas_call x4, Pallas kernels, gather_tiles(): pl.pallas_call(gather_kernel, out_shape=jax.ShapeDtypeStruct(out_shape, d...  18.1 us
    pallas_call x2, Pallas kernels, collect_tiles(): pl.pallas_call(collect_kernel, out_shape=jax.ShapeDtypeStruct((data.shape...  17.2 us
    all_to_all x2, starting transfers between devices, fast_shards(): lax.all_to_all(back, 'band', split_axis=0, concat_axis=0, tiled=True)  14.3 us
    all_to_all x2, waiting for transfers between devices, fast_shards(): lax.all_to_all(back, 'band', split_axis=0, concat_axis=0, tiled=True)  13.6 us
    slice x1, local copies, waits for them, and re-layouts, fast_shards(): imag_lines = jnp.pad(mode_field[0, :, 1], edges)  13.4 us
    ppermute x2, waiting for transfers between devices, fast_shards(): pieces[step].append(lax.ppermute(low, 'mode', ring))  12.8 us
  transfers between devices with their start and end apart: 6, of which 4 were waited for; matrix products, arithmetic and copies ran while one was open for 14% of the time, Pallas kernels for 30%

profile of v2, /device:TPU:12, one launch (start us, length us, event | category | flops | bytes accessed | tf_op | source)
XLA Modules:
  0.0 256.8 jit_solution(482891385544406996)
XLA Ops:
  0.0 0.9 add_select_fusion
  0.9 0.7 broadcast_compare_fusion
  1.6 0.5 convert_reduce_fusion
  2.1 1.0 convert_reduce_fusion.1
  3.1 0.1 reshape.112.block_ref
  3.1 0.0 copy-done
  3.1 0.1 dynamic-slice_bitcast_fusion.data_ref
  3.2 4.4 %shard_map.65 = bf16[16,128,512]{2,1,0:T(8,128)(2,1)S(1)} custom-call(s32[128]{0:T(128)S(1)} %broadcast_in_dim.32.band_ref, s32[128]{0:T(128)S(1)} %reshape.112.block_ref, bf16[1,128,4096]{2,1,0:T(8,128)(2,1)S(1)} %dynamic-slice_bitcast_fusion.data_ref), custom_call_target="tpu_custom_call" | custom-call | bytes 6291456 | tf_op jit(solution)/shard_map/pallas_call | solution.py:195
  7.6 1.4 copy-done.1
  9.0 6.2 %all-to-all-start.1 = ((bf16[16,128,512]{2,1,0:T(8,128)(2,1)}), bf16[16,128,512]{2,1,0:T(8,128)(2,1)}, u32[]{:S(2)}, u32[]{:S(2)}) async-start(bf16[16,128,512]{2,1,0:T(8,128)(2,1)} %copy-done.1), calls=%async_computation.1 | async-start | bytes 4194304 | tf_op jit(solution)/shard_map/all_to_all | solution.py:446
  15.3 13.4 %fusion.10 = (bf16[1,256,1,4096]{3,2,1,0:T(2,128)(2,1)S(1)}, bf16[1,256,1,4096]{3,2,1,0:T(2,128)(2,1)S(1)}) fusion(bf16[1,256,2,4096]{3,2,1,0:T(2,128)(2,1)} %param.6), kind=kLoop, calls=%fused_computation.50 | loop fusion | bytes 8388608 | tf_op jit(solution)/shard_map/slice | solution.py:455
  28.7 4.7 %copy_bitcast_fusion = (bf16[256,4096]{1,0:T(8,128)(2,1)S(1)}, bf16[256,4096]{1,0:T(8,128)(2,1)S(1)}) fusion(bf16[1,256,1,4096]{3,2,1,0:T(2,128)(2,1)S(1)} %get-tuple-element.13, bf16[1,256,1,4096]{3,2,1,0:T(2,128)(2,1)S(1)} %get-tuple-element.14), kind=kLoop, calls=%fused_computation | loop fusion | bytes 8388608 | tf_op jit(solution)/shard_map/squeeze | solution.py:455
  33.5 1.5 pad.7.real_ref
  35.0 1.6 pad.8.imag_ref
  36.7 0.1 pad_maximum_fusion
  36.7 0.3 copy.33
  37.0 0.3 reshape.119.weight_ref
  37.4 12.4 %shard_map.64 = (bf16[32,64,512]{2,1,0:T(8,128)(2,1)S(1)}, bf16[32,64,512]{2,1,0:T(8,128)(2,1)S(1)}) custom-call(bf16[256,4352]{1,0:T(8,128)(2,1)} %pad.7.real_ref, bf16[256,4352]{1,0:T(8,128)(2,1)} %pad.8.imag_ref, bf16[256,768]{1,0:T(8,128)(2,1)S(1)} %reshape.119.weight_ref), custom_call_target="tpu_custom_call" | custom-call | flops 3221225472 | bytes 8388608 | tf_op jit(solution)/shard_map/pallas_call | solution.py:261
  49.8 0.0 copy-start.4
  49.8 1.3 copy-done.4
  51.1 1.3 copy-done.6
  52.4 10.3 %all-to-all-done.1.data_ref = bf16[16,128,512]{2,1,0:T(8,128)(2,1)} async-done(((bf16[16,128,512]{2,1,0:T(8,128)(2,1)}), bf16[16,128,512]{2,1,0:T(8,128)(2,1)}, u32[]{:S(2)}, u32[]{:S(2)}) %all-to-all-start.1) | async-done | bytes 2097184 | tf_op jit(solution)/shard_map/all_to_all | solution.py:446
  62.6 51.5 %all_to_all.25.moved_ref = bf16[32,64,512]{2,1,0:T(8,128)(2,1)} all-to-all(bf16[32,64,512]{2,1,0:T(8,128)(2,1)} %copy-done.6), channel_id=1, replica_groups=mesh['mode'=2,'band'=16] {'mode','band'}, dimensions={0} | all-to-all | bytes 4194304 | tf_op jit(solution)/shard_map/all_to_all | solution.py:458
  114.1 6.6 %all-to-all-start.3 = ((bf16[32,64,512]{2,1,0:T(8,128)(2,1)}), bf16[32,64,512]{2,1,0:T(8,128)(2,1)}, u32[]{:S(2)}, u32[]{:S(2)}) async-start(bf16[32,64,512]{2,1,0:T(8,128)(2,1)} %copy-done.4), calls=%async_computation.3 | async-start | bytes 4194304 | tf_op jit(solution)/shard_map/all_to_all | solution.py:458
  120.8 0.4 select_reduce_fusion
  121.1 0.1 reshape.114.block_ref
  121.2 0.4 copy.29
  121.6 0.1 copy.47
  121.8 0.8 fusion.8
  122.6 1.0 rev.3
  123.6 1.1 copy.32
  124.7 0.4 copy.31
  125.1 1.3 copy_bitcast_fusion.2
  126.4 0.0 copy-done.13
  126.4 0.0 copy-start.9
  126.4 0.0 copy-start.11
  126.5 0.1 constant_dynamic-slice_fusion.2.target_ref
  126.6 0.0 copy-start.7
  126.6 4.0 %shard_map.66 = bf16[1,128,4096]{2,1,0:T(8,128)(2,1)S(1)} custom-call(s32[64]{0:T(128)S(1)} %get-tuple-element.29.band_ref, s32[64]{0:T(128)S(1)} %get-tuple-element.30.block_ref, bf16[16,128,512]{2,1,0:T(8,128)(2,1)} %all-to-all-done.1.data_ref), custom_call_target="tpu_custom_call" | custom-call | bytes 6291456 | tf_op jit(solution)/shard_map/pallas_call | solution.py:195
  130.6 8.3 %sine_bitcast_fusion = (f32[128,4096]{1,0:T(8,128)}, f32[128,4096]{1,0:T(8,128)}) fusion(bf16[1,128,4096]{2,1,0:T(8,128)(2,1)S(1)} %shard_map.66), kind=kLoop, calls=%fused_computation.2 | loop fusion | flops 1048576 | bytes 5242880 | tf_op jit(solution)/shard_map/sin | solution.py:465
  139.0 16.0 %shard_map.67 = bf16[64,4096]{1,0:T(8,128)(2,1)S(1)} custom-call(bf16[32,64,512]{2,1,0:T(8,128)(2,1)S(1)} %copy-done.5, f32[128,4096]{1,0:T(8,128)} %get-tuple-element.16.cos_ref, f32[128,4096]{1,0:T(8,128)} %get-tuple-element.15.sin_ref, bf16[128,4096]{1,0:T(8,128)(2,1)S(1)} %constant_dynamic-slice_fusion.2.target_ref, bf16[768,256]{1,0:T(8,128)(2,1)S(1)} %bitcast.59, ...), custom_call_target="tpu_custom_call" | custom-call | flops 4831838208 | bytes 12582912 | tf_op jit(solution)/shard_map/pallas_call | solution.py:371
  155.0 4.8 %shard_map.68 = bf16[16,64,512]{2,1,0:T(8,128)(2,1)} custom-call(s32[128]{0:T(128)S(1)} %broadcast_in_dim.32.band_ref, s32[128]{0:T(128)S(1)} %reshape.114.block_ref, bf16[1,64,4096]{2,1,0:T(8,128)(2,1)S(1)} %bitcast.58), custom_call_target="tpu_custom_call" | custom-call | bytes 6291456 | tf_op jit(solution)/shard_map/pallas_call | solution.py:195
  159.8 6.6 %all-to-all-done.3.moved_ref = bf16[32,64,512]{2,1,0:T(8,128)(2,1)} async-done(((bf16[32,64,512]{2,1,0:T(8,128)(2,1)}), bf16[32,64,512]{2,1,0:T(8,128)(2,1)}, u32[]{:S(2)}, u32[]{:S(2)}) %all-to-all-start.3) | async-done | bytes 2097184 | tf_op jit(solution)/shard_map/all_to_all | solution.py:458
  166.5 8.2 %all-to-all-start.2 = ((bf16[16,64,512]{2,1,0:T(8,128)(2,1)}), bf16[16,64,512]{2,1,0:T(8,128)(2,1)S(1)}, u32[]{:S(2)}, u32[]{:S(2)}) async-start(bf16[16,64,512]{2,1,0:T(8,128)(2,1)} %shard_map.68), calls=%async_computation.2 | async-start | bytes 2097152 | tf_op jit(solution)/shard_map/all_to_all | solution.py:474
  174.7 1.2 copy-done.8
  175.9 1.0 copy-done.10
  176.9 1.0 copy-done.12
  177.9 17.1 %shard_map.70 = bf16[64,4096]{1,0:T(8,128)(2,1)S(1)} custom-call(bf16[32,64,512]{2,1,0:T(8,128)(2,1)} %all-to-all-done.3.moved_ref, f32[128,4096]{1,0:T(8,128)} %get-tuple-element.16.cos_ref, f32[128,4096]{1,0:T(8,128)} %get-tuple-element.15.sin_ref, bf16[128,4096]{1,0:T(8,128)(2,1)S(1)} %copy-done.8, bf16[768,256]{1,0:T(8,128)(2,1)S(1)} %bitcast.60, ...), custom_call_target="tpu_custom_call" | custom-call | flops 4831838208 | bytes 12582912 | tf_op jit(solution)/shard_map/pallas_call | solution.py:371
  195.1 4.9 %shard_map.71 = bf16[16,64,512]{2,1,0:T(8,128)(2,1)} custom-call(s32[128]{0:T(128)S(1)} %broadcast_in_dim.32.band_ref, s32[128]{0:T(128)S(1)} %reshape.114.block_ref, bf16[1,64,4096]{2,1,0:T(8,128)(2,1)S(1)} %bitcast.57), custom_call_target="tpu_custom_call" | custom-call | bytes 6291456 | tf_op jit(solution)/shard_map/pallas_call | solution.py:195
  199.9 0.0 all-to-all-done.2.data_ref
  199.9 6.1 %all-to-all-start.4 = ((bf16[16,64,512]{2,1,0:T(8,128)(2,1)}), bf16[16,64,512]{2,1,0:T(8,128)(2,1)}, u32[]{:S(2)}, u32[]{:S(2)}) async-start(bf16[16,64,512]{2,1,0:T(8,128)(2,1)} %shard_map.71), calls=%async_computation.4 | async-start | bytes 2097152 | tf_op jit(solution)/shard_map/all_to_all | solution.py:474
  206.0 0.1 reshape.113.valid_ref
  206.1 0.0 copy-start.3
  206.1 1.2 copy-done.3
  207.3 8.3 %shard_map.69.refs_0_ = f32[64,4096]{1,0:T(8,128)S(1)} custom-call(s32[128]{0:T(128)S(1)} %reshape.112.block_ref, s32[128]{0:T(128)S(1)} %reshape.113.valid_ref, bf16[16,64,512]{2,1,0:T(8,128)(2,1)S(1)} %copy-done.3), custom_call_target="tpu_custom_call" | custom-call | bytes 6291456 | tf_op jit(solution)/shard_map/pallas_call | solution.py:228
  215.6 0.8 convert_element_type.22
  216.4 0.8 collective-permute-start
  217.2 13.6 %all-to-all-done.4.data_ref = bf16[16,64,512]{2,1,0:T(8,128)(2,1)} async-done(((bf16[16,64,512]{2,1,0:T(8,128)(2,1)}), bf16[16,64,512]{2,1,0:T(8,128)(2,1)}, u32[]{:S(2)}, u32[]{:S(2)}) %all-to-all-start.4) | async-done | bytes 1048608 | tf_op jit(solution)/shard_map/all_to_all | solution.py:474
  230.8 9.0 %shard_map.72.refs_1_ = f32[64,4096]{1,0:T(8,128)S(1)} custom-call(s32[128]{0:T(128)S(1)} %reshape.112.block_ref, s32[128]{0:T(128)S(1)} %reshape.113.valid_ref, bf16[16,64,512]{2,1,0:T(8,128)(2,1)} %all-to-all-done.4.data_ref), custom_call_target="tpu_custom_call" | custom-call | bytes 6291456 | tf_op jit(solution)/shard_map/pallas_call | solution.py:228
  239.8 0.1 convert_element_type.23
  239.9 0.8 collective-permute-start.1
  240.7 0.0 collective-permute-done.refs_2_
  240.7 12.8 %collective-permute-done.1.refs_3_ = bf16[64,4096]{1,0:T(8,128)(2,1)S(1)} collective-permute-done((bf16[64,4096]{1,0:T(8,128)(2,1)S(1)}, bf16[64,4096]{1,0:T(8,128)(2,1)S(1)}, u32[]{:S(2)}, u32[]{:S(2)}) %collective-permute-start.1) | collective-permute-done | bytes 524320 | tf_op jit(solution)/shard_map/ppermute | solution.py:480
  253.5 3.3 %shard_map.73 = f32[256,4096]{1,0:T(8,128)} custom-call(s32[2]{0:T(128)S(1)} %and_select_fusion.owner_ref, f32[64,4096]{1,0:T(8,128)S(1)} %shard_map.69.refs_0_, f32[64,4096]{1,0:T(8,128)S(1)} %shard_map.72.refs_1_, bf16[64,4096]{1,0:T(8,128)(2,1)} %collective-permute-done.refs_2_, bf16[64,4096]{1,0:T(8,128)(2,1)S(1)} %collective-permute-done.1.refs_3_), custom_call_target="tpu_custom_call" | custom-call | bytes 8388608 | tf_op jit(solution)/shard_map/pallas_call | solution.py:402
  (32 shorter events, 0.2 us)
Async XLA Ops:
  0.0 3.1 %copy-start = (bf16[256,4096]{1,0:T(8,128)(2,1)S(1)}, bf16[256,4096]{1,0:T(8,128)(2,1)}, u32[]{:S(2)}) copy-start(bf16[256,4096]{1,0:T(8,128)(2,1)} %param.7) | copy-start | bytes 6291460
  7.6 1.4 copy-start.1
  9.0 53.6 %all-to-all-start.1 = ((bf16[16,128,512]{2,1,0:T(8,128)(2,1)}), bf16[16,128,512]{2,1,0:T(8,128)(2,1)}, u32[]{:S(2)}, u32[]{:S(2)}) async-start(bf16[16,128,512]{2,1,0:T(8,128)(2,1)} %copy-done.1), calls=%async_computation.1 | async-start | bytes 4194304 | tf_op jit(solution)/shard_map/all_to_all | solution.py:446
  35.0 1.6 copy-start.14
  49.8 1.3 copy-start.4
  51.1 1.3 copy-start.6
  114.1 7.6 %copy-start.15 = (bf16[3,2,128,128]{3,2,1,0:T(8,128)(2,1)S(1)}, bf16[3,2,128,128]{3,2,1,0:T(8,128)(2,1)}, u32[]{:S(2)}) copy-start(bf16[3,2,128,128]{3,2,1,0:T(8,128)(2,1)} %param.11) | copy-start | bytes 589828
  114.1 52.3 %all-to-all-start.3 = ((bf16[32,64,512]{2,1,0:T(8,128)(2,1)}), bf16[32,64,512]{2,1,0:T(8,128)(2,1)}, u32[]{:S(2)}, u32[]{:S(2)}) async-start(bf16[32,64,512]{2,1,0:T(8,128)(2,1)} %copy-done.4), calls=%async_computation.3 | async-start | bytes 4194304 | tf_op jit(solution)/shard_map/all_to_all | solution.py:458
  124.7 1.7 copy-start.13
  126.4 12.5 %copy-start.9 = (bf16[768,256]{1,0:T(8,128)(2,1)}, bf16[768,256]{1,0:T(8,128)(2,1)S(1)}, u32[]{:S(2)}) copy-start(bf16[768,256]{1,0:T(8,128)(2,1)S(1)} %get-tuple-element.33.adjoint_ref) | copy-start | bytes 1179652
  126.4 12.5 %copy-start.11 = (bf16[768,256]{1,0:T(8,128)(2,1)}, bf16[768,256]{1,0:T(8,128)(2,1)S(1)}, u32[]{:S(2)}) copy-start(bf16[768,256]{1,0:T(8,128)(2,1)S(1)} %get-tuple-element.34.focus_ref) | copy-start | bytes 1179652
  126.6 12.4 %copy-start.7 = (bf16[128,4096]{1,0:T(8,128)(2,1)}, bf16[128,4096]{1,0:T(8,128)(2,1)S(1)}, u32[]{:S(2)}) copy-start(bf16[128,4096]{1,0:T(8,128)(2,1)S(1)} %constant_dynamic-slice_fusion.2.target_ref) | copy-start | bytes 3145732
  130.6 8.4 %copy-start.5 = (bf16[32,64,512]{2,1,0:T(8,128)(2,1)S(1)}, bf16[32,64,512]{2,1,0:T(8,128)(2,1)}, u32[]{:S(2)}) copy-start(bf16[32,64,512]{2,1,0:T(8,128)(2,1)} %all_to_all.25.moved_ref) | copy-start | bytes 6291460
  166.5 33.5 %all-to-all-start.2 = ((bf16[16,64,512]{2,1,0:T(8,128)(2,1)}), bf16[16,64,512]{2,1,0:T(8,128)(2,1)S(1)}, u32[]{:S(2)}, u32[]{:S(2)}) async-start(bf16[16,64,512]{2,1,0:T(8,128)(2,1)} %shard_map.68), calls=%async_computation.2 | async-start | bytes 2097152 | tf_op jit(solution)/shard_map/all_to_all | solution.py:474
  174.7 1.2 copy-start.8
  175.9 1.0 copy-start.10
  176.9 1.0 copy-start.12
  195.0 11.0 %copy-start.16 = (s32[16,8]{1,0:T(8,128)S(1)}, s32[16,8]{1,0:T(8,128)}, u32[]{:S(2)}) copy-start(s32[16,8]{1,0:T(8,128)} %get-tuple-element.9) | copy-start | bytes 1540
  199.9 6.1 %copy-start.2 = (bf16[16,64,512]{2,1,0:T(8,128)(2,1)}, bf16[16,64,512]{2,1,0:T(8,128)(2,1)S(1)}, u32[]{:S(2)}) copy-start(bf16[16,64,512]{2,1,0:T(8,128)(2,1)S(1)} %all-to-all-done.2.data_ref) | copy-start | bytes 3145732
  199.9 30.9 %all-to-all-start.4 = ((bf16[16,64,512]{2,1,0:T(8,128)(2,1)}), bf16[16,64,512]{2,1,0:T(8,128)(2,1)}, u32[]{:S(2)}, u32[]{:S(2)}) async-start(bf16[16,64,512]{2,1,0:T(8,128)(2,1)} %shard_map.71), calls=%async_computation.4 | async-start | bytes 2097152 | tf_op jit(solution)/shard_map/all_to_all | solution.py:474
  206.1 1.2 copy-start.3
  216.4 24.2 %collective-permute-start = (bf16[64,4096]{1,0:T(8,128)(2,1)}, bf16[64,4096]{1,0:T(8,128)(2,1)}, u32[]{:S(2)}, u32[]{:S(2)}) collective-permute-start(bf16[64,4096]{1,0:T(8,128)(2,1)} %convert_element_type.22), channel_id=1, source_target_pairs={{0,16},{16,0},{1,17},{17,1},{2,18},{18,2},{3,19},{19,3},{4,20},{20... | collective-permute-start | bytes 1572872 | tf_op jit(solution)/shard_map/ppermute | solution.py:480
  239.9 13.6 %collective-permute-start.1 = (bf16[64,4096]{1,0:T(8,128)(2,1)S(1)}, bf16[64,4096]{1,0:T(8,128)(2,1)S(1)}, u32[]{:S(2)}, u32[]{:S(2)}) collective-permute-start(bf16[64,4096]{1,0:T(8,128)(2,1)S(1)} %convert_element_type.23), channel_id=1, source_target_pairs={{0,16},{16,0},{1,17},{17,1},{2,18},{18,2},{3,19},{19,3},{4,20},{20... | collective-permute-start | bytes 1572872 | tf_op jit(solution)/shard_map/ppermute | solution.py:480

commit v3 on v2

--- a/solution.py
+++ b/solution.py
@@ -1,4 +1,5 @@
 import functools
+import math
 
 import jax
 import jax.numpy as jnp
@@ -161,7 +162,7 @@
 
 
 VMEM_GRANT = 48 * 1024 * 1024
-CHUNKS = 2
+EIGHTHS = (5, 3)
 
 
 def half_chunk(data_ref, band, block, to_right):
@@ -186,7 +187,7 @@
         ).astype(out_ref.dtype)
         return carry
 
-    lax.fori_loop(0, pairs, one_pair, 0, unroll=2)
+    lax.fori_loop(0, pairs, one_pair, 0, unroll=8)
 
 
 def gather_tiles(bands, blocks, data, out_shape):
@@ -202,34 +203,45 @@
     )(bands, blocks, data)
 
 
-def collect_kernel(block_ref, valid_ref, data_ref, out_ref):
-    out_ref[...] = jnp.zeros_like(out_ref)
+def collect_kernel(block_ref, valid_ref, data_ref, out_ref, low_ref, *totals):
     bands, rows, length = data_ref.shape
     slots = length // MIRROR_TILE
     lane_half = lax.broadcasted_iota(jnp.int32, (rows, 128), 1) // MIRROR_TILE
-
-    def one_slot(slot, carry):
-        block = block_ref[slot]
-
-        @pl.when(valid_ref[slot] > 0)
-        def _():
-            tile = half_chunk(data_ref, slot // slots, slot % slots, block % 2)
+    for total in totals:
+        total[...] = jnp.zeros_like(total)
+
+    def some_slots(step, carry):
+        for turn, total in enumerate(totals):
+            slot = step * len(totals) + turn
+            block = block_ref[slot]
+            side = block % 2
+            tile = half_chunk(data_ref, slot // slots, slot % slots, side)
+            lanes = lane_half == jnp.where(valid_ref[slot] > 0, side, 2)
             start = pl.multiple_of((block // 2) * 128, 128)
-            out_ref[:, pl.ds(start, 128)] += jnp.where(lane_half == block % 2, tile, 0.0)
-
+            total[:, pl.ds(start, 128)] += jnp.where(lanes, tile, 0.0)
         return carry
 
-    lax.fori_loop(0, bands * slots, one_slot, 0)
+    lax.fori_loop(0, bands * slots // len(totals), some_slots, 0, unroll=2)
+    surface = totals[0][...]
+    for total in totals[1:]:
+        surface = surface + total[...]
+    out_ref[...] = surface
+    low_ref[...] = surface.astype(low_ref.dtype)
 
 
 def collect_tiles(blocks, valid, data, length):
     smem = pl.BlockSpec(memory_space=pltpu.SMEM)
     vmem = pl.BlockSpec(memory_space=pltpu.VMEM)
+    extent = (data.shape[1], length)
     return pl.pallas_call(
         collect_kernel,
-        out_shape=jax.ShapeDtypeStruct((data.shape[1], length), jnp.float32),
+        out_shape=[
+            jax.ShapeDtypeStruct(extent, jnp.float32),
+            jax.ShapeDtypeStruct(extent, jnp.bfloat16),
+        ],
         in_specs=[smem, smem, vmem],
-        out_specs=vmem,
+        out_specs=[vmem, vmem],
+        scratch_shapes=[pltpu.VMEM(extent, jnp.float32)] * 4,
         compiler_params=pltpu.CompilerParams(vmem_limit_bytes=VMEM_GRANT),
         cost_estimate=pl.CostEstimate(flops=0, bytes_accessed=6 << 20, transcendentals=0),
     )(blocks, valid, data)
@@ -244,23 +256,24 @@
     turned = lax.dot_general(
         weight_ref[...], lines, (((1,), (1,)), ((), ())), preferred_element_type=jnp.float32
     ).astype(out_refs[0].dtype)
-    lines_each = tile // len(out_refs)
     for half in range(lines.shape[0] // tile):
         for part in range(2):
-            for chunk, out_ref in enumerate(out_refs):
-                first = part * tile + chunk * lines_each
+            first = part * tile
+            for out_ref in out_refs:
+                last = first + out_ref.shape[1]
                 out_ref[0, :, pl.ds((2 * half + part) * tile, tile)] = turned[
-                    first : first + lines_each, half * tile : (half + 1) * tile
+                    first:last, half * tile : (half + 1) * tile
                 ]
-
-
-def approach_turned(real_lines, imag_lines, weight, modes, bands):
+                first = last
+
+
+def approach_turned(real_lines, imag_lines, weight, modes, bands, chunks):
     rows = real_lines.shape[0]
     tile = weight.shape[0] // 2
     tiles = modes * bands
     return pl.pallas_call(
         approach_kernel,
-        out_shape=[jax.ShapeDtypeStruct((tiles, tile // CHUNKS, 2 * rows), jnp.bfloat16)] * CHUNKS,
+        out_shape=[jax.ShapeDtypeStruct((tiles, each, 2 * rows), jnp.bfloat16) for each in chunks],
         grid=(tiles,),
         in_specs=[
             pl.BlockSpec(real_lines.shape, lambda t: (0, 0)),
@@ -269,10 +282,10 @@
         ],
         out_specs=[
             pl.BlockSpec(
-                (1, tile // CHUNKS, 2 * rows), lambda t: ((t % modes) * bands + t // modes, 0, 0)
+                (1, each, 2 * rows), lambda t: ((t % modes) * bands + t // modes, 0, 0)
             )
-        ]
-        * CHUNKS,
+            for each in chunks
+        ],
         compiler_params=pltpu.CompilerParams(vmem_limit_bytes=VMEM_GRANT),
         cost_estimate=pl.CostEstimate(
             flops=2 * rows * weight.size * tiles, bytes_accessed=8 << 20, transcendentals=0
@@ -281,7 +294,7 @@
 
 
 def beam_kernel(
-    modes, moved_ref, cos_ref, sin_ref, target_ref, approach_ref, focus_ref, adjoint_ref,
+    modes, first, moved_ref, cos_ref, sin_ref, target_ref, approach_ref, focus_ref, adjoint_ref,
     sens_ref, lines, screens, grads, sems,
 ):
     sources, rows, width = moved_ref.shape
@@ -317,7 +330,7 @@
         ref[:, pl.ds(pl.multiple_of((at + 1) * pair, pair), pair)] = value
 
     def columns(ref, at):
-        return ref[:, pl.ds(pl.multiple_of(at * tile, tile), tile)]
+        return ref[pl.ds(first, rows), pl.ds(pl.multiple_of(at * tile, tile), tile)]
 
     def product(ref, at, weight_ref):
         return jnp.dot(window(ref, at), weight_ref[...], preferred_element_type=jnp.float32)
@@ -358,21 +371,19 @@
         ).astype(sens_ref.dtype)
         return carry
 
-    lax.fori_loop(0, tiles, screen_step, 0, unroll=2)
-    lax.fori_loop(0, tiles, detect_step, 0, unroll=2)
-    lax.fori_loop(0, tiles, sens_step, 0, unroll=2)
-
-
-def beam_sensitivity(chunk, moved, cosine, sine, target, approach, focus, adjoint, modes):
+    lax.fori_loop(0, tiles, screen_step, 0, unroll=4)
+    lax.fori_loop(0, tiles, detect_step, 0, unroll=4)
+    lax.fori_loop(0, tiles, sens_step, 0, unroll=4)
+
+
+def beam_sensitivity(first, moved, cosine, sine, target, approach, focus, adjoint, modes):
     rows, length = moved.shape[1], cosine.shape[1]
-    part = pl.BlockSpec((rows, length), lambda i: (chunk, 0))
     vmem = pl.BlockSpec(memory_space=pltpu.VMEM)
     held = pltpu.VMEM((modes * rows, 2 * length + 2 * focus.shape[1]), jnp.bfloat16)
     return pl.pallas_call(
-        functools.partial(beam_kernel, modes),
+        functools.partial(beam_kernel, modes, first),
         out_shape=jax.ShapeDtypeStruct((rows, length), jnp.bfloat16),
-        grid=(1,),
-        in_specs=[pl.BlockSpec(memory_space=pl.ANY)] + [part] * 3 + [vmem] * 3,
+        in_specs=[pl.BlockSpec(memory_space=pl.ANY)] + [vmem] * 6,
         out_specs=vmem,
         scratch_shapes=[held, held, held, pltpu.SemaphoreType.DMA((moved.shape[0],))],
         compiler_params=pltpu.CompilerParams(vmem_limit_bytes=VMEM_GRANT),
@@ -387,13 +398,16 @@
 def join_kernel(owner_ref, *refs):
     out_ref = refs[-1]
     steps = owner_ref.shape[0]
-    lines = refs[0].shape[0]
     each = (len(refs) - 1) // steps
+    share = out_ref.shape[0] // steps
+    unit = math.gcd(*[ref.shape[0] for ref in refs])
     for step in range(steps):
-        first = owner_ref[step] * (each * lines)
-        for chunk in range(each):
-            at = pl.multiple_of(first + chunk * lines, lines)
-            out_ref[pl.ds(at, lines), :] = refs[step * each + chunk][...].astype(out_ref.dtype)
+        first = owner_ref[step] * share
+        for ref in refs[step * each : (step + 1) * each]:
+            lines = ref.shape[0]
+            at = pl.multiple_of(first, unit)
+            out_ref[pl.ds(at, lines), :] = ref[...].astype(out_ref.dtype)
+            first = first + lines
 
 
 def join_shares(owners, pieces, rows, length):
@@ -418,6 +432,7 @@
     share = rows // modes
     blocks = length // MIRROR_TILE
     slots = max(2, 2 * blocks // bands)
+    chunks = [share * eighths // sum(EIGHTHS) for eighths in EIGHTHS]
     tile = approach_tiles.shape[-1]
 
     source_band = footprint // blocks
@@ -453,7 +468,7 @@
     edges = ((0, 0), (tile, tile))
     real_lines = jnp.pad(mode_field[0, :, 0], edges)
     imag_lines = jnp.pad(mode_field[0, :, 1], edges)
-    turned = approach_turned(real_lines, imag_lines, turned_weight, modes, bands)
+    turned = approach_turned(real_lines, imag_lines, turned_weight, modes, bands, chunks)
     moved = [
         lax.all_to_all(part, ("mode", "band"), split_axis=0, concat_axis=0, tiled=True)
         for part in turned
@@ -466,15 +481,16 @@
     target_here = lax.dynamic_slice_in_dim(target, mode_index * share, share, 0)
 
     weights = (approach.reshape(flat), focus.reshape(flat), adjoint.reshape(flat))
-    packed_part = (bands, share // CHUNKS, slots * MIRROR_TILE)
     pieces = [[] for step in range(modes)]
-    for chunk in range(CHUNKS):
-        beam = beam_sensitivity(chunk, moved[chunk], cosine, sine, target_here, *weights, modes)
+    first = 0
+    for each, lines in zip(chunks, moved):
+        beam = beam_sensitivity(first, lines, cosine, sine, target_here, *weights, modes)
+        first += each
+        packed_part = (bands, each, slots * MIRROR_TILE)
         back = gather_tiles(no_band, back_column, beam[None], packed_part)
         returned = lax.all_to_all(back, "band", split_axis=0, concat_axis=0, tiled=True)
-        surface = collect_tiles(asked_block, asked, returned, length)
+        surface, low = collect_tiles(asked_block, asked, returned, length)
         pieces[0].append(surface)
-        low = surface.astype(jnp.bfloat16)
         for step in range(1, modes):
             ring = [(i, (i + step) % modes) for i in range(modes)]
             pieces[step].append(lax.ppermute(low, "mode", ring))

time: 259 us -> 249 us (0.961)
  blocking collectives: 51.5 us -> 0 us
  waiting for transfers between devices: 43.3 us -> 94.4 us
  Pallas kernels: 84.2 us -> 68.1 us
  starting transfers between devices: 28.7 us -> 32.9 us
  local copies, waits for them, and re-layouts: 35.2 us -> 39.4 us
    all_to_all x1 -> x0, blocking collectives: 51.5 us -> none  [fast_shards(): lax.all_to_all(part, ('mode', 'band'), split_axis=0, concat_axis=0, tiled...]
    all_to_all x1 -> x2, waiting for transfers between devices: 6.61 us -> 56 us  [fast_shards(): lax.all_to_all(part, ('mode', 'band'), split_axis=0, concat_axis=0, tiled...]
    all_to_all x2, waiting for transfers between devices: 13.6 us -> 22 us  [fast_shards(): lax.all_to_all(back, 'band', split_axis=0, concat_axis=0, tiled=True)]
    pallas_call x5, Pallas kernels: 62.7 us -> 54.5 us  [the longest x2 28.7 us: beam_sensitivity(): pl.pallas_call(functools.partial(beam_kernel, modes, first), out_shape=ja...]
    pallas_call x4, Pallas kernels: 18.1 us -> 10.8 us  [gather_tiles(): pl.pallas_call(gather_kernel, out_shape=jax.ShapeDtypeStruct(out_shape, d...]
    all_to_all x1 -> x2, starting transfers between devices: 6.58 us -> 12.6 us  [fast_shards(): lax.all_to_all(part, ('mode', 'band'), split_axis=0, concat_axis=0, tiled...]
    all_to_all x1, waiting for transfers between devices: 10.3 us -> 5.71 us  [fast_shards(): lax.all_to_all(outbound, 'band', split_axis=0, concat_axis=0, tiled=True)]
    unnamed x35 -> x41, local copies, waits for them, and re-layouts: 8.54 us -> 12.7 us
  transfers between devices with their start and end apart: 6 -> 7, of which waited for: 4 -> 5; matrix products, arithmetic and copies ran while one was open for 14% -> 15% of each run, Pallas kernels for 30% -> 25%
where the time goes in v3:
time: 249 us; the launch traced here: 248 us
  waiting for transfers between devices  94.4 us (38%)
  Pallas kernels  68.1 us (27%)
  local copies, waits for them, and re-layouts  39.4 us (16%)
  starting transfers between devices  32.9 us (13%)
  other arithmetic  12.3 us (5%)
    all_to_all x2, waiting for transfers between devices, fast_shards(): lax.all_to_all(part, ('mode', 'band'), split_axis=0, concat_axis=0, tiled...  56 us
    pallas_call x2, Pallas kernels, beam_sensitivity(): pl.pallas_call(functools.partial(beam_kernel, modes, first), out_shape=ja...  28.7 us
    all_to_all x2, waiting for transfers between devices, fast_shards(): lax.all_to_all(back, 'band', split_axis=0, concat_axis=0, tiled=True)  22 us
    pallas_call x1, Pallas kernels, approach_turned(): pl.pallas_call(approach_kernel, out_shape=[jax.ShapeDtypeStruct((tiles, e...  16.8 us
    slice x1, local copies, waits for them, and re-layouts, fast_shards(): imag_lines = jnp.pad(mode_field[0, :, 1], edges)  13.4 us
    unnamed x41, local copies, waits for them, and re-layouts  12.7 us
    all_to_all x2, starting transfers between devices, fast_shards(): lax.all_to_all(part, ('mode', 'band'), split_axis=0, concat_axis=0, tiled...  12.6 us
    all_to_all x2, starting transfers between devices, fast_shards(): lax.all_to_all(back, 'band', split_axis=0, concat_axis=0, tiled=True)  12.5 us
  transfers between devices with their start and end apart: 7, of which 5 were waited for; matrix products, arithmetic and copies ran while one was open for 15% of the time, Pallas kernels for 25%

profile of v3, /device:TPU:12, one launch (start us, length us, event | category | flops | bytes accessed | tf_op | source)
XLA Modules:
  0.0 247.5 jit_solution(2927867812038286386)
XLA Ops:
  0.0 0.9 add_select_fusion
  0.9 0.7 broadcast_compare_fusion
  1.6 0.5 convert_reduce_fusion
  2.1 0.6 convert_reduce_fusion.1
  2.7 0.1 reshape.112.block_ref
  2.8 0.1 dynamic-slice_bitcast_fusion.data_ref
  2.9 2.9 %shard_map.65 = bf16[16,128,512]{2,1,0:T(8,128)(2,1)S(1)} custom-call(s32[128]{0:T(128)S(1)} %broadcast_in_dim.32.band_ref, s32[128]{0:T(128)S(1)} %reshape.112.block_ref, bf16[1,128,4096]{2,1,0:T(8,128)(2,1)S(1)} %dynamic-slice_bitcast_fusion.data_ref), custom_call_target="tpu_custom_call" | custom-call | bytes 6291456 | tf_op jit(solution)/shard_map/pallas_call | solution.py:196
  5.9 1.3 copy-done.1
  7.2 6.2 %all-to-all-start.1 = ((bf16[16,128,512]{2,1,0:T(8,128)(2,1)}), bf16[16,128,512]{2,1,0:T(8,128)(2,1)}, u32[]{:S(2)}, u32[]{:S(2)}) async-start(bf16[16,128,512]{2,1,0:T(8,128)(2,1)} %copy-done.1), calls=%async_computation.1 | async-start | bytes 4194304 | tf_op jit(solution)/shard_map/all_to_all | solution.py:461
  13.4 13.4 %fusion.10 = (bf16[1,256,1,4096]{3,2,1,0:T(2,128)(2,1)S(1)}, bf16[1,256,1,4096]{3,2,1,0:T(2,128)(2,1)S(1)}) fusion(bf16[1,256,2,4096]{3,2,1,0:T(2,128)(2,1)} %param.6), kind=kLoop, calls=%fused_computation.50 | loop fusion | bytes 8388608 | tf_op jit(solution)/shard_map/slice | solution.py:470
  26.9 4.7 %copy_bitcast_fusion = (bf16[256,4096]{1,0:T(8,128)(2,1)S(1)}, bf16[256,4096]{1,0:T(8,128)(2,1)S(1)}) fusion(bf16[1,256,1,4096]{3,2,1,0:T(2,128)(2,1)S(1)} %get-tuple-element.21, bf16[1,256,1,4096]{3,2,1,0:T(2,128)(2,1)S(1)} %get-tuple-element.22), kind=kLoop, calls=%fused_computation | loop fusion | bytes 8388608 | tf_op jit(solution)/shard_map/squeeze | solution.py:470
  31.6 1.5 pad.7.real_ref
  33.2 1.6 pad.8.imag_ref
  34.8 0.1 pad_maximum_fusion
  34.9 0.3 copy.33
  35.2 0.3 reshape.119.weight_ref
  35.5 0.0 copy-start.4
  35.5 1.6 copy-done.4
  37.2 16.8 %shard_map.64 = (bf16[32,80,512]{2,1,0:T(8,128)(2,1)}, bf16[32,48,512]{2,1,0:T(8,128)(2,1)S(1)}) custom-call(bf16[256,4352]{1,0:T(8,128)(2,1)S(1)} %copy-done.4, bf16[256,4352]{1,0:T(8,128)(2,1)} %pad.8.imag_ref, bf16[256,768]{1,0:T(8,128)(2,1)S(1)} %reshape.119.weight_ref), custom_call_target="tpu_custom_call" | custom-call | flops 3221225472 | bytes 8388608 | tf_op jit(solution)/shard_map/pallas_call | solution.py:274
  53.9 1.1 copy-done.6
  55.1 5.7 %all-to-all-done.1.data_ref = bf16[16,128,512]{2,1,0:T(8,128)(2,1)} async-done(((bf16[16,128,512]{2,1,0:T(8,128)(2,1)}), bf16[16,128,512]{2,1,0:T(8,128)(2,1)}, u32[]{:S(2)}, u32[]{:S(2)}) %all-to-all-start.1) | async-done | bytes 2097184 | tf_op jit(solution)/shard_map/all_to_all | solution.py:461
  60.8 4.9 %all-to-all-start = ((bf16[32,80,512]{2,1,0:T(8,128)(2,1)}), bf16[32,80,512]{2,1,0:T(8,128)(2,1)}, u32[]{:S(2)}, u32[]{:S(2)}) async-start(bf16[32,80,512]{2,1,0:T(8,128)(2,1)} %get-tuple-element.11), calls=%async_computation | async-start | bytes 5242880 | tf_op jit(solution)/shard_map/all_to_all | solution.py:473
  65.7 0.4 select_reduce_fusion
  66.1 0.1 reshape.114.block_ref
  66.1 0.4 copy.29
  66.6 0.0 copy-start.19
  66.6 0.1 copy.47
  66.7 56.0 %all-to-all-done.moved_ref = bf16[32,80,512]{2,1,0:T(8,128)(2,1)} async-done(((bf16[32,80,512]{2,1,0:T(8,128)(2,1)}), bf16[32,80,512]{2,1,0:T(8,128)(2,1)}, u32[]{:S(2)}, u32[]{:S(2)}) %all-to-all-start) | async-done | bytes 2621472 | tf_op jit(solution)/shard_map/all_to_all | solution.py:473
  122.6 7.8 %all-to-all-start.3 = ((bf16[32,48,512]{2,1,0:T(8,128)(2,1)}), bf16[32,48,512]{2,1,0:T(8,128)(2,1)}, u32[]{:S(2)}, u32[]{:S(2)}) async-start(bf16[32,48,512]{2,1,0:T(8,128)(2,1)} %copy-done.6), calls=%async_computation.3 | async-start | bytes 3145728 | tf_op jit(solution)/shard_map/all_to_all | solution.py:473
  130.5 0.8 fusion.8
  131.3 1.0 rev.3
  132.3 1.1 copy.32
  133.4 0.4 copy.31
  133.8 1.3 copy_bitcast_fusion.2
  135.2 0.1 constant_dynamic-slice_fusion.2.target_ref
  135.3 0.0 copy-start.9
  135.3 3.2 %shard_map.66 = bf16[1,128,4096]{2,1,0:T(8,128)(2,1)S(1)} custom-call(s32[64]{0:T(128)S(1)} %get-tuple-element.37.band_ref, s32[64]{0:T(128)S(1)} %get-tuple-element.38.block_ref, bf16[16,128,512]{2,1,0:T(8,128)(2,1)} %all-to-all-done.1.data_ref), custom_call_target="tpu_custom_call" | custom-call | bytes 6291456 | tf_op jit(solution)/shard_map/pallas_call | solution.py:196
  138.5 8.2 %sine_bitcast_fusion = (f32[128,4096]{1,0:T(8,128)}, f32[128,4096]{1,0:T(8,128)S(1)}) fusion(bf16[1,128,4096]{2,1,0:T(8,128)(2,1)S(1)} %shard_map.66), kind=kLoop, calls=%fused_computation.2 | loop fusion | flops 1048576 | bytes 5242880 | tf_op jit(solution)/shard_map/sin | solution.py:480
  146.8 15.1 %shard_map.67 = bf16[80,4096]{1,0:T(8,128)(2,1)S(1)} custom-call(bf16[32,80,512]{2,1,0:T(8,128)(2,1)} %all-to-all-done.moved_ref, f32[128,4096]{1,0:T(8,128)S(1)} %get-tuple-element.24.cos_ref, f32[128,4096]{1,0:T(8,128)} %get-tuple-element.23.sin_ref, bf16[128,4096]{1,0:T(8,128)(2,1)S(1)} %constant_dynamic-slice_fusion.2.target_ref, ...), custom_call_target="tpu_custom_call" | custom-call | flops 6039797760 | bytes 12582912 | tf_op jit(solution)/shard_map/pallas_call | solution.py:383
  161.9 2.4 shard_map.68
  164.3 1.1 copy-done.2
  165.4 0.0 all-to-all-done.3.moved_ref
  165.4 7.5 %all-to-all-start.2 = ((bf16[16,80,512]{2,1,0:T(8,128)(2,1)}), bf16[16,80,512]{2,1,0:T(8,128)(2,1)S(1)}, u32[]{:S(2)}, u32[]{:S(2)}) async-start(bf16[16,80,512]{2,1,0:T(8,128)(2,1)} %copy-done.2), calls=%async_computation.2 | async-start | bytes 2621440 | tf_op jit(solution)/shard_map/all_to_all | solution.py:491
  172.9 1.2 copy-done.10
  174.1 1.0 copy-done.12
  175.1 1.0 copy-done.14
  176.1 1.0 copy-done.16
  177.1 13.5 %shard_map.70 = bf16[48,4096]{1,0:T(8,128)(2,1)S(1)} custom-call(bf16[32,48,512]{2,1,0:T(8,128)(2,1)} %all-to-all-done.3.moved_ref, f32[128,4096]{1,0:T(8,128)} %copy-done.5, f32[128,4096]{1,0:T(8,128)} %get-tuple-element.23.sin_ref, bf16[128,4096]{1,0:T(8,128)(2,1)S(1)} %copy-done.10, bf16[768,256]{1,0:T(8,128)(2,1)S(1)} %bitcast.59, ...), custom_call_target="tpu_custom_call" | custom-call | flops 3623878656 | bytes 12582912 | tf_op jit(solution)/shard_map/pallas_call | solution.py:383
  190.7 2.3 shard_map.71
  193.0 0.0 copy-start.3
  193.0 0.9 copy-done.3
  193.8 9.5 %all-to-all-done.2.data_ref = bf16[16,80,512]{2,1,0:T(8,128)(2,1)S(1)} async-done(((bf16[16,80,512]{2,1,0:T(8,128)(2,1)}), bf16[16,80,512]{2,1,0:T(8,128)(2,1)S(1)}, u32[]{:S(2)}, u32[]{:S(2)}) %all-to-all-start.2) | async-done | bytes 1310752 | tf_op jit(solution)/shard_map/all_to_all | solution.py:491
  203.4 5.0 %all-to-all-start.4 = ((bf16[16,48,512]{2,1,0:T(8,128)(2,1)}), bf16[16,48,512]{2,1,0:T(8,128)(2,1)}, u32[]{:S(2)}, u32[]{:S(2)}) async-start(bf16[16,48,512]{2,1,0:T(8,128)(2,1)} %copy-done.3), calls=%async_computation.4 | async-start | bytes 1572864 | tf_op jit(solution)/shard_map/all_to_all | solution.py:491
  208.3 0.1 reshape.113.valid_ref
  208.4 4.8 %shard_map.69 = (f32[80,4096]{1,0:T(8,128)S(1)}, bf16[80,4096]{1,0:T(8,128)(2,1)}) custom-call(s32[128]{0:T(128)S(1)} %reshape.112.block_ref, s32[128]{0:T(128)S(1)} %reshape.113.valid_ref, bf16[16,80,512]{2,1,0:T(8,128)(2,1)S(1)} %all-to-all-done.2.data_ref), custom_call_target="tpu_custom_call" | custom-call | bytes 6291456 | tf_op jit(solution)/shard_map/pallas_call | solution.py:236
  213.2 1.1 copy-done.7
  214.3 0.8 collective-permute-start
  215.1 12.5 %all-to-all-done.4.data_ref = bf16[16,48,512]{2,1,0:T(8,128)(2,1)} async-done(((bf16[16,48,512]{2,1,0:T(8,128)(2,1)}), bf16[16,48,512]{2,1,0:T(8,128)(2,1)}, u32[]{:S(2)}, u32[]{:S(2)}) %all-to-all-start.4) | async-done | bytes 786464 | tf_op jit(solution)/shard_map/all_to_all | solution.py:491
  227.5 4.3 %shard_map.72 = (f32[48,4096]{1,0:T(8,128)S(1)}, bf16[48,4096]{1,0:T(8,128)(2,1)S(1)}) custom-call(s32[128]{0:T(128)S(1)} %reshape.112.block_ref, s32[128]{0:T(128)S(1)} %reshape.113.valid_ref, bf16[16,48,512]{2,1,0:T(8,128)(2,1)} %all-to-all-done.4.data_ref), custom_call_target="tpu_custom_call" | custom-call | bytes 6291456 | tf_op jit(solution)/shard_map/pallas_call | solution.py:236
  231.8 0.8 collective-permute-start.1
  232.7 10.7 %collective-permute-done.1.refs_3_ = bf16[48,4096]{1,0:T(8,128)(2,1)S(1)} collective-permute-done((bf16[48,4096]{1,0:T(8,128)(2,1)S(1)}, bf16[48,4096]{1,0:T(8,128)(2,1)S(1)}, u32[]{:S(2)}, u32[]{:S(2)}) %collective-permute-start.1) | collective-permute-done | bytes 393248 | tf_op jit(solution)/shard_map/ppermute | solution.py:496
  243.4 0.0 collective-permute-done.refs_2_
  243.4 1.3 copy-done.8
  244.7 2.8 %shard_map.73 = f32[256,4096]{1,0:T(8,128)} custom-call(s32[2]{0:T(128)S(1)} %and_select_fusion.owner_ref, f32[80,4096]{1,0:T(8,128)S(1)} %copy-done.8, f32[48,4096]{1,0:T(8,128)S(1)} %get-tuple-element.14.refs_1_, bf16[80,4096]{1,0:T(8,128)(2,1)S(1)} %collective-permute-done.refs_2_, bf16[48,4096]{1,0:T(8,128)(2,1)S(1)} %collective-permute-done.1.refs_3_), custom_call_target="tpu_custom_call" | custom-call | bytes 8388608 | tf_op jit(solution)/shard_map/pallas_call | solution.py:416
  (37 shorter events, 0.2 us)
Async XLA Ops:
  0.0 2.8 %copy-start = (bf16[256,4096]{1,0:T(8,128)(2,1)S(1)}, bf16[256,4096]{1,0:T(8,128)(2,1)}, u32[]{:S(2)}) copy-start(bf16[256,4096]{1,0:T(8,128)(2,1)} %param.7) | copy-start | bytes 6291460
  5.9 1.3 copy-start.1
  7.2 53.6 %all-to-all-start.1 = ((bf16[16,128,512]{2,1,0:T(8,128)(2,1)}), bf16[16,128,512]{2,1,0:T(8,128)(2,1)}, u32[]{:S(2)}, u32[]{:S(2)}) async-start(bf16[16,128,512]{2,1,0:T(8,128)(2,1)} %copy-done.1), calls=%async_computation.1 | async-start | bytes 4194304 | tf_op jit(solution)/shard_map/all_to_all | solution.py:461
  33.2 1.6 copy-start.18
  35.5 1.6 copy-start.4
  53.9 1.1 copy-start.6
  60.8 61.8 %all-to-all-start = ((bf16[32,80,512]{2,1,0:T(8,128)(2,1)}), bf16[32,80,512]{2,1,0:T(8,128)(2,1)}, u32[]{:S(2)}, u32[]{:S(2)}) async-start(bf16[32,80,512]{2,1,0:T(8,128)(2,1)} %get-tuple-element.11), calls=%async_computation | async-start | bytes 5242880 | tf_op jit(solution)/shard_map/all_to_all | solution.py:473
  66.6 63.8 %copy-start.19 = (bf16[3,2,128,128]{3,2,1,0:T(8,128)(2,1)S(1)}, bf16[3,2,128,128]{3,2,1,0:T(8,128)(2,1)}, u32[]{:S(2)}) copy-start(bf16[3,2,128,128]{3,2,1,0:T(8,128)(2,1)} %param.11) | copy-start | bytes 589828
  66.6 80.1 %copy-start.11 = (bf16[96,8,2,128]{3,1,2,0:T(8,128)(2,1)}, bf16[96,8,2,128]{3,1,2,0:T(8,128)(2,1)S(1)}, u32[]{:S(2)}) copy-start(bf16[96,8,2,128]{3,1,2,0:T(8,128)(2,1)S(1)} %copy.47) | copy-start | bytes 1179652
  122.6 42.8 %all-to-all-start.3 = ((bf16[32,48,512]{2,1,0:T(8,128)(2,1)}), bf16[32,48,512]{2,1,0:T(8,128)(2,1)}, u32[]{:S(2)}, u32[]{:S(2)}) async-start(bf16[32,48,512]{2,1,0:T(8,128)(2,1)} %copy-done.6), calls=%async_computation.3 | async-start | bytes 3145728 | tf_op jit(solution)/shard_map/all_to_all | solution.py:473
  133.4 1.8 copy-start.17
  135.2 11.6 %copy-start.13 = (bf16[768,256]{1,0:T(8,128)(2,1)}, bf16[768,256]{1,0:T(8,128)(2,1)S(1)}, u32[]{:S(2)}) copy-start(bf16[768,256]{1,0:T(8,128)(2,1)S(1)} %get-tuple-element.41.adjoint_ref) | copy-start | bytes 1179652
  135.2 11.6 %copy-start.15 = (bf16[768,256]{1,0:T(8,128)(2,1)}, bf16[768,256]{1,0:T(8,128)(2,1)S(1)}, u32[]{:S(2)}) copy-start(bf16[768,256]{1,0:T(8,128)(2,1)S(1)} %get-tuple-element.42.focus_ref) | copy-start | bytes 1179652
  135.3 11.5 %copy-start.9 = (bf16[128,4096]{1,0:T(8,128)(2,1)}, bf16[128,4096]{1,0:T(8,128)(2,1)S(1)}, u32[]{:S(2)}) copy-start(bf16[128,4096]{1,0:T(8,128)(2,1)S(1)} %constant_dynamic-slice_fusion.2.target_ref) | copy-start | bytes 3145732
  146.8 15.1 %copy-start.5 = (f32[128,4096]{1,0:T(8,128)}, f32[128,4096]{1,0:T(8,128)S(1)}, u32[]{:S(2)}) copy-start(f32[128,4096]{1,0:T(8,128)S(1)} %get-tuple-element.24.cos_ref) | copy-start | bytes 6291460
  164.3 1.1 copy-start.2
  165.4 38.0 %all-to-all-start.2 = ((bf16[16,80,512]{2,1,0:T(8,128)(2,1)}), bf16[16,80,512]{2,1,0:T(8,128)(2,1)S(1)}, u32[]{:S(2)}, u32[]{:S(2)}) async-start(bf16[16,80,512]{2,1,0:T(8,128)(2,1)} %copy-done.2), calls=%async_computation.2 | async-start | bytes 2621440 | tf_op jit(solution)/shard_map/all_to_all | solution.py:491
  172.9 1.2 copy-start.10
  174.1 1.0 copy-start.12
  175.1 1.0 copy-start.14
  176.1 1.0 copy-start.16
  193.0 0.9 copy-start.3
  203.4 24.2 %all-to-all-start.4 = ((bf16[16,48,512]{2,1,0:T(8,128)(2,1)}), bf16[16,48,512]{2,1,0:T(8,128)(2,1)}, u32[]{:S(2)}, u32[]{:S(2)}) async-start(bf16[16,48,512]{2,1,0:T(8,128)(2,1)} %copy-done.3), calls=%async_computation.4 | async-start | bytes 1572864 | tf_op jit(solution)/shard_map/all_to_all | solution.py:491
  213.2 1.1 copy-start.7
  214.3 29.1 %collective-permute-start = (bf16[80,4096]{1,0:T(8,128)(2,1)}, bf16[80,4096]{1,0:T(8,128)(2,1)S(1)}, u32[]{:S(2)}, u32[]{:S(2)}) collective-permute-start(bf16[80,4096]{1,0:T(8,128)(2,1)} %get-tuple-element.15), channel_id=1, source_target_pairs={{0,16},{16,0},{1,17},{17,1},{2,18},{18,2},{3,19},{19,3},{4,20},{20... | collective-permute-start | bytes 1966088 | tf_op jit(solution)/shard_map/ppermute | solution.py:496
  231.8 11.6 %collective-permute-start.1 = (bf16[48,4096]{1,0:T(8,128)(2,1)S(1)}, bf16[48,4096]{1,0:T(8,128)(2,1)S(1)}, u32[]{:S(2)}, u32[]{:S(2)}) collective-permute-start(bf16[48,4096]{1,0:T(8,128)(2,1)S(1)} %get-tuple-element.16), channel_id=1, source_target_pairs={{0,16},{16,0},{1,17},{17,1},{2,18},{18,2},{3,19},{19,3},{4,20},{20... | collective-permute-start | bytes 1179656 | tf_op jit(solution)/shard_map/ppermute | solution.py:496
  243.4 1.3 copy-start.8

commit v4 on v3

--- a/solution.py
+++ b/solution.py
@@ -162,7 +162,8 @@
 
 
 VMEM_GRANT = 48 * 1024 * 1024
-EIGHTHS = (5, 3)
+EIGHTHS = (6, 2)
+GROUP = 4
 
 
 def half_chunk(data_ref, band, block, to_right):
@@ -332,48 +333,57 @@
     def columns(ref, at):
         return ref[pl.ds(first, rows), pl.ds(pl.multiple_of(at * tile, tile), tile)]
 
-    def product(ref, at, weight_ref):
-        return jnp.dot(window(ref, at), weight_ref[...], preferred_element_type=jnp.float32)
-
-    def screen_step(at, carry):
-        advanced = product(lines, at, approach_ref).astype(jnp.bfloat16).astype(jnp.float32)
-        cosine = jnp.concatenate([columns(cos_ref, at)] * modes, axis=0)
-        sine = jnp.concatenate([columns(sin_ref, at)] * modes, axis=0)
-        real, imag = advanced[:, :tile], advanced[:, tile:]
-        screened = jnp.concatenate(
-            [real * cosine - imag * sine, real * sine + imag * cosine], axis=1
-        )
-        put(screens, at, screened.astype(jnp.bfloat16))
+    group = math.gcd(GROUP, tiles)
+    stacked = modes * rows
+
+    def products(ref, first_at, weight_ref):
+        windows = jnp.concatenate([window(ref, first_at + turn) for turn in range(group)], axis=0)
+        out = jnp.dot(windows, weight_ref[...], preferred_element_type=jnp.float32)
+        return [
+            (first_at + turn, out[turn * stacked : (turn + 1) * stacked]) for turn in range(group)
+        ]
+
+    def mode_sum(value):
+        total = value[:rows]
+        for mode in range(1, modes):
+            total = total + value[mode * rows : (mode + 1) * rows]
+        return total
+
+    def screen_step(step, carry):
+        for at, advanced in products(lines, step * group, approach_ref):
+            advanced = advanced.astype(jnp.bfloat16).astype(jnp.float32)
+            cosine = jnp.concatenate([columns(cos_ref, at)] * modes, axis=0)
+            sine = jnp.concatenate([columns(sin_ref, at)] * modes, axis=0)
+            real, imag = advanced[:, :tile], advanced[:, tile:]
+            screened = jnp.concatenate(
+                [real * cosine - imag * sine, real * sine + imag * cosine], axis=1
+            )
+            put(screens, at, screened.astype(jnp.bfloat16))
         return carry
 
-    def detect_step(at, carry):
-        detected = product(screens, at, focus_ref)
-        power = detected * detected
-        power = power[:, :tile] + power[:, tile:]
-        intensity = power[:rows]
-        for mode in range(1, modes):
-            intensity = intensity + power[mode * rows : (mode + 1) * rows]
-        residual = intensity - columns(target_ref, at).astype(jnp.float32)
-        residual = jnp.concatenate([jnp.concatenate([residual] * modes, axis=0)] * 2, axis=1)
-        put(grads, at, (detected * residual).astype(jnp.bfloat16))
+    def detect_step(step, carry):
+        for at, detected in products(screens, step * group, focus_ref):
+            power = detected * detected
+            intensity = mode_sum(power[:, :tile] + power[:, tile:])
+            residual = intensity - columns(target_ref, at).astype(jnp.float32)
+            residual = jnp.concatenate([residual] * modes, axis=0)
+            residual = jnp.concatenate([residual] * 2, axis=1)
+            put(grads, at, (detected * residual).astype(jnp.bfloat16))
         return carry
 
-    def sens_step(at, carry):
-        grad = product(grads, at, adjoint_ref)
-        screened = screens[:, pl.ds(pl.multiple_of((at + 1) * pair, pair), pair)]
-        screened = screened.astype(jnp.float32)
-        terms = grad[:, tile:] * screened[:, :tile] - grad[:, :tile] * screened[:, tile:]
-        sens = terms[:rows]
-        for mode in range(1, modes):
-            sens = sens + terms[mode * rows : (mode + 1) * rows]
-        sens_ref[:, pl.ds(pl.multiple_of(at * tile, tile), tile)] = (
-            2.0 * PHASE_FACTOR * sens
-        ).astype(sens_ref.dtype)
+    def sens_step(step, carry):
+        for at, grad in products(grads, step * group, adjoint_ref):
+            screened = screens[:, pl.ds(pl.multiple_of((at + 1) * pair, pair), pair)]
+            screened = screened.astype(jnp.float32)
+            terms = grad[:, tile:] * screened[:, :tile] - grad[:, :tile] * screened[:, tile:]
+            sens_ref[:, pl.ds(pl.multiple_of(at * tile, tile), tile)] = (
+                2.0 * PHASE_FACTOR * mode_sum(terms)
+            ).astype(sens_ref.dtype)
         return carry
 
-    lax.fori_loop(0, tiles, screen_step, 0, unroll=4)
-    lax.fori_loop(0, tiles, detect_step, 0, unroll=4)
-    lax.fori_loop(0, tiles, sens_step, 0, unroll=4)
+    lax.fori_loop(0, tiles // group, screen_step, 0)
+    lax.fori_loop(0, tiles // group, detect_step, 0)
+    lax.fori_loop(0, tiles // group, sens_step, 0)
 
 
 def beam_sensitivity(first, moved, cosine, sine, target, approach, focus, adjoint, modes):
@@ -469,22 +479,28 @@
     real_lines = jnp.pad(mode_field[0, :, 0], edges)
     imag_lines = jnp.pad(mode_field[0, :, 1], edges)
     turned = approach_turned(real_lines, imag_lines, turned_weight, modes, bands, chunks)
-    moved = [
-        lax.all_to_all(part, ("mode", "band"), split_axis=0, concat_axis=0, tiled=True)
-        for part in turned
-    ]
+    def to_all(part):
+        return lax.all_to_all(part, ("mode", "band"), split_axis=0, concat_axis=0, tiled=True)
+
+    moved = [to_all(turned[0])]
 
     heights_here = gather_tiles(my_band, my_rank, inbound, (1, share, length))[0]
     phase_delay = PHASE_FACTOR * heights_here.astype(jnp.float32)
-    cosine = jnp.cos(phase_delay)
-    sine = jnp.sin(phase_delay)
-    target_here = lax.dynamic_slice_in_dim(target, mode_index * share, share, 0)
-
-    weights = (approach.reshape(flat), focus.reshape(flat), adjoint.reshape(flat))
+    beside = (
+        jnp.cos(phase_delay),
+        jnp.sin(phase_delay),
+        lax.dynamic_slice_in_dim(target, mode_index * share, share, 0),
+        approach.reshape(flat),
+        focus.reshape(flat),
+        adjoint.reshape(flat),
+    )
+    later, beside = lax.optimization_barrier((turned[1:], beside))
+    moved += [to_all(part) for part in later]
+
     pieces = [[] for step in range(modes)]
     first = 0
     for each, lines in zip(chunks, moved):
-        beam = beam_sensitivity(first, lines, cosine, sine, target_here, *weights, modes)
+        beam = beam_sensitivity(first, lines, *beside, modes)
         first += each
         packed_part = (bands, each, slots * MIRROR_TILE)
         back = gather_tiles(no_band, back_column, beam[None], packed_part)

time: 249 us -> 255 us (1.024)
  local copies, waits for them, and re-layouts: 39.4 us -> 44.8 us
  Pallas kernels: 68.1 us -> 64.1 us
  waiting for transfers between devices: 94.4 us -> 97 us
    ppermute x2, waiting for transfers between devices: 10.7 us -> 15.4 us  [fast_shards(): pieces[step].append(lax.ppermute(low, 'mode', ring))]
    all_to_all x2, waiting for transfers between devices: 56 us -> 51.6 us  [to_all(): lax.all_to_all(part, ('mode', 'band'), split_axis=0, concat_axis=0, tiled...]
    unnamed x41 -> x33, local copies, waits for them, and re-layouts: 12.7 us -> 16.5 us
    pallas_call x2, Pallas kernels: 28.7 us -> 25.2 us  [beam_sensitivity(): pl.pallas_call(functools.partial(beam_kernel, modes, first), out_shape=ja...]
  transfers between devices with their start and end apart: 7 -> 7, of which waited for: 5 -> 5; matrix products, arithmetic and copies ran while one was open for 15% -> 15% of each run, Pallas kernels for 25% -> 23%
where the time goes in v4:
time: 255 us; the launch traced here: 252 us
  waiting for transfers between devices  97 us (38%)
  Pallas kernels  64.1 us (25%)
  local copies, waits for them, and re-layouts  44.8 us (18%)
  starting transfers between devices  32.8 us (13%)
  other arithmetic  13.3 us (5%)
    all_to_all x2, waiting for transfers between devices, to_all(): lax.all_to_all(part, ('mode', 'band'), split_axis=0, concat_axis=0, tiled...  51.6 us
    pallas_call x2, Pallas kernels, beam_sensitivity(): pl.pallas_call(functools.partial(beam_kernel, modes, first), out_shape=ja...  25.2 us
    all_to_all x2, waiting for transfers between devices, fast_shards(): lax.all_to_all(back, 'band', split_axis=0, concat_axis=0, tiled=True)  24.4 us
    unnamed x33, local copies, waits for them, and re-layouts  16.5 us
    ppermute x2, waiting for transfers between devices, fast_shards(): pieces[step].append(lax.ppermute(low, 'mode', ring))  15.4 us
    pallas_call x1, Pallas kernels, approach_turned(): pl.pallas_call(approach_kernel, out_shape=[jax.ShapeDtypeStruct((tiles, e...  15.3 us
    slice x1, local copies, waits for them, and re-layouts, fast_shards(): imag_lines = jnp.pad(mode_field[0, :, 1], edges)  13.4 us
    all_to_all x2, starting transfers between devices, to_all(): lax.all_to_all(part, ('mode', 'band'), split_axis=0, concat_axis=0, tiled...  12.4 us
  transfers between devices with their start and end apart: 7, of which 5 were waited for; matrix products, arithmetic and copies ran while one was open for 15% of the time, Pallas kernels for 23%

profile of v4, /device:TPU:12, one launch (start us, length us, event | category | flops | bytes accessed | tf_op | source)
XLA Modules:
  0.0 252.3 jit_solution(357063093230207546)
XLA Ops:
  0.0 0.9 add_select_fusion
  0.9 0.7 broadcast_compare_fusion
  1.6 0.5 convert_reduce_fusion
  2.1 1.0 convert_reduce_fusion.1
  3.1 0.1 reshape.112.block_ref
  3.1 0.0 copy-done
  3.1 0.1 dynamic-slice_bitcast_fusion.data_ref
  3.3 2.9 %shard_map.65 = bf16[16,128,512]{2,1,0:T(8,128)(2,1)S(1)} custom-call(s32[128]{0:T(128)S(1)} %broadcast_in_dim.32.band_ref, s32[128]{0:T(128)S(1)} %reshape.112.block_ref, bf16[1,128,4096]{2,1,0:T(8,128)(2,1)S(1)} %dynamic-slice_bitcast_fusion.data_ref), custom_call_target="tpu_custom_call" | custom-call | bytes 6291456 | tf_op jit(solution)/shard_map/pallas_call | solution.py:197
  6.2 1.3 copy-done.1
  7.5 6.2 %all-to-all-start.1 = ((bf16[16,128,512]{2,1,0:T(8,128)(2,1)}), bf16[16,128,512]{2,1,0:T(8,128)(2,1)}, u32[]{:S(2)}, u32[]{:S(2)}) async-start(bf16[16,128,512]{2,1,0:T(8,128)(2,1)} %copy-done.1), calls=%async_computation.1 | async-start | bytes 4194304 | tf_op jit(solution)/shard_map/all_to_all | solution.py:471
  13.7 13.4 %fusion.10 = (bf16[1,256,1,4096]{3,2,1,0:T(2,128)(2,1)S(1)}, bf16[1,256,1,4096]{3,2,1,0:T(2,128)(2,1)S(1)}) fusion(bf16[1,256,2,4096]{3,2,1,0:T(2,128)(2,1)} %param.6), kind=kLoop, calls=%fused_computation.50 | loop fusion | bytes 8388608 | tf_op jit(solution)/shard_map/slice | solution.py:480
  27.2 4.7 %copy_bitcast_fusion = (bf16[256,4096]{1,0:T(8,128)(2,1)S(1)}, bf16[256,4096]{1,0:T(8,128)(2,1)S(1)}) fusion(bf16[1,256,1,4096]{3,2,1,0:T(2,128)(2,1)S(1)} %get-tuple-element.35, bf16[1,256,1,4096]{3,2,1,0:T(2,128)(2,1)S(1)} %get-tuple-element.36), kind=kLoop, calls=%fused_computation | loop fusion | bytes 8388608 | tf_op jit(solution)/shard_map/squeeze | solution.py:480
  31.9 1.5 pad.7.real_ref
  33.5 1.6 pad.8.imag_ref
  35.1 0.1 pad_maximum_fusion
  35.2 0.3 copy.33
  35.5 0.3 reshape.119.weight_ref
  35.9 0.0 copy-start.3
  35.9 1.6 copy-done.3
  37.5 1.6 copy-done.4
  39.1 15.3 %shard_map.64 = (bf16[32,96,512]{2,1,0:T(8,128)(2,1)}, bf16[32,32,512]{2,1,0:T(8,128)(2,1)S(1)}) custom-call(bf16[256,4352]{1,0:T(8,128)(2,1)S(1)} %copy-done.3, bf16[256,4352]{1,0:T(8,128)(2,1)S(1)} %copy-done.4, bf16[256,768]{1,0:T(8,128)(2,1)S(1)} %reshape.119.weight_ref), custom_call_target="tpu_custom_call" | custom-call | flops 3221225472 | bytes 8388608 | tf_op jit(solution)/shard_map/pallas_call | solution.py:275
  54.4 1.1 copy-done.9
  55.5 5.6 %all-to-all-done.1.data_ref = bf16[16,128,512]{2,1,0:T(8,128)(2,1)} async-done(((bf16[16,128,512]{2,1,0:T(8,128)(2,1)}), bf16[16,128,512]{2,1,0:T(8,128)(2,1)}, u32[]{:S(2)}, u32[]{:S(2)}) %all-to-all-start.1) | async-done | bytes 2097184 | tf_op jit(solution)/shard_map/all_to_all | solution.py:471
  61.1 4.9 %all-to-all-start = ((bf16[32,96,512]{2,1,0:T(8,128)(2,1)}), bf16[32,96,512]{2,1,0:T(8,128)(2,1)}, u32[]{:S(2)}, u32[]{:S(2)}) async-start(bf16[32,96,512]{2,1,0:T(8,128)(2,1)} %get-tuple-element.18), calls=%async_computation | async-start | bytes 6291456 | tf_op jit(solution)/shard_map/all_to_all | solution.py:483
  66.0 0.4 copy.29
  66.4 0.1 copy.47
  66.6 0.8 fusion.8
  67.4 0.4 copy.32
  67.8 1.4 copy.31
  69.2 1.0 copy_bitcast_fusion.2
  70.3 1.3 constant_dynamic-slice_fusion.2.target_ref
  71.6 2.7 %shard_map.66 = bf16[1,128,4096]{2,1,0:T(8,128)(2,1)S(1)} custom-call(s32[64]{0:T(128)S(1)} %get-tuple-element.51.band_ref, s32[64]{0:T(128)S(1)} %get-tuple-element.52.block_ref, bf16[16,128,512]{2,1,0:T(8,128)(2,1)} %all-to-all-done.1.data_ref), custom_call_target="tpu_custom_call" | custom-call | bytes 6291456 | tf_op jit(solution)/shard_map/pallas_call | solution.py:197
  74.3 8.4 %sine_bitcast_fusion = (f32[128,4096]{1,0:T(8,128)}, f32[128,4096]{1,0:T(8,128)}) fusion(bf16[1,128,4096]{2,1,0:T(8,128)(2,1)S(1)} %shard_map.66), kind=kLoop, calls=%fused_computation.2 | loop fusion | flops 1048576 | bytes 5242880 | tf_op jit(solution)/shard_map/sin | solution.py:491
  82.6 51.6 %all-to-all-done.moved_ref = bf16[32,96,512]{2,1,0:T(8,128)(2,1)} async-done(((bf16[32,96,512]{2,1,0:T(8,128)(2,1)}), bf16[32,96,512]{2,1,0:T(8,128)(2,1)}, u32[]{:S(2)}, u32[]{:S(2)}) %all-to-all-start) | async-done | bytes 3145760 | tf_op jit(solution)/shard_map/all_to_all | solution.py:483
  134.2 7.5 %all-to-all-start.3 = ((bf16[32,32,512]{2,1,0:T(8,128)(2,1)}), bf16[32,32,512]{2,1,0:T(8,128)(2,1)}, u32[]{:S(2)}, u32[]{:S(2)}) async-start(bf16[32,32,512]{2,1,0:T(8,128)(2,1)} %copy-done.9), calls=%async_computation.3 | async-start | bytes 2097152 | tf_op jit(solution)/shard_map/all_to_all | solution.py:483
  141.8 1.0 select_reduce_fusion
  142.7 0.8 reshape.114.block_ref
  143.5 1.6 copy-done.5
  145.1 1.0 copy-done.10
  146.1 1.0 copy-done.12
  147.1 15.6 %shard_map.67 = bf16[96,4096]{1,0:T(8,128)(2,1)S(1)} custom-call(bf16[32,96,512]{2,1,0:T(8,128)(2,1)} %all-to-all-done.moved_ref, f32[128,4096]{1,0:T(8,128)S(1)} %copy-done.5, f32[128,4096]{1,0:T(8,128)} %get-tuple-element.21.sin_ref, bf16[128,4096]{1,0:T(8,128)(2,1)S(1)} %constant_dynamic-slice_fusion.2.target_ref, bf16[768,256]{1,0:T(8,128)(2,1)S(1)} %bitcast.58, ...), custom_call_target="tpu_custom_call" | custom-call | flops 7247757312 | bytes 12582912 | tf_op jit(solution)/shard_map/pallas_call | solution.py:393
  162.6 2.5 %shard_map.68 = bf16[16,96,512]{2,1,0:T(8,128)(2,1)S(1)} custom-call(s32[128]{0:T(128)S(1)} %broadcast_in_dim.32.band_ref, s32[128]{0:T(128)S(1)} %reshape.114.block_ref, bf16[1,96,4096]{2,1,0:T(8,128)(2,1)S(1)} %bitcast.57), custom_call_target="tpu_custom_call" | custom-call | bytes 6291456 | tf_op jit(solution)/shard_map/pallas_call | solution.py:197
  165.2 0.0 copy-start.2
  165.2 1.1 copy-done.2
  166.3 0.0 all-to-all-done.3.moved_ref
  166.3 7.1 %all-to-all-start.2 = ((bf16[16,96,512]{2,1,0:T(8,128)(2,1)}), bf16[16,96,512]{2,1,0:T(8,128)(2,1)}, u32[]{:S(2)}, u32[]{:S(2)}) async-start(bf16[16,96,512]{2,1,0:T(8,128)(2,1)} %copy-done.2), calls=%async_computation.2 | async-start | bytes 3145728 | tf_op jit(solution)/shard_map/all_to_all | solution.py:507
  173.4 1.6 copy-done.6
  175.0 1.0 copy-done.11
  176.0 1.0 copy-done.13
  177.0 9.7 %shard_map.70 = bf16[32,4096]{1,0:T(8,128)(2,1)S(1)} custom-call(bf16[32,32,512]{2,1,0:T(8,128)(2,1)} %all-to-all-done.3.moved_ref, f32[128,4096]{1,0:T(8,128)S(1)} %copy-done.6, f32[128,4096]{1,0:T(8,128)} %get-tuple-element.21.sin_ref, bf16[128,4096]{1,0:T(8,128)(2,1)S(1)} %constant_dynamic-slice_fusion.2.target_ref, bf16[768,256]{1,0:T(8,128)(2,1)S(1)} %bitcast.59, ...), custom_call_target="tpu_custom_call" | custom-call | flops 2415919104 | bytes 12582912 | tf_op jit(solution)/shard_map/pallas_call | solution.py:393
  186.7 3.0 %shard_map.71 = bf16[16,32,512]{2,1,0:T(8,128)(2,1)} custom-call(s32[128]{0:T(128)S(1)} %broadcast_in_dim.32.band_ref, s32[128]{0:T(128)S(1)} %reshape.114.block_ref, bf16[1,32,4096]{2,1,0:T(8,128)(2,1)S(1)} %bitcast.60), custom_call_target="tpu_custom_call" | custom-call | bytes 6291456 | tf_op jit(solution)/shard_map/pallas_call | solution.py:197
  189.7 19.9 %all-to-all-done.2.data_ref = bf16[16,96,512]{2,1,0:T(8,128)(2,1)} async-done(((bf16[16,96,512]{2,1,0:T(8,128)(2,1)}), bf16[16,96,512]{2,1,0:T(8,128)(2,1)}, u32[]{:S(2)}, u32[]{:S(2)}) %all-to-all-start.2) | async-done | bytes 1572896 | tf_op jit(solution)/shard_map/all_to_all | solution.py:507
  209.6 5.0 %all-to-all-start.4 = ((bf16[16,32,512]{2,1,0:T(8,128)(2,1)}), bf16[16,32,512]{2,1,0:T(8,128)(2,1)S(1)}, u32[]{:S(2)}, u32[]{:S(2)}) async-start(bf16[16,32,512]{2,1,0:T(8,128)(2,1)} %shard_map.71), calls=%async_computation.4 | async-start | bytes 1048576 | tf_op jit(solution)/shard_map/all_to_all | solution.py:507
  214.6 0.8 reshape.113.valid_ref
  215.4 6.0 %shard_map.69 = (f32[96,4096]{1,0:T(8,128)S(1)}, bf16[96,4096]{1,0:T(8,128)(2,1)}) custom-call(s32[128]{0:T(128)S(1)} %reshape.112.block_ref, s32[128]{0:T(128)S(1)} %reshape.113.valid_ref, bf16[16,96,512]{2,1,0:T(8,128)(2,1)} %all-to-all-done.2.data_ref), custom_call_target="tpu_custom_call" | custom-call | bytes 6291456 | tf_op jit(solution)/shard_map/pallas_call | solution.py:237
  221.4 1.1 copy-done.7
  222.6 1.0 collective-permute-start
  223.6 4.5 %all-to-all-done.4.data_ref = bf16[16,32,512]{2,1,0:T(8,128)(2,1)S(1)} async-done(((bf16[16,32,512]{2,1,0:T(8,128)(2,1)}), bf16[16,32,512]{2,1,0:T(8,128)(2,1)S(1)}, u32[]{:S(2)}, u32[]{:S(2)}) %all-to-all-start.4) | async-done | bytes 524320 | tf_op jit(solution)/shard_map/all_to_all | solution.py:507
  228.1 3.5 %shard_map.72 = (f32[32,4096]{1,0:T(8,128)S(1)}, bf16[32,4096]{1,0:T(8,128)(2,1)S(1)}) custom-call(s32[128]{0:T(128)S(1)} %reshape.112.block_ref, s32[128]{0:T(128)S(1)} %reshape.113.valid_ref, bf16[16,32,512]{2,1,0:T(8,128)(2,1)S(1)} %all-to-all-done.4.data_ref), custom_call_target="tpu_custom_call" | custom-call | bytes 6291456 | tf_op jit(solution)/shard_map/pallas_call | solution.py:237
  231.6 1.0 collective-permute-start.1
  232.7 15.4 %collective-permute-done.1.refs_3_ = bf16[32,4096]{1,0:T(8,128)(2,1)S(1)} collective-permute-done((bf16[32,4096]{1,0:T(8,128)(2,1)S(1)}, bf16[32,4096]{1,0:T(8,128)(2,1)S(1)}, u32[]{:S(2)}, u32[]{:S(2)}) %collective-permute-start.1) | collective-permute-done | bytes 262176 | tf_op jit(solution)/shard_map/ppermute | solution.py:512
  248.0 0.0 collective-permute-done.refs_2_
  248.0 1.4 copy-done.8
  249.4 2.8 %shard_map.73 = f32[256,4096]{1,0:T(8,128)} custom-call(s32[2]{0:T(128)S(1)} %and_select_fusion.owner_ref, f32[96,4096]{1,0:T(8,128)S(1)} %copy-done.8, f32[32,4096]{1,0:T(8,128)S(1)} %get-tuple-element.28.refs_1_, bf16[96,4096]{1,0:T(8,128)(2,1)S(1)} %collective-permute-done.refs_2_, bf16[32,4096]{1,0:T(8,128)(2,1)S(1)} %collective-permute-done.1.refs_3_), custom_call_target="tpu_custom_call" | custom-call | bytes 8388608 | tf_op jit(solution)/shard_map/pallas_call | solution.py:426
  (29 shorter events, 0.2 us)
Async XLA Ops:
  0.0 3.1 %copy-start = (bf16[256,4096]{1,0:T(8,128)(2,1)S(1)}, bf16[256,4096]{1,0:T(8,128)(2,1)}, u32[]{:S(2)}) copy-start(bf16[256,4096]{1,0:T(8,128)(2,1)} %param.7) | copy-start | bytes 6291460
  6.2 1.3 copy-start.1
  7.5 53.6 %all-to-all-start.1 = ((bf16[16,128,512]{2,1,0:T(8,128)(2,1)}), bf16[16,128,512]{2,1,0:T(8,128)(2,1)}, u32[]{:S(2)}, u32[]{:S(2)}) async-start(bf16[16,128,512]{2,1,0:T(8,128)(2,1)} %copy-done.1), calls=%async_computation.1 | async-start | bytes 4194304 | tf_op jit(solution)/shard_map/all_to_all | solution.py:471
  33.5 1.6 copy-start.14
  35.9 1.6 copy-start.3
  37.5 1.6 copy-start.4
  54.4 1.1 copy-start.9
  61.1 5.4 %copy-start.15 = (bf16[3,2,128,128]{3,2,1,0:T(8,128)(2,1)S(1)}, bf16[3,2,128,128]{3,2,1,0:T(8,128)(2,1)}, u32[]{:S(2)}) copy-start(bf16[3,2,128,128]{3,2,1,0:T(8,128)(2,1)} %param.11) | copy-start | bytes 589828
  61.1 73.1 %all-to-all-start = ((bf16[32,96,512]{2,1,0:T(8,128)(2,1)}), bf16[32,96,512]{2,1,0:T(8,128)(2,1)}, u32[]{:S(2)}, u32[]{:S(2)}) async-start(bf16[32,96,512]{2,1,0:T(8,128)(2,1)} %get-tuple-element.18), calls=%async_computation | async-start | bytes 6291456 | tf_op jit(solution)/shard_map/all_to_all | solution.py:483
  134.2 32.1 %all-to-all-start.3 = ((bf16[32,32,512]{2,1,0:T(8,128)(2,1)}), bf16[32,32,512]{2,1,0:T(8,128)(2,1)}, u32[]{:S(2)}, u32[]{:S(2)}) async-start(bf16[32,32,512]{2,1,0:T(8,128)(2,1)} %copy-done.9), calls=%async_computation.3 | async-start | bytes 2097152 | tf_op jit(solution)/shard_map/all_to_all | solution.py:483
  143.5 1.6 copy-start.5
  145.1 1.0 copy-start.10
  146.1 1.0 copy-start.12
  165.2 1.1 copy-start.2
  166.3 43.3 %all-to-all-start.2 = ((bf16[16,96,512]{2,1,0:T(8,128)(2,1)}), bf16[16,96,512]{2,1,0:T(8,128)(2,1)}, u32[]{:S(2)}, u32[]{:S(2)}) async-start(bf16[16,96,512]{2,1,0:T(8,128)(2,1)} %copy-done.2), calls=%async_computation.2 | async-start | bytes 3145728 | tf_op jit(solution)/shard_map/all_to_all | solution.py:507
  173.4 1.6 copy-start.6
  175.0 1.0 copy-start.11
  176.0 1.0 copy-start.13
  209.6 18.5 %all-to-all-start.4 = ((bf16[16,32,512]{2,1,0:T(8,128)(2,1)}), bf16[16,32,512]{2,1,0:T(8,128)(2,1)S(1)}, u32[]{:S(2)}, u32[]{:S(2)}) async-start(bf16[16,32,512]{2,1,0:T(8,128)(2,1)} %shard_map.71), calls=%async_computation.4 | async-start | bytes 1048576 | tf_op jit(solution)/shard_map/all_to_all | solution.py:507
  221.4 1.1 copy-start.7
  222.6 25.4 %collective-permute-start = (bf16[96,4096]{1,0:T(8,128)(2,1)}, bf16[96,4096]{1,0:T(8,128)(2,1)S(1)}, u32[]{:S(2)}, u32[]{:S(2)}) collective-permute-start(bf16[96,4096]{1,0:T(8,128)(2,1)} %get-tuple-element.29), channel_id=1, source_target_pairs={{0,16},{16,0},{1,17},{17,1},{2,18},{18,2},{3,19},{19,3},{4,20},{20... | collective-permute-start | bytes 2359304 | tf_op jit(solution)/shard_map/ppermute | solution.py:512
  231.6 16.4 %collective-permute-start.1 = (bf16[32,4096]{1,0:T(8,128)(2,1)S(1)}, bf16[32,4096]{1,0:T(8,128)(2,1)S(1)}, u32[]{:S(2)}, u32[]{:S(2)}) collective-permute-start(bf16[32,4096]{1,0:T(8,128)(2,1)S(1)} %get-tuple-element.30), channel_id=1, source_target_pairs={{0,16},{16,0},{1,17},{17,1},{2,18},{18,2},{3,19},{19,3},{4,20},{20... | collective-permute-start | bytes 786440 | tf_op jit(solution)/shard_map/ppermute | solution.py:512
  248.0 1.4 copy-start.8

commit v5 on v4

--- a/solution.py
+++ b/solution.py
@@ -162,7 +162,7 @@
 
 
 VMEM_GRANT = 48 * 1024 * 1024
-EIGHTHS = (6, 2)
+EIGHTHS = (5, 3)
 GROUP = 4
 
 
@@ -222,7 +222,7 @@
             total[:, pl.ds(start, 128)] += jnp.where(lanes, tile, 0.0)
         return carry
 
-    lax.fori_loop(0, bands * slots // len(totals), some_slots, 0, unroll=2)
+    lax.fori_loop(0, bands * slots // len(totals), some_slots, 0, unroll=4)
     surface = totals[0][...]
     for total in totals[1:]:
         surface = surface + total[...]
@@ -405,32 +405,40 @@
     )(moved, cosine, sine, target, approach, focus, adjoint)
 
 
-def join_kernel(owner_ref, *refs):
+def join_kernel(counts, owner_ref, *refs):
     out_ref = refs[-1]
     steps = owner_ref.shape[0]
-    each = (len(refs) - 1) // steps
     share = out_ref.shape[0] // steps
     unit = math.gcd(*[ref.shape[0] for ref in refs])
+    position = 0
     for step in range(steps):
         first = owner_ref[step] * share
-        for ref in refs[step * each : (step + 1) * each]:
+        for ref in refs[position : position + counts[step]]:
             lines = ref.shape[0]
             at = pl.multiple_of(first, unit)
             out_ref[pl.ds(at, lines), :] = ref[...].astype(out_ref.dtype)
             first = first + lines
+        position += counts[step]
 
 
 def join_shares(owners, pieces, rows, length):
-    flat = [piece for step in pieces for piece in step]
+    early = [pieces[0]] + [others[:-1] for others in pieces[1:]]
+    flat = [piece for step in early for piece in step]
     vmem = pl.BlockSpec(memory_space=pltpu.VMEM)
-    return pl.pallas_call(
-        join_kernel,
+    joined = pl.pallas_call(
+        functools.partial(join_kernel, [len(step) for step in early]),
         out_shape=jax.ShapeDtypeStruct((rows, length), jnp.float32),
         in_specs=[pl.BlockSpec(memory_space=pltpu.SMEM)] + [vmem] * len(flat),
         out_specs=vmem,
         compiler_params=pltpu.CompilerParams(vmem_limit_bytes=VMEM_GRANT),
         cost_estimate=pl.CostEstimate(flops=0, bytes_accessed=8 << 20, transcendentals=0),
     )(owners, *flat)
+    share = rows // len(pieces)
+    for step in range(1, len(pieces)):
+        last = pieces[step][-1].astype(jnp.float32)
+        first = (owners[step] + 1) * share - last.shape[0]
+        joined = lax.dynamic_update_slice_in_dim(joined, last, first, 0)
+    return joined
 
 
 def fast_shards(mode_field, figure, target, footprint, approach_tiles, focus_tiles):

time: 255 us -> 249 us (0.976)
  waiting for transfers between devices: 97 us -> 86.6 us
    ppermute x2, waiting for transfers between devices: 15.4 us -> 5.78 us  [fast_shards(): pieces[step].append(lax.ppermute(low, 'mode', ring))]
    unnamed x33 -> x45, local copies, waits for them, and re-layouts: 16.5 us -> 16.4 us
  transfers between devices with their start and end apart: 7 -> 7, of which waited for: 5 -> 6; matrix products, arithmetic and copies ran while one was open for 15% -> 16% of each run, Pallas kernels for 23% -> 25%
where the time goes in v5:
time: 249 us; the launch traced here: 247 us
  waiting for transfers between devices  86.6 us (35%)
  Pallas kernels  65.7 us (26%)
  local copies, waits for them, and re-layouts  45.2 us (18%)
  starting transfers between devices  32.9 us (13%)
  other arithmetic  15.3 us (6%)
    all_to_all x2, waiting for transfers between devices, to_all(): lax.all_to_all(part, ('mode', 'band'), split_axis=0, concat_axis=0, tiled...  51.3 us
    pallas_call x2, Pallas kernels, beam_sensitivity(): pl.pallas_call(functools.partial(beam_kernel, modes, first), out_shape=ja...  25.7 us
    all_to_all x2, waiting for transfers between devices, fast_shards(): lax.all_to_all(back, 'band', split_axis=0, concat_axis=0, tiled=True)  23.9 us
    pallas_call x1, Pallas kernels, approach_turned(): pl.pallas_call(approach_kernel, out_shape=[jax.ShapeDtypeStruct((tiles, e...  16.8 us
    unnamed x45, local copies, waits for them, and re-layouts  16.4 us
    slice x1, local copies, waits for them, and re-layouts, fast_shards(): imag_lines = jnp.pad(mode_field[0, :, 1], edges)  13.4 us
    all_to_all x2, starting transfers between devices, to_all(): lax.all_to_all(part, ('mode', 'band'), split_axis=0, concat_axis=0, tiled...  12.6 us
    all_to_all x2, starting transfers between devices, fast_shards(): lax.all_to_all(back, 'band', split_axis=0, concat_axis=0, tiled=True)  12.6 us
  transfers between devices with their start and end apart: 7, of which 6 were waited for; matrix products, arithmetic and copies ran while one was open for 16% of the time, Pallas kernels for 25%

profile of v5, /device:TPU:12, one launch (start us, length us, event | category | flops | bytes accessed | tf_op | source)
XLA Modules:
  0.0 246.7 jit_solution(1829755120150301515)
XLA Ops:
  0.0 0.9 add_select_fusion
  0.9 0.7 broadcast_compare_fusion
  1.6 0.5 convert_reduce_fusion
  2.1 0.9 convert_reduce_fusion.1
  3.1 0.1 reshape.120.block_ref
  3.2 0.1 dynamic-slice_bitcast_fusion.data_ref
  3.3 2.9 %shard_map.65 = bf16[16,128,512]{2,1,0:T(8,128)(2,1)S(1)} custom-call(s32[128]{0:T(128)S(1)} %broadcast_in_dim.32.band_ref, s32[128]{0:T(128)S(1)} %reshape.120.block_ref, bf16[1,128,4096]{2,1,0:T(8,128)(2,1)S(1)} %dynamic-slice_bitcast_fusion.data_ref), custom_call_target="tpu_custom_call" | custom-call | bytes 6291456 | tf_op jit(solution)/shard_map/pallas_call | solution.py:197
  6.2 1.4 copy-done.1
  7.6 6.2 %all-to-all-start.1 = ((bf16[16,128,512]{2,1,0:T(8,128)(2,1)}), bf16[16,128,512]{2,1,0:T(8,128)(2,1)}, u32[]{:S(2)}, u32[]{:S(2)}) async-start(bf16[16,128,512]{2,1,0:T(8,128)(2,1)} %copy-done.1), calls=%async_computation.1 | async-start | bytes 4194304 | tf_op jit(solution)/shard_map/all_to_all | solution.py:479
  13.8 13.4 %fusion.10 = (bf16[1,256,1,4096]{3,2,1,0:T(2,128)(2,1)S(1)}, bf16[1,256,1,4096]{3,2,1,0:T(2,128)(2,1)S(1)}) fusion(bf16[1,256,2,4096]{3,2,1,0:T(2,128)(2,1)} %param.6), kind=kLoop, calls=%fused_computation.51 | loop fusion | bytes 8388608 | tf_op jit(solution)/shard_map/slice | solution.py:488
  27.2 4.7 %copy_bitcast_fusion = (bf16[256,4096]{1,0:T(8,128)(2,1)S(1)}, bf16[256,4096]{1,0:T(8,128)(2,1)S(1)}) fusion(bf16[1,256,1,4096]{3,2,1,0:T(2,128)(2,1)S(1)} %get-tuple-element.35, bf16[1,256,1,4096]{3,2,1,0:T(2,128)(2,1)S(1)} %get-tuple-element.36), kind=kLoop, calls=%fused_computation | loop fusion | bytes 8388608 | tf_op jit(solution)/shard_map/squeeze | solution.py:488
  32.0 1.5 pad.7.real_ref
  33.5 1.6 pad.8.imag_ref
  35.2 0.1 pad_maximum_fusion
  35.3 0.3 copy.33
  35.6 0.3 reshape.127.weight_ref
  35.9 1.6 copy-done.4
  37.5 16.8 %shard_map.64 = (bf16[32,80,512]{2,1,0:T(8,128)(2,1)}, bf16[32,48,512]{2,1,0:T(8,128)(2,1)S(1)}) custom-call(bf16[256,4352]{1,0:T(8,128)(2,1)S(1)} %copy-done.4, bf16[256,4352]{1,0:T(8,128)(2,1)} %pad.8.imag_ref, bf16[256,768]{1,0:T(8,128)(2,1)S(1)} %reshape.127.weight_ref), custom_call_target="tpu_custom_call" | custom-call | flops 3221225472 | bytes 8388608 | tf_op jit(solution)/shard_map/pallas_call | solution.py:275
  54.3 1.2 copy-done.6
  55.5 5.6 %all-to-all-done.1.data_ref = bf16[16,128,512]{2,1,0:T(8,128)(2,1)} async-done(((bf16[16,128,512]{2,1,0:T(8,128)(2,1)}), bf16[16,128,512]{2,1,0:T(8,128)(2,1)}, u32[]{:S(2)}, u32[]{:S(2)}) %all-to-all-start.1) | async-done | bytes 2097184 | tf_op jit(solution)/shard_map/all_to_all | solution.py:479
  61.2 4.9 %all-to-all-start = ((bf16[32,80,512]{2,1,0:T(8,128)(2,1)}), bf16[32,80,512]{2,1,0:T(8,128)(2,1)}, u32[]{:S(2)}, u32[]{:S(2)}) async-start(bf16[32,80,512]{2,1,0:T(8,128)(2,1)} %get-tuple-element.18), calls=%async_computation | async-start | bytes 5242880 | tf_op jit(solution)/shard_map/all_to_all | solution.py:491
  66.1 0.4 copy.29
  66.5 0.1 copy.47
  66.6 0.8 fusion.8
  67.5 0.4 copy.32
  67.9 1.4 copy.31
  69.3 0.7 fusion.3
  70.0 1.0 copy_bitcast_fusion.2
  71.0 1.3 constant_dynamic-slice_fusion.target_ref
  72.3 3.1 %shard_map.66 = bf16[1,128,4096]{2,1,0:T(8,128)(2,1)S(1)} custom-call(s32[64]{0:T(128)S(1)} %get-tuple-element.51.band_ref, s32[64]{0:T(128)S(1)} %get-tuple-element.52.block_ref, bf16[16,128,512]{2,1,0:T(8,128)(2,1)} %all-to-all-done.1.data_ref), custom_call_target="tpu_custom_call" | custom-call | bytes 6291456 | tf_op jit(solution)/shard_map/pallas_call | solution.py:197
  75.4 8.4 %sine_bitcast_fusion = (f32[128,4096]{1,0:T(8,128)}, f32[128,4096]{1,0:T(8,128)}) fusion(bf16[1,128,4096]{2,1,0:T(8,128)(2,1)S(1)} %shard_map.66), kind=kLoop, calls=%fused_computation.2 | loop fusion | flops 1048576 | bytes 5242880 | tf_op jit(solution)/shard_map/sin | solution.py:499
  83.8 39.2 %all-to-all-done.moved_ref = bf16[32,80,512]{2,1,0:T(8,128)(2,1)} async-done(((bf16[32,80,512]{2,1,0:T(8,128)(2,1)}), bf16[32,80,512]{2,1,0:T(8,128)(2,1)}, u32[]{:S(2)}, u32[]{:S(2)}) %all-to-all-start) | async-done | bytes 2621472 | tf_op jit(solution)/shard_map/all_to_all | solution.py:491
  123.0 7.7 %all-to-all-start.3 = ((bf16[32,48,512]{2,1,0:T(8,128)(2,1)}), bf16[32,48,512]{2,1,0:T(8,128)(2,1)}, u32[]{:S(2)}, u32[]{:S(2)}) async-start(bf16[32,48,512]{2,1,0:T(8,128)(2,1)} %copy-done.6), calls=%async_computation.3 | async-start | bytes 3145728 | tf_op jit(solution)/shard_map/all_to_all | solution.py:491
  130.8 1.0 select_reduce_fusion
  131.7 0.8 reshape.122.block_ref
  132.5 1.6 copy-done.5
  134.1 1.0 copy-done.13
  135.1 1.0 copy-done.15
  136.1 14.0 %shard_map.67 = bf16[80,4096]{1,0:T(8,128)(2,1)S(1)} custom-call(bf16[32,80,512]{2,1,0:T(8,128)(2,1)} %all-to-all-done.moved_ref, f32[128,4096]{1,0:T(8,128)S(1)} %copy-done.5, f32[128,4096]{1,0:T(8,128)} %get-tuple-element.21.sin_ref, bf16[128,4096]{1,0:T(8,128)(2,1)S(1)} %constant_dynamic-slice_fusion.target_ref, bf16[768,256]{1,0:T(8,128)(2,1)S(1)} %bitcast.60, ...), custom_call_target="tpu_custom_call" | custom-call | flops 6039797760 | bytes 12582912 | tf_op jit(solution)/shard_map/pallas_call | solution.py:393
  150.1 2.4 shard_map.68
  152.6 1.0 copy-done.2
  153.6 12.1 %all-to-all-done.3.moved_ref = bf16[32,48,512]{2,1,0:T(8,128)(2,1)} async-done(((bf16[32,48,512]{2,1,0:T(8,128)(2,1)}), bf16[32,48,512]{2,1,0:T(8,128)(2,1)}, u32[]{:S(2)}, u32[]{:S(2)}) %all-to-all-start.3) | async-done | bytes 1572896 | tf_op jit(solution)/shard_map/all_to_all | solution.py:491
  165.7 7.6 %all-to-all-start.2 = ((bf16[16,80,512]{2,1,0:T(8,128)(2,1)}), bf16[16,80,512]{2,1,0:T(8,128)(2,1)S(1)}, u32[]{:S(2)}, u32[]{:S(2)}) async-start(bf16[16,80,512]{2,1,0:T(8,128)(2,1)} %copy-done.2), calls=%async_computation.2 | async-start | bytes 2621440 | tf_op jit(solution)/shard_map/all_to_all | solution.py:515
  173.3 1.2 copy-done.10
  174.5 1.0 copy-done.12
  175.5 1.0 copy-done.14
  176.5 1.0 copy-done.16
  177.5 11.7 %shard_map.70 = bf16[48,4096]{1,0:T(8,128)(2,1)S(1)} custom-call(bf16[32,48,512]{2,1,0:T(8,128)(2,1)} %all-to-all-done.3.moved_ref, f32[128,4096]{1,0:T(8,128)} %get-tuple-element.20.cos_ref, f32[128,4096]{1,0:T(8,128)} %get-tuple-element.21.sin_ref, bf16[128,4096]{1,0:T(8,128)(2,1)S(1)} %copy-done.10, bf16[768,256]{1,0:T(8,128)(2,1)S(1)} %bitcast.61, ...), custom_call_target="tpu_custom_call" | custom-call | flops 3623878656 | bytes 12582912 | tf_op jit(solution)/shard_map/pallas_call | solution.py:393
  189.3 2.3 shard_map.71
  191.5 0.9 copy-done.3
  192.4 11.3 %all-to-all-done.2.data_ref = bf16[16,80,512]{2,1,0:T(8,128)(2,1)S(1)} async-done(((bf16[16,80,512]{2,1,0:T(8,128)(2,1)}), bf16[16,80,512]{2,1,0:T(8,128)(2,1)S(1)}, u32[]{:S(2)}, u32[]{:S(2)}) %all-to-all-start.2) | async-done | bytes 1310752 | tf_op jit(solution)/shard_map/all_to_all | solution.py:515
  203.7 5.0 %all-to-all-start.4 = ((bf16[16,48,512]{2,1,0:T(8,128)(2,1)}), bf16[16,48,512]{2,1,0:T(8,128)(2,1)}, u32[]{:S(2)}, u32[]{:S(2)}) async-start(bf16[16,48,512]{2,1,0:T(8,128)(2,1)} %copy-done.3), calls=%async_computation.4 | async-start | bytes 1572864 | tf_op jit(solution)/shard_map/all_to_all | solution.py:515
  208.7 0.1 reshape.121.valid_ref
  208.8 4.7 %shard_map.69 = (f32[80,4096]{1,0:T(8,128)S(1)}, bf16[80,4096]{1,0:T(8,128)(2,1)}) custom-call(s32[128]{0:T(128)S(1)} %reshape.120.block_ref, s32[128]{0:T(128)S(1)} %reshape.121.valid_ref, bf16[16,80,512]{2,1,0:T(8,128)(2,1)S(1)} %all-to-all-done.2.data_ref), custom_call_target="tpu_custom_call" | custom-call | bytes 6291456 | tf_op jit(solution)/shard_map/pallas_call | solution.py:237
  213.5 1.1 copy-done.7
  214.6 0.8 collective-permute-start
  215.4 12.6 %all-to-all-done.4.data_ref = bf16[16,48,512]{2,1,0:T(8,128)(2,1)} async-done(((bf16[16,48,512]{2,1,0:T(8,128)(2,1)}), bf16[16,48,512]{2,1,0:T(8,128)(2,1)}, u32[]{:S(2)}, u32[]{:S(2)}) %all-to-all-start.4) | async-done | bytes 786464 | tf_op jit(solution)/shard_map/all_to_all | solution.py:515
  227.9 5.0 %shard_map.72 = (f32[48,4096]{1,0:T(8,128)S(1)}, bf16[48,4096]{1,0:T(8,128)(2,1)}) custom-call(s32[128]{0:T(128)S(1)} %reshape.120.block_ref, s32[128]{0:T(128)S(1)} %reshape.121.valid_ref, bf16[16,48,512]{2,1,0:T(8,128)(2,1)} %all-to-all-done.4.data_ref), custom_call_target="tpu_custom_call" | custom-call | bytes 6291456 | tf_op jit(solution)/shard_map/pallas_call | solution.py:237
  232.9 0.8 collective-permute-start.1
  233.7 0.6 slice.27
  234.9 1.3 copy-done.8
  236.2 2.8 %shard_map.73 = f32[256,4096]{1,0:T(8,128)} custom-call(s32[2]{0:T(128)S(1)} %and_select_fusion.owner_ref, f32[80,4096]{1,0:T(8,128)S(1)} %copy-done.8, f32[48,4096]{1,0:T(8,128)S(1)} %get-tuple-element.28.refs_1_, bf16[80,4096]{1,0:T(8,128)(2,1)S(1)} %collective-permute-done.refs_2_), custom_call_target="tpu_custom_call" | custom-call | bytes 8388608 | tf_op jit(solution)/shard_map/pallas_call | solution.py:428
  238.9 5.8 %collective-permute-done.1 = bf16[48,4096]{1,0:T(8,128)(2,1)} collective-permute-done((bf16[48,4096]{1,0:T(8,128)(2,1)}, bf16[48,4096]{1,0:T(8,128)(2,1)}, u32[]{:S(2)}, u32[]{:S(2)}) %collective-permute-start.1) | collective-permute-done | bytes 393248 | tf_op jit(solution)/shard_map/ppermute | solution.py:520
  244.7 1.9 convert_dynamic-update-slice_fusion
  (43 shorter events, 0.3 us)
Async XLA Ops:
  0.0 3.2 %copy-start = (bf16[256,4096]{1,0:T(8,128)(2,1)S(1)}, bf16[256,4096]{1,0:T(8,128)(2,1)}, u32[]{:S(2)}) copy-start(bf16[256,4096]{1,0:T(8,128)(2,1)} %param.7) | copy-start | bytes 6291460
  1.6 1.5 copy-start.19
  2.1 1.0 copy-start.20
  6.2 1.4 copy-start.1
  7.6 53.6 %all-to-all-start.1 = ((bf16[16,128,512]{2,1,0:T(8,128)(2,1)}), bf16[16,128,512]{2,1,0:T(8,128)(2,1)}, u32[]{:S(2)}, u32[]{:S(2)}) async-start(bf16[16,128,512]{2,1,0:T(8,128)(2,1)} %copy-done.1), calls=%async_computation.1 | async-start | bytes 4194304 | tf_op jit(solution)/shard_map/all_to_all | solution.py:479
  33.5 1.6 copy-start.17
  35.9 1.6 copy-start.4
  54.3 1.2 copy-start.6
  61.2 5.4 %copy-start.18 = (bf16[3,2,128,128]{3,2,1,0:T(8,128)(2,1)S(1)}, bf16[3,2,128,128]{3,2,1,0:T(8,128)(2,1)}, u32[]{:S(2)}) copy-start(bf16[3,2,128,128]{3,2,1,0:T(8,128)(2,1)} %param.11) | copy-start | bytes 589828
  61.2 61.8 %all-to-all-start = ((bf16[32,80,512]{2,1,0:T(8,128)(2,1)}), bf16[32,80,512]{2,1,0:T(8,128)(2,1)}, u32[]{:S(2)}, u32[]{:S(2)}) async-start(bf16[32,80,512]{2,1,0:T(8,128)(2,1)} %get-tuple-element.18), calls=%async_computation | async-start | bytes 5242880 | tf_op jit(solution)/shard_map/all_to_all | solution.py:491
  66.5 66.0 %copy-start.11 = (bf16[96,8,2,128]{3,1,2,0:T(8,128)(2,1)}, bf16[96,8,2,128]{3,1,2,0:T(8,128)(2,1)S(1)}, u32[]{:S(2)}) copy-start(bf16[96,8,2,128]{3,1,2,0:T(8,128)(2,1)S(1)} %copy.47) | copy-start | bytes 1179652
  72.3 60.2 %copy-start.9 = (bf16[128,4096]{1,0:T(8,128)(2,1)}, bf16[128,4096]{1,0:T(8,128)(2,1)S(1)}, u32[]{:S(2)}) copy-start(bf16[128,4096]{1,0:T(8,128)(2,1)S(1)} %constant_dynamic-slice_fusion.target_ref) | copy-start | bytes 3145732
  123.0 42.7 %all-to-all-start.3 = ((bf16[32,48,512]{2,1,0:T(8,128)(2,1)}), bf16[32,48,512]{2,1,0:T(8,128)(2,1)}, u32[]{:S(2)}, u32[]{:S(2)}) async-start(bf16[32,48,512]{2,1,0:T(8,128)(2,1)} %copy-done.6), calls=%async_computation.3 | async-start | bytes 3145728 | tf_op jit(solution)/shard_map/all_to_all | solution.py:491
  132.5 1.6 copy-start.5
  134.1 1.0 copy-start.13
  135.1 1.0 copy-start.15
  152.6 1.1 copy-start.2
  165.7 38.0 %all-to-all-start.2 = ((bf16[16,80,512]{2,1,0:T(8,128)(2,1)}), bf16[16,80,512]{2,1,0:T(8,128)(2,1)S(1)}, u32[]{:S(2)}, u32[]{:S(2)}) async-start(bf16[16,80,512]{2,1,0:T(8,128)(2,1)} %copy-done.2), calls=%async_computation.2 | async-start | bytes 2621440 | tf_op jit(solution)/shard_map/all_to_all | solution.py:515
  173.3 1.2 copy-start.10
  174.5 1.0 copy-start.12
  175.5 1.0 copy-start.14
  176.5 1.0 copy-start.16
  189.2 19.5 %copy-start.21 = (s32[16,8]{1,0:T(8,128)S(1)}, s32[16,8]{1,0:T(8,128)}, u32[]{:S(2)}) copy-start(s32[16,8]{1,0:T(8,128)} %get-tuple-element.31) | copy-start | bytes 1540
  191.5 0.9 copy-start.3
  203.7 24.2 %all-to-all-start.4 = ((bf16[16,48,512]{2,1,0:T(8,128)(2,1)}), bf16[16,48,512]{2,1,0:T(8,128)(2,1)}, u32[]{:S(2)}, u32[]{:S(2)}) async-start(bf16[16,48,512]{2,1,0:T(8,128)(2,1)} %copy-done.3), calls=%async_computation.4 | async-start | bytes 1572864 | tf_op jit(solution)/shard_map/all_to_all | solution.py:515
  213.5 1.1 copy-start.7
  214.6 20.2 %collective-permute-start = (bf16[80,4096]{1,0:T(8,128)(2,1)}, bf16[80,4096]{1,0:T(8,128)(2,1)S(1)}, u32[]{:S(2)}, u32[]{:S(2)}) collective-permute-start(bf16[80,4096]{1,0:T(8,128)(2,1)} %get-tuple-element.29), channel_id=1, source_target_pairs={{0,16},{16,0},{1,17},{17,1},{2,18},{18,2},{3,19},{19,3},{4,20},{20... | collective-permute-start | bytes 1966088 | tf_op jit(solution)/shard_map/ppermute | solution.py:520
  232.9 11.8 %collective-permute-start.1 = (bf16[48,4096]{1,0:T(8,128)(2,1)}, bf16[48,4096]{1,0:T(8,128)(2,1)}, u32[]{:S(2)}, u32[]{:S(2)}) collective-permute-start(bf16[48,4096]{1,0:T(8,128)(2,1)} %get-tuple-element.30), channel_id=1, source_target_pairs={{0,16},{16,0},{1,17},{17,1},{2,18},{18,2},{3,19},{19,3},{4,20},{20... | collective-permute-start | bytes 1179656 | tf_op jit(solution)/shard_map/ppermute | solution.py:520
  234.8 1.3 copy-start.8

commit v6 on v5

--- a/solution.py
+++ b/solution.py
@@ -222,7 +222,7 @@
             total[:, pl.ds(start, 128)] += jnp.where(lanes, tile, 0.0)
         return carry
 
-    lax.fori_loop(0, bands * slots // len(totals), some_slots, 0, unroll=4)
+    lax.fori_loop(0, bands * slots // len(totals), some_slots, 0, unroll=2)
     surface = totals[0][...]
     for total in totals[1:]:
         surface = surface + total[...]
@@ -246,6 +246,83 @@
         compiler_params=pltpu.CompilerParams(vmem_limit_bytes=VMEM_GRANT),
         cost_estimate=pl.CostEstimate(flops=0, bytes_accessed=6 << 20, transcendentals=0),
     )(blocks, valid, data)
+
+
+def pack_kernel(column_ref, data_ref, *out_refs):
+    left_lanes = lax.broadcasted_iota(jnp.int32, (data_ref.shape[1], 128), 1) < MIRROR_TILE
+    slots = out_refs[0].shape[1] // MIRROR_TILE
+    for turn, out_ref in enumerate(out_refs):
+        for slot in range(0, slots, 2):
+            at = turn * slots + slot
+            left = half_chunk(data_ref, 0, column_ref[at], 0)
+            right = half_chunk(data_ref, 0, column_ref[at + 1], 1)
+            out_ref[:, pl.ds(slot * MIRROR_TILE, 128)] = jnp.where(
+                left_lanes, left, right
+            ).astype(out_ref.dtype)
+
+
+def collect_blocks_kernel(count, block_ref, valid_ref, *refs):
+    data_refs, (out_ref, low_ref), totals = refs[:count], refs[count : count + 2], refs[count + 2 :]
+    rows, width = data_refs[0].shape
+    slots = width // MIRROR_TILE
+    lane_half = lax.broadcasted_iota(jnp.int32, (rows, 128), 1) // MIRROR_TILE
+    for total in totals:
+        total[...] = jnp.zeros_like(total)
+    for turn, data_ref in enumerate(data_refs):
+        for slot in range(slots):
+            total = totals[slot % len(totals)]
+            block = block_ref[turn * slots + slot]
+            side = block % 2
+            chunk = data_ref[:, pl.ds(slot // 2 * 128, 128)].astype(jnp.float32)
+            tile = jnp.where(side != slot % 2, pltpu.roll(chunk, MIRROR_TILE, 1), chunk)
+            lanes = lane_half == jnp.where(valid_ref[turn * slots + slot] > 0, side, 2)
+            start = pl.multiple_of((block // 2) * 128, 128)
+            total[:, pl.ds(start, 128)] += jnp.where(lanes, tile, 0.0)
+    surface = totals[0][...]
+    for total in totals[1:]:
+        surface = surface + total[...]
+    out_ref[...] = surface
+    low_ref[...] = surface.astype(low_ref.dtype)
+
+
+def return_by_permutes(beam, columns, blocks, valid, length):
+    bands, slots = columns.shape
+    rows = beam.shape[1]
+    me = lax.axis_index("band")
+    steps = jnp.arange(bands, dtype=jnp.int32)
+    ahead = jnp.take(columns, (me + steps) % bands, axis=0).reshape(-1)
+    behind = (me - steps + bands) % bands
+    smem = pl.BlockSpec(memory_space=pltpu.SMEM)
+    vmem = pl.BlockSpec(memory_space=pltpu.VMEM)
+    parts = pl.pallas_call(
+        pack_kernel,
+        out_shape=[jax.ShapeDtypeStruct((rows, slots * MIRROR_TILE), beam.dtype)] * bands,
+        in_specs=[smem, vmem],
+        out_specs=[vmem] * bands,
+        compiler_params=pltpu.CompilerParams(vmem_limit_bytes=VMEM_GRANT),
+        cost_estimate=pl.CostEstimate(flops=0, bytes_accessed=2 << 20, transcendentals=0),
+    )(ahead, beam)
+    arrived = [parts[0]]
+    for step in range(1, bands):
+        ring = [(i, (i + step) % bands) for i in range(bands)]
+        arrived.append(lax.ppermute(parts[step], "band", ring))
+    extent = (rows, length)
+    return pl.pallas_call(
+        functools.partial(collect_blocks_kernel, bands),
+        out_shape=[
+            jax.ShapeDtypeStruct(extent, jnp.float32),
+            jax.ShapeDtypeStruct(extent, jnp.bfloat16),
+        ],
+        in_specs=[smem, smem] + [vmem] * bands,
+        out_specs=[vmem, vmem],
+        scratch_shapes=[pltpu.VMEM(extent, jnp.float32)] * 4,
+        compiler_params=pltpu.CompilerParams(vmem_limit_bytes=VMEM_GRANT),
+        cost_estimate=pl.CostEstimate(flops=0, bytes_accessed=2 << 20, transcendentals=0),
+    )(
+        jnp.take(blocks, behind, axis=0).reshape(-1),
+        jnp.take(valid, behind, axis=0).reshape(-1),
+        *arrived,
+    )
 
 
 def approach_kernel(real_ref, imag_ref, weight_ref, *out_refs):
@@ -511,9 +588,13 @@
         beam = beam_sensitivity(first, lines, *beside, modes)
         first += each
         packed_part = (bands, each, slots * MIRROR_TILE)
-        back = gather_tiles(no_band, back_column, beam[None], packed_part)
-        returned = lax.all_to_all(back, "band", split_axis=0, concat_axis=0, tiled=True)
-        surface, low = collect_tiles(asked_block, asked, returned, length)
+        if first < share:
+            back = gather_tiles(no_band, back_column, beam[None], packed_part)
+            returned = lax.all_to_all(back, "band", split_axis=0, concat_axis=0, tiled=True)
+            surface, low = collect_tiles(asked_block, asked, returned, length)
+        else:
+            tables = [t.reshape(bands, slots) for t in (back_column, asked_block, asked)]
+            surface, low = return_by_permutes(beam[None], *tables, length)
         pieces[0].append(surface)
         for step in range(1, modes):
             ring = [(i, (i + step) % modes) for i in range(modes)]

time: 249 us -> 274 us (1.10); the launches traced: 247 us -> 268 us
  local copies, waits for them, and re-layouts: 45.2 us -> 73.7 us
  waiting for transfers between devices: 86.6 us -> 62.7 us
  starting transfers between devices: 32.9 us -> 49.1 us
    all_to_all x2 -> x1, waiting for transfers between devices: 23.9 us -> 0.01 us  [fast_shards(): lax.all_to_all(back, 'band', split_axis=0, concat_axis=0, tiled=True)]
    unnamed x45 -> x115, local copies, waits for them, and re-layouts: 16.4 us -> 39.8 us
    ppermute x0 -> x15, starting transfers between devices: none -> 20.7 us  [return_by_permutes(): arrived.append(lax.ppermute(parts[step], 'band', ring))]
    pallas_call x0 -> x2, Pallas kernels: none -> 5.25 us  [the longest x1 3.03 us: return_by_permutes(): pl.pallas_call(functools.partial(collect_blocks_kernel, bands), out_shape...]
    all_to_all x2 -> x1, starting transfers between devices: 12.6 us -> 7.57 us  [fast_shards(): lax.all_to_all(back, 'band', split_axis=0, concat_axis=0, tiled=True)]
    pallas_call x2 -> x1, Pallas kernels: 9.7 us -> 4.81 us  [collect_tiles(): pl.pallas_call(collect_kernel, out_shape=[jax.ShapeDtypeStruct(extent, jn...]
    gather x0 -> x3, local copies, waits for them, and re-layouts: none -> 3.07 us  [the longest x1 1.26 us: return_by_permutes(): jnp.take(blocks, behind, axis=0).reshape(-1)]
    pallas_call x4 -> x3, Pallas kernels: 10.7 us -> 9.45 us  [gather_tiles(): pl.pallas_call(gather_kernel, out_shape=jax.ShapeDtypeStruct(out_shape, d...]
  transfers between devices with their start and end apart: 7 -> 21, of which waited for: 6 -> 4; matrix products, arithmetic and copies ran while one was open for 16% -> 17% of each run, Pallas kernels for 25% -> 23%
where the time goes in v6:
time: 274 us; the launch traced here: 268 us
  local copies, waits for them, and re-layouts  73.7 us (27%)
  Pallas kernels  64.8 us (24%)
  waiting for transfers between devices  62.7 us (23%)
  starting transfers between devices  49.1 us (18%)
  other arithmetic  17.1 us (6%)
    all_to_all x2, waiting for transfers between devices, to_all(): lax.all_to_all(part, ('mode', 'band'), split_axis=0, concat_axis=0, tiled...  51.5 us
    unnamed x115, local copies, waits for them, and re-layouts  39.8 us
    pallas_call x2, Pallas kernels, beam_sensitivity(): pl.pallas_call(functools.partial(beam_kernel, modes, first), out_shape=ja...  25.7 us
    ppermute x15, starting transfers between devices, return_by_permutes(): arrived.append(lax.ppermute(parts[step], 'band', ring))  20.7 us
    pallas_call x1, Pallas kernels, approach_turned(): pl.pallas_call(approach_kernel, out_shape=[jax.ShapeDtypeStruct((tiles, e...  16.8 us
    slice x1, local copies, waits for them, and re-layouts, fast_shards(): imag_lines = jnp.pad(mode_field[0, :, 1], edges)  13.4 us
    all_to_all x2, starting transfers between devices, to_all(): lax.all_to_all(part, ('mode', 'band'), split_axis=0, concat_axis=0, tiled...  12.6 us
    pallas_call x3, Pallas kernels, gather_tiles(): pl.pallas_call(gather_kernel, out_shape=jax.ShapeDtypeStruct(out_shape, d...  9.45 us
  transfers between devices with their start and end apart: 21, of which 4 were waited for; matrix products, arithmetic and copies ran while one was open for 17% of the time, Pallas kernels for 23%

profile of v6, /device:TPU:12, one launch (start us, length us, event | category | flops | bytes accessed | tf_op | source)
XLA Modules:
  0.0 268.5 jit_solution(2395158979337233348)
XLA Ops:
  0.0 0.9 add_select_fusion
  2.1 1.0 convert_reduce_fusion.1
  3.3 2.9 %shard_map.65 = bf16[16,128,512]{2,1,0:T(8,128)(2,1)S(1)} custom-call(s32[128]{0:T(128)S(1)} %broadcast_in_dim.59.band_ref, s32[128]{0:T(128)S(1)} %reshape.134.block_ref, bf16[1,128,4096]{2,1,0:T(8,128)(2,1)S(1)} %dynamic-slice_bitcast_fusion.data_ref), custom_call_target="tpu_custom_call" | custom-call | bytes 6291456 | tf_op jit(solution)/shard_map/pallas_call | solution.py:197
  6.3 1.3 copy-done.1
  7.6 6.2 %all-to-all-start.1 = ((bf16[16,128,512]{2,1,0:T(8,128)(2,1)}), bf16[16,128,512]{2,1,0:T(8,128)(2,1)}, u32[]{:S(2)}, u32[]{:S(2)}) async-start(bf16[16,128,512]{2,1,0:T(8,128)(2,1)} %copy-done.1), calls=%async_computation.1 | async-start | bytes 4194304 | tf_op jit(solution)/shard_map/all_to_all | solution.py:556
  13.8 13.4 %fusion.12 = (bf16[1,256,1,4096]{3,2,1,0:T(2,128)(2,1)S(1)}, bf16[1,256,1,4096]{3,2,1,0:T(2,128)(2,1)S(1)}) fusion(bf16[1,256,2,4096]{3,2,1,0:T(2,128)(2,1)} %param.8), kind=kLoop, calls=%fused_computation.71 | loop fusion | bytes 8388608 | tf_op jit(solution)/shard_map/slice | solution.py:565
  27.2 4.7 %copy_bitcast_fusion = (bf16[256,4096]{1,0:T(8,128)(2,1)S(1)}, bf16[256,4096]{1,0:T(8,128)(2,1)S(1)}) fusion(bf16[1,256,1,4096]{3,2,1,0:T(2,128)(2,1)S(1)} %get-tuple-element.68, bf16[1,256,1,4096]{3,2,1,0:T(2,128)(2,1)S(1)} %get-tuple-element.69), kind=kLoop, calls=%fused_computation.3 | loop fusion | bytes 8388608 | tf_op jit(solution)/shard_map/squeeze | solution.py:565
  32.0 1.5 pad.7.real_ref
  33.5 1.5 pad.8.imag_ref
  35.9 1.6 copy-done.2
  37.5 16.8 %shard_map.64 = (bf16[32,80,512]{2,1,0:T(8,128)(2,1)}, bf16[32,48,512]{2,1,0:T(8,128)(2,1)S(1)}) custom-call(bf16[256,4352]{1,0:T(8,128)(2,1)S(1)} %copy-done.2, bf16[256,4352]{1,0:T(8,128)(2,1)} %pad.8.imag_ref, bf16[256,768]{1,0:T(8,128)(2,1)S(1)} %reshape.177.weight_ref), custom_call_target="tpu_custom_call" | custom-call | flops 3221225472 | bytes 8388608 | tf_op jit(solution)/shard_map/pallas_call | solution.py:352
  54.3 1.3 copy-done.4
  55.5 5.6 %all-to-all-done.1.data_ref = bf16[16,128,512]{2,1,0:T(8,128)(2,1)} async-done(((bf16[16,128,512]{2,1,0:T(8,128)(2,1)}), bf16[16,128,512]{2,1,0:T(8,128)(2,1)}, u32[]{:S(2)}, u32[]{:S(2)}) %all-to-all-start.1) | async-done | bytes 2097184 | tf_op jit(solution)/shard_map/all_to_all | solution.py:556
  61.2 4.9 %all-to-all-start = ((bf16[32,80,512]{2,1,0:T(8,128)(2,1)}), bf16[32,80,512]{2,1,0:T(8,128)(2,1)}, u32[]{:S(2)}, u32[]{:S(2)}) async-start(bf16[32,80,512]{2,1,0:T(8,128)(2,1)} %get-tuple-element.35), calls=%async_computation | async-start | bytes 5242880 | tf_op jit(solution)/shard_map/all_to_all | solution.py:568
  66.6 0.8 fusion.10
  67.9 2.2 copy.31
  70.1 2.1 copy_bitcast_fusion.2
  72.1 1.3 constant_dynamic-slice_fusion.target_ref
  73.5 3.1 %shard_map.66 = bf16[1,128,4096]{2,1,0:T(8,128)(2,1)S(1)} custom-call(s32[64]{0:T(128)S(1)} %get-tuple-element.90.band_ref, s32[64]{0:T(128)S(1)} %get-tuple-element.91.block_ref, bf16[16,128,512]{2,1,0:T(8,128)(2,1)} %all-to-all-done.1.data_ref), custom_call_target="tpu_custom_call" | custom-call | bytes 6291456 | tf_op jit(solution)/shard_map/pallas_call | solution.py:197
  76.5 8.4 %sine_bitcast_fusion = (f32[128,4096]{1,0:T(8,128)}, f32[128,4096]{1,0:T(8,128)}) fusion(bf16[1,128,4096]{2,1,0:T(8,128)(2,1)S(1)} %shard_map.66), kind=kLoop, calls=%fused_computation.5 | loop fusion | flops 1048576 | bytes 5242880 | tf_op jit(solution)/shard_map/sin | solution.py:576
  84.9 38.1 %all-to-all-done.moved_ref = bf16[32,80,512]{2,1,0:T(8,128)(2,1)} async-done(((bf16[32,80,512]{2,1,0:T(8,128)(2,1)}), bf16[32,80,512]{2,1,0:T(8,128)(2,1)}, u32[]{:S(2)}, u32[]{:S(2)}) %all-to-all-start) | async-done | bytes 2621472 | tf_op jit(solution)/shard_map/all_to_all | solution.py:568
  123.0 7.8 %all-to-all-start.3 = ((bf16[32,48,512]{2,1,0:T(8,128)(2,1)}), bf16[32,48,512]{2,1,0:T(8,128)(2,1)}, u32[]{:S(2)}, u32[]{:S(2)}) async-start(bf16[32,48,512]{2,1,0:T(8,128)(2,1)} %copy-done.4), calls=%async_computation.3 | async-start | bytes 3145728 | tf_op jit(solution)/shard_map/all_to_all | solution.py:568
  131.3 1.6 copy-done.3
  132.8 1.0 copy-done.11
  133.8 1.0 copy-done.13
  134.8 14.0 %shard_map.67 = bf16[80,4096]{1,0:T(8,128)(2,1)S(1)} custom-call(bf16[32,80,512]{2,1,0:T(8,128)(2,1)} %all-to-all-done.moved_ref, f32[128,4096]{1,0:T(8,128)S(1)} %copy-done.3, f32[128,4096]{1,0:T(8,128)} %get-tuple-element.38.sin_ref, bf16[128,4096]{1,0:T(8,128)(2,1)S(1)} %constant_dynamic-slice_fusion.target_ref, bf16[768,256]{1,0:T(8,128)(2,1)S(1)} %bitcast.60, ...), custom_call_target="tpu_custom_call" | custom-call | flops 6039797760 | bytes 12582912 | tf_op jit(solution)/shard_map/pallas_call | solution.py:470
  148.9 3.5 %shard_map.68 = bf16[16,80,512]{2,1,0:T(8,128)(2,1)} custom-call(s32[128]{0:T(128)S(1)} %broadcast_in_dim.59.band_ref, s32[128]{0:T(128)S(1)} %reshape.136.block_ref, bf16[1,80,4096]{2,1,0:T(8,128)(2,1)S(1)} %bitcast.59), custom_call_target="tpu_custom_call" | custom-call | bytes 6291456 | tf_op jit(solution)/shard_map/pallas_call | solution.py:197
  152.3 13.4 %all-to-all-done.3.moved_ref = bf16[32,48,512]{2,1,0:T(8,128)(2,1)} async-done(((bf16[32,48,512]{2,1,0:T(8,128)(2,1)}), bf16[32,48,512]{2,1,0:T(8,128)(2,1)}, u32[]{:S(2)}, u32[]{:S(2)}) %all-to-all-start.3) | async-done | bytes 1572896 | tf_op jit(solution)/shard_map/all_to_all | solution.py:568
  165.7 7.6 %all-to-all-start.2 = ((bf16[16,80,512]{2,1,0:T(8,128)(2,1)}), bf16[16,80,512]{2,1,0:T(8,128)(2,1)S(1)}, u32[]{:S(2)}, u32[]{:S(2)}) async-start(bf16[16,80,512]{2,1,0:T(8,128)(2,1)} %shard_map.68), calls=%async_computation.2 | async-start | bytes 2621440 | tf_op jit(solution)/shard_map/all_to_all | solution.py:593
  175.1 1.2 copy-done.8
  176.3 1.0 copy-done.10
  177.3 1.0 copy-done.12
  178.3 1.0 copy-done.14
  179.3 11.7 %shard_map.70 = bf16[48,4096]{1,0:T(8,128)(2,1)S(1)} custom-call(bf16[32,48,512]{2,1,0:T(8,128)(2,1)} %all-to-all-done.3.moved_ref, f32[128,4096]{1,0:T(8,128)} %get-tuple-element.37.cos_ref, f32[128,4096]{1,0:T(8,128)} %get-tuple-element.38.sin_ref, bf16[128,4096]{1,0:T(8,128)(2,1)S(1)} %copy-done.8, bf16[768,256]{1,0:T(8,128)(2,1)S(1)} %bitcast.61, ...), custom_call_target="tpu_custom_call" | custom-call | flops 3623878656 | bytes 12582912 | tf_op jit(solution)/shard_map/pallas_call | solution.py:470
  191.0 2.2 shard_map.71
  198.9 1.5 collective-permute-start.1
  200.4 2.2 collective-permute-start.2
  203.9 2.4 collective-permute-start.5
  207.0 3.1 %collective-permute-start.6 = (bf16[48,512]{1,0:T(8,128)(2,1)}, bf16[48,512]{1,0:T(8,128)(2,1)}, u32[]{:S(2)}, u32[]{:S(2)}) collective-permute-start(bf16[48,512]{1,0:T(8,128)(2,1)} %get-tuple-element.52), channel_id=1, source_target_pairs={{0,7},{1,8},{2,9},{3,10},{4,11},{5,12},{6,13},{7,14},{8,15},{9,0},... | collective-permute-start | bytes 147464 | tf_op jit(solution)/shard_map/ppermute | solution.py:308
  210.0 1.4 reshape.135.valid_ref
  212.7 4.8 %shard_map.69 = (f32[80,4096]{1,0:T(8,128)S(1)}, bf16[80,4096]{1,0:T(8,128)(2,1)}) custom-call(s32[128]{0:T(128)S(1)} %copy-done.44, s32[128]{0:T(128)S(1)} %copy-done.45, bf16[16,80,512]{2,1,0:T(8,128)(2,1)S(1)} %all-to-all-done.2.data_ref), custom_call_target="tpu_custom_call" | custom-call | bytes 6291456 | tf_op jit(solution)/shard_map/pallas_call | solution.py:237
  217.5 1.1 copy-done.5
  221.7 1.7 collective-permute-start.9
  223.4 3.3 %collective-permute-start.10 = (bf16[48,512]{1,0:T(8,128)(2,1)}, bf16[48,512]{1,0:T(8,128)(2,1)S(1)}, u32[]{:S(2)}, u32[]{:S(2)}) collective-permute-start(bf16[48,512]{1,0:T(8,128)(2,1)} %copy-done.50), channel_id=1, source_target_pairs={{0,11},{1,12},{2,13},{3,14},{4,15},{5,0},{6,1},{7,2},{8,3},{9,4},{... | collective-permute-start | bytes 147464 | tf_op jit(solution)/shard_map/ppermute | solution.py:308
  228.1 1.3 gather_fusion.1
  229.3 1.3 gather_fusion
  232.4 1.4 collective-permute-start.13
  234.5 2.4 collective-permute-start.14
  240.3 0.8 copy-done.16
  241.0 0.8 copy-done.18
  242.6 0.8 copy-done.22
  243.4 0.8 copy-done.24
  244.2 0.8 copy-done.26
  245.0 0.8 copy-done.28
  245.8 0.8 copy-done.30
  246.6 0.8 copy-done.32
  247.4 0.8 copy-done.34
  249.0 0.8 copy-done.38
  251.4 3.0 %shard_map.72 = (f32[48,4096]{1,0:T(8,128)S(1)}, bf16[48,4096]{1,0:T(8,128)(2,1)}) custom-call(s32[128]{0:T(128)S(1)} %reshape.141.block_ref, s32[128]{0:T(128)S(1)} %reshape.142.valid_ref, bf16[48,512]{1,0:T(8,128)(2,1)S(1)} %copy-done.16, bf16[48,512]{1,0:T(8,128)(2,1)S(1)} %copy-done.18, bf16[48,512]{1,0:T(8,128)(2,1)S(1)} %copy-done.20, ...), custom_call_target="tpu_custom_call" | custom-call | bytes 2097152 | tf_op jit(solution)/shard_map/pallas_call | solution.py:310
  254.5 1.3 collective-permute-start.16
  257.0 1.3 copy-done.6
  258.3 2.8 %shard_map.73 = f32[256,4096]{1,0:T(8,128)} custom-call(s32[2]{0:T(128)S(1)} %and_select_fusion.2.owner_ref, f32[80,4096]{1,0:T(8,128)S(1)} %copy-done.6, f32[48,4096]{1,0:T(8,128)S(1)} %get-tuple-element.61.refs_1_, bf16[80,4096]{1,0:T(8,128)(2,1)S(1)} %collective-permute-done.15.refs_2_), custom_call_target="tpu_custom_call" | custom-call | bytes 8388608 | tf_op jit(solution)/shard_map/pallas_call | solution.py:505
  261.1 5.5 %collective-permute-done.16 = bf16[48,4096]{1,0:T(8,128)(2,1)} collective-permute-done((bf16[48,4096]{1,0:T(8,128)(2,1)}, bf16[48,4096]{1,0:T(8,128)(2,1)}, u32[]{:S(2)}, u32[]{:S(2)}) %collective-permute-start.16) | collective-permute-done | bytes 393248 | tf_op jit(solution)/shard_map/ppermute | solution.py:601
  266.6 1.9 convert_dynamic-update-slice_fusion
  (153 shorter events, 28.3 us)
Async XLA Ops:
  0.0 3.2 %copy-start = (bf16[256,4096]{1,0:T(8,128)(2,1)S(1)}, bf16[256,4096]{1,0:T(8,128)(2,1)}, u32[]{:S(2)}) copy-start(bf16[256,4096]{1,0:T(8,128)(2,1)} %param.9) | copy-start | bytes 6291460
  3.1 3.2 %copy-start.54 = (s32[16,8]{1,0:T(8,128)}, s32[16,8]{1,0:T(8,128)S(1)}, u32[]{:S(2)}) copy-start(s32[16,8]{1,0:T(8,128)S(1)} %get-tuple-element.65) | copy-start | bytes 1540
  3.1 3.1 %copy-start.43 = (s32[128]{0:T(128)}, s32[128]{0:T(128)S(1)}, u32[]{:S(2)}) copy-start(s32[128]{0:T(128)S(1)} %reshape.134.block_ref) | copy-start | bytes 1540
  6.2 1.3 copy-start.1
  7.6 53.6 %all-to-all-start.1 = ((bf16[16,128,512]{2,1,0:T(8,128)(2,1)}), bf16[16,128,512]{2,1,0:T(8,128)(2,1)}, u32[]{:S(2)}, u32[]{:S(2)}) async-start(bf16[16,128,512]{2,1,0:T(8,128)(2,1)} %copy-done.1), calls=%async_computation.1 | async-start | bytes 4194304 | tf_op jit(solution)/shard_map/all_to_all | solution.py:556
  33.5 1.5 copy-start.55
  35.9 1.6 copy-start.2
  54.3 1.3 copy-start.4
  61.2 5.4 %copy-start.56 = (bf16[3,2,128,128]{3,2,1,0:T(8,128)(2,1)S(1)}, bf16[3,2,128,128]{3,2,1,0:T(8,128)(2,1)}, u32[]{:S(2)}) copy-start(bf16[3,2,128,128]{3,2,1,0:T(8,128)(2,1)} %param.13) | copy-start | bytes 589828
  61.2 61.8 %all-to-all-start = ((bf16[32,80,512]{2,1,0:T(8,128)(2,1)}), bf16[32,80,512]{2,1,0:T(8,128)(2,1)}, u32[]{:S(2)}, u32[]{:S(2)}) async-start(bf16[32,80,512]{2,1,0:T(8,128)(2,1)} %get-tuple-element.35), calls=%async_computation | async-start | bytes 5242880 | tf_op jit(solution)/shard_map/all_to_all | solution.py:568
  66.5 64.7 %copy-start.9 = (bf16[96,8,2,128]{3,1,2,0:T(8,128)(2,1)}, bf16[96,8,2,128]{3,1,2,0:T(8,128)(2,1)S(1)}, u32[]{:S(2)}) copy-start(bf16[96,8,2,128]{3,1,2,0:T(8,128)(2,1)S(1)} %copy.47) | copy-start | bytes 1179652
  73.4 57.8 %copy-start.7 = (bf16[128,4096]{1,0:T(8,128)(2,1)}, bf16[128,4096]{1,0:T(8,128)(2,1)S(1)}, u32[]{:S(2)}) copy-start(bf16[128,4096]{1,0:T(8,128)(2,1)S(1)} %constant_dynamic-slice_fusion.target_ref) | copy-start | bytes 3145732
  123.0 42.7 %all-to-all-start.3 = ((bf16[32,48,512]{2,1,0:T(8,128)(2,1)}), bf16[32,48,512]{2,1,0:T(8,128)(2,1)}, u32[]{:S(2)}, u32[]{:S(2)}) async-start(bf16[32,48,512]{2,1,0:T(8,128)(2,1)} %copy-done.4), calls=%async_computation.3 | async-start | bytes 3145728 | tf_op jit(solution)/shard_map/all_to_all | solution.py:568
  131.2 1.6 copy-start.3
  132.8 1.0 copy-start.11
  133.8 1.0 copy-start.13
  165.7 45.6 %all-to-all-start.2 = ((bf16[16,80,512]{2,1,0:T(8,128)(2,1)}), bf16[16,80,512]{2,1,0:T(8,128)(2,1)S(1)}, u32[]{:S(2)}, u32[]{:S(2)}) async-start(bf16[16,80,512]{2,1,0:T(8,128)(2,1)} %shard_map.68), calls=%async_computation.2 | async-start | bytes 2621440 | tf_op jit(solution)/shard_map/all_to_all | solution.py:593
  175.1 1.2 copy-start.8
  176.3 1.0 copy-start.10
  177.3 1.0 copy-start.12
  178.3 1.0 copy-start.14
  193.9 0.6 copy-start.46
  196.9 0.6 copy-start.51
  198.8 4.5 %collective-permute-start = (bf16[48,512]{1,0:T(8,128)(2,1)S(1)}, bf16[48,512]{1,0:T(8,128)(2,1)S(1)}, u32[]{:S(2)}, u32[]{:S(2)}) collective-permute-start(bf16[48,512]{1,0:T(8,128)(2,1)S(1)} %get-tuple-element.46), channel_id=1, source_target_pairs={{0,1},{1,2},{2,3},{3,4},{4,5},{5,6},{6,7},{7,8},{8,9},{9,10},{10,1... | collective-permute-start | bytes 147464 | tf_op jit(solution)/shard_map/ppermute | solution.py:308
  198.9 7.4 %collective-permute-start.1 = (bf16[48,512]{1,0:T(8,128)(2,1)S(1)}, bf16[48,512]{1,0:T(8,128)(2,1)S(1)}, u32[]{:S(2)}, u32[]{:S(2)}) collective-permute-start(bf16[48,512]{1,0:T(8,128)(2,1)S(1)} %get-tuple-element.47), channel_id=1, source_target_pairs={{0,2},{1,3},{2,4},{3,5},{4,6},{5,7},{6,8},{7,9},{8,10},{9,11},{10,... | collective-permute-start | bytes 147464 | tf_op jit(solution)/shard_map/ppermute | solution.py:308
  200.4 18.2 %collective-permute-start.2 = (bf16[48,512]{1,0:T(8,128)(2,1)}, bf16[48,512]{1,0:T(8,128)(2,1)S(1)}, u32[]{:S(2)}, u32[]{:S(2)}) collective-permute-start(bf16[48,512]{1,0:T(8,128)(2,1)} %get-tuple-element.48), channel_id=1, source_target_pairs={{0,3},{1,4},{2,5},{3,6},{4,7},{5,8},{6,9},{7,10},{8,11},{9,12},{10... | collective-permute-start | bytes 147464 | tf_op jit(solution)/shard_map/ppermute | solution.py:308
  202.6 17.2 %collective-permute-start.3 = (bf16[48,512]{1,0:T(8,128)(2,1)}, bf16[48,512]{1,0:T(8,128)(2,1)S(1)}, u32[]{:S(2)}, u32[]{:S(2)}) collective-permute-start(bf16[48,512]{1,0:T(8,128)(2,1)} %get-tuple-element.49), channel_id=1, source_target_pairs={{0,4},{1,5},{2,6},{3,7},{4,8},{5,9},{6,10},{7,11},{8,12},{9,13},{1... | collective-permute-start | bytes 147464 | tf_op jit(solution)/shard_map/ppermute | solution.py:308
  203.0 18.1 %collective-permute-start.4 = (bf16[48,512]{1,0:T(8,128)(2,1)}, bf16[48,512]{1,0:T(8,128)(2,1)S(1)}, u32[]{:S(2)}, u32[]{:S(2)}) collective-permute-start(bf16[48,512]{1,0:T(8,128)(2,1)} %get-tuple-element.50), channel_id=1, source_target_pairs={{0,5},{1,6},{2,7},{3,8},{4,9},{5,10},{6,11},{7,12},{8,13},{9,14},{... | collective-permute-start | bytes 147464 | tf_op jit(solution)/shard_map/ppermute | solution.py:308
  203.3 0.6 copy-start.17
  203.9 19.4 %collective-permute-start.5 = (bf16[48,512]{1,0:T(8,128)(2,1)}, bf16[48,512]{1,0:T(8,128)(2,1)}, u32[]{:S(2)}, u32[]{:S(2)}) collective-permute-start(bf16[48,512]{1,0:T(8,128)(2,1)} %get-tuple-element.51), channel_id=1, source_target_pairs={{0,6},{1,7},{2,8},{3,9},{4,10},{5,11},{6,12},{7,13},{8,14},{9,15},... | collective-permute-start | bytes 147464 | tf_op jit(solution)/shard_map/ppermute | solution.py:308
  207.0 19.7 %collective-permute-start.6 = (bf16[48,512]{1,0:T(8,128)(2,1)}, bf16[48,512]{1,0:T(8,128)(2,1)}, u32[]{:S(2)}, u32[]{:S(2)}) collective-permute-start(bf16[48,512]{1,0:T(8,128)(2,1)} %get-tuple-element.52), channel_id=1, source_target_pairs={{0,7},{1,8},{2,9},{3,10},{4,11},{5,12},{6,13},{7,14},{8,15},{9,0},... | collective-permute-start | bytes 147464 | tf_op jit(solution)/shard_map/ppermute | solution.py:308
  211.4 0.7 copy-start.44
  212.0 0.7 copy-start.45
  217.5 1.1 copy-start.5
  219.2 11.4 %collective-permute-start.7 = (bf16[48,512]{1,0:T(8,128)(2,1)}, bf16[48,512]{1,0:T(8,128)(2,1)S(1)}, u32[]{:S(2)}, u32[]{:S(2)}) collective-permute-start(bf16[48,512]{1,0:T(8,128)(2,1)} %copy-done.53), channel_id=1, source_target_pairs={{0,8},{1,9},{2,10},{3,11},{4,12},{5,13},{6,14},{7,15},{8,0},{9,1},... | collective-permute-start | bytes 147464 | tf_op jit(solution)/shard_map/ppermute | solution.py:308
  220.5 10.7 %collective-permute-start.8 = (bf16[48,512]{1,0:T(8,128)(2,1)}, bf16[48,512]{1,0:T(8,128)(2,1)S(1)}, u32[]{:S(2)}, u32[]{:S(2)}) collective-permute-start(bf16[48,512]{1,0:T(8,128)(2,1)} %copy-done.52), channel_id=1, source_target_pairs={{0,9},{1,10},{2,11},{3,12},{4,13},{5,14},{6,15},{7,0},{8,1},{9,2},... | collective-permute-start | bytes 147464 | tf_op jit(solution)/shard_map/ppermute | solution.py:308
  221.1 0.6 copy-start.25
  221.7 10.1 %collective-permute-start.9 = (bf16[48,512]{1,0:T(8,128)(2,1)}, bf16[48,512]{1,0:T(8,128)(2,1)S(1)}, u32[]{:S(2)}, u32[]{:S(2)}) collective-permute-start(bf16[48,512]{1,0:T(8,128)(2,1)} %copy-done.51), channel_id=1, source_target_pairs={{0,10},{1,11},{2,12},{3,13},{4,14},{5,15},{6,0},{7,1},{8,2},{9,3},... | collective-permute-start | bytes 147464 | tf_op jit(solution)/shard_map/ppermute | solution.py:308
  223.4 10.5 %collective-permute-start.10 = (bf16[48,512]{1,0:T(8,128)(2,1)}, bf16[48,512]{1,0:T(8,128)(2,1)S(1)}, u32[]{:S(2)}, u32[]{:S(2)}) collective-permute-start(bf16[48,512]{1,0:T(8,128)(2,1)} %copy-done.50), channel_id=1, source_target_pairs={{0,11},{1,12},{2,13},{3,14},{4,15},{5,0},{6,1},{7,2},{8,3},{9,4},{... | collective-permute-start | bytes 147464 | tf_op jit(solution)/shard_map/ppermute | solution.py:308
  226.7 30.3 %collective-permute-start.15 = (bf16[80,4096]{1,0:T(8,128)(2,1)}, bf16[80,4096]{1,0:T(8,128)(2,1)S(1)}, u32[]{:S(2)}, u32[]{:S(2)}) collective-permute-start(bf16[80,4096]{1,0:T(8,128)(2,1)} %get-tuple-element.62), channel_id=1, source_target_pairs={{0,16},{16,0},{1,17},{17,1},{2,18},{18,2},{3,19},{19,3},{4,20},{20... | collective-permute-start | bytes 1966088 | tf_op jit(solution)/shard_map/ppermute | solution.py:601
  230.6 9.0 %copy-start.27 = (bf16[48,512]{1,0:T(8,128)(2,1)}, bf16[48,512]{1,0:T(8,128)(2,1)S(1)}, u32[]{:S(2)}) copy-start(bf16[48,512]{1,0:T(8,128)(2,1)S(1)} %collective-permute-done.7.refs_8_) | copy-start | bytes 147460
  230.6 7.2 %collective-permute-start.11 = (bf16[48,512]{1,0:T(8,128)(2,1)}, bf16[48,512]{1,0:T(8,128)(2,1)S(1)}, u32[]{:S(2)}, u32[]{:S(2)}) collective-permute-start(bf16[48,512]{1,0:T(8,128)(2,1)} %copy-done.49), channel_id=1, source_target_pairs={{0,12},{1,13},{2,14},{3,15},{4,0},{5,1},{6,2},{7,3},{8,4},{9,5},{1... | collective-permute-start | bytes 147464 | tf_op jit(solution)/shard_map/ppermute | solution.py:308
  231.8 6.6 %collective-permute-start.12 = (bf16[48,512]{1,0:T(8,128)(2,1)}, bf16[48,512]{1,0:T(8,128)(2,1)S(1)}, u32[]{:S(2)}, u32[]{:S(2)}) collective-permute-start(bf16[48,512]{1,0:T(8,128)(2,1)} %copy-done.48), channel_id=1, source_target_pairs={{0,13},{1,14},{2,15},{3,0},{4,1},{5,2},{6,3},{7,4},{8,5},{9,6},{10... | collective-permute-start | bytes 147464 | tf_op jit(solution)/shard_map/ppermute | solution.py:308
  231.8 0.6 copy-start.31
  232.4 6.6 %collective-permute-start.13 = (bf16[48,512]{1,0:T(8,128)(2,1)}, bf16[48,512]{1,0:T(8,128)(2,1)S(1)}, u32[]{:S(2)}, u32[]{:S(2)}) collective-permute-start(bf16[48,512]{1,0:T(8,128)(2,1)} %copy-done.47), channel_id=1, source_target_pairs={{0,14},{1,15},{2,0},{3,1},{4,2},{5,3},{6,4},{7,5},{8,6},{9,7},{10,... | collective-permute-start | bytes 147464 | tf_op jit(solution)/shard_map/ppermute | solution.py:308
  233.8 0.6 copy-start.33
  234.5 5.2 %collective-permute-start.14 = (bf16[48,512]{1,0:T(8,128)(2,1)}, bf16[48,512]{1,0:T(8,128)(2,1)S(1)}, u32[]{:S(2)}, u32[]{:S(2)}) collective-permute-start(bf16[48,512]{1,0:T(8,128)(2,1)} %copy-done.46), channel_id=1, source_target_pairs={{0,15},{1,0},{2,1},{3,2},{4,3},{5,4},{6,5},{7,6},{8,7},{9,8},{10,9... | collective-permute-start | bytes 147464 | tf_op jit(solution)/shard_map/ppermute | solution.py:308
  239.6 0.6 copy-start.41
  240.2 0.8 copy-start.16
  241.0 0.8 copy-start.18
  241.8 0.8 copy-start.20
  242.6 0.8 copy-start.22
  243.4 0.8 copy-start.24
  244.2 0.8 copy-start.26
  245.0 0.8 copy-start.28
  245.8 0.8 copy-start.30
  246.6 0.8 copy-start.32
  247.4 0.8 copy-start.34
  248.2 0.8 copy-start.36
  249.0 0.8 copy-start.38
  249.8 0.8 copy-start.40
  250.6 0.8 copy-start.42
  254.5 12.1 %collective-permute-start.16 = (bf16[48,4096]{1,0:T(8,128)(2,1)}, bf16[48,4096]{1,0:T(8,128)(2,1)}, u32[]{:S(2)}, u32[]{:S(2)}) collective-permute-start(bf16[48,4096]{1,0:T(8,128)(2,1)} %get-tuple-element.63), channel_id=1, source_target_pairs={{0,16},{16,0},{1,17},{17,1},{2,18},{18,2},{3,19},{19,3},{4,20},{20... | collective-permute-start | bytes 1179656 | tf_op jit(solution)/shard_map/ppermute | solution.py:601
  257.0 1.3 copy-start.6
  (14 other events, 8.6 us)
